TPU v7x, 512 devices: a whole 4x8x8 slice. The times are simulated.
512 devices in a mesh: fsdp: 32 (over y, x), blk: 16 (over z, core).
Axes of the slice: x: 4, y: 8, z: 8, core: 2. Of those that a mesh axis runs over, the one named last changes fastest.
Arguments:
- out_grad: bfloat16 [6144, 8192], P('fsdp'), may hold values from -6 to 6
- layer_input: bfloat16 [6144, 8192], P('fsdp', 'blk'), may hold values from -6 to 6
- gate_pre: bfloat16 [6144, 14336], P('fsdp', 'blk'), may hold values from -8 to 8
- up_pre: bfloat16 [6144, 14336], P('fsdp', 'blk'), may hold values from -6 to 6
- down_weight: bfloat16 [14336, 8192], P('blk', 'fsdp'), may hold values from -0.0625 to 0.0625
- proj_hidden: bfloat16 [14336, 64], P('blk'), may hold values from -0.046875 to 0.046875
- proj_model: bfloat16 [8192, 128], P('blk'), may hold values from -0.0625 to 0.0625
- example_ids: int32 [32, 192], P('fsdp'), may hold values from 0 to 1, as said below
Outputs:
- down_scores: float32 [64, 8192], P('fsdp', 'blk')
- up_scores: float32 [64, 8192], P('fsdp', 'blk')
Inputs may be any that keep to these rules, and one draw needn't show every extreme that they name: `example_ids`: within each row the example number never falls, and each of the 2 examples holds 48 to 144 neighbouring tokens; in some row one example holds exactly 144.
All inputs are finite; a program needn't handle non-finite values.
Results may differ from a plain program's by a relative error of at most 0.0029.
Values may be sent and summed in bfloat16 or wider, within the bound.
No kernel may reach another device: no remote copies, remote signals or barrier semaphores. Data moves between devices by JAX's collectives and lax.ppermute only.
A program may use at most 64 MiB of HBM per device.

v0:
```python
import jax
import jax.numpy as jnp
from jax import lax
from jax.sharding import PartitionSpec as P

EX_DEV = 2


def per_example(left, right, onehot):
    weighted = onehot[:, :, None] * left[:, None, :]
    scores = jnp.einsum("tek,tm->ekm", weighted, right, precision=lax.Precision.HIGHEST)
    return scores.reshape(onehot.shape[1], left.shape[1] * right.shape[1])


def on_device(
    out_grad, layer_input, gate_pre, up_pre, down_weight, proj_hidden, proj_model, example_ids
):
    blk_index = lax.axis_index("blk")
    feat_width = layer_input.shape[1]
    grad_cols = lax.dynamic_slice_in_dim(out_grad, blk_index * feat_width, feat_width, 1)
    grad_part = jnp.dot(grad_cols, proj_model, preferred_element_type=jnp.float32)
    input_part = jnp.dot(layer_input, proj_model, preferred_element_type=jnp.float32)
    grad_side, input_side = lax.psum((grad_part, input_part), "blk")
    silu_gate = jax.nn.silu(gate_pre.astype(jnp.float32))
    hidden = (silu_gate * up_pre.astype(jnp.float32)).astype(jnp.bfloat16)
    hid_part = jnp.dot(hidden, proj_hidden, preferred_element_type=jnp.float32)
    grad_hidden = lax.dot_general(
        out_grad,
        lax.all_gather(down_weight, "fsdp", axis=1, tiled=True),
        (((1,), (1,)), ((), ())),
        preferred_element_type=jnp.float32,
    )
    grad_up = (grad_hidden * silu_gate).astype(jnp.bfloat16)
    up_part = jnp.dot(grad_up, proj_hidden, preferred_element_type=jnp.float32)
    onehot = (example_ids[0][:, None] == jnp.arange(EX_DEV, dtype=jnp.int32)[None, :]).astype(
        jnp.float32
    )
    down_full = per_example(hid_part, grad_side, onehot)
    up_full = per_example(up_part, input_side, onehot)
    down_scores, up_scores = (
        lax.psum_scatter(down_full, "blk", scatter_dimension=1, tiled=True),
        lax.psum_scatter(up_full, "blk", scatter_dimension=1, tiled=True),
    )
    return (down_scores, up_scores)


def solution(mesh):
    in_specs = (
        P("fsdp", None),
        P("fsdp", "blk"),
        P("fsdp", "blk"),
        P("fsdp", "blk"),
        P("blk", "fsdp"),
        P("blk", None),
        P("blk", None),
        P("fsdp", None),
    )
    out_specs = (P("fsdp", "blk"), P("fsdp", "blk"))
    return jax.shard_map(
        on_device, mesh=mesh, in_specs=in_specs, out_specs=out_specs, check_vma=False
    )
```

profile of v0, /device:TPU:1, one launch (start us, length us, event | category | flops | bytes accessed | tf_op | source)
XLA Modules:
  0.0 273.8 jit_solution(12563792531889700550)
XLA Ops:
  8.0 0.0 copy-start
  8.0 0.0 all-reduce.3.cloned.1.call-start
  8.1 2.0 fusion.21
  10.1 0.0 copy-done
  10.1 1.7 fusion.6
  11.8 0.0 all-reduce.3.cloned.1.call-update
  11.8 0.0 all-gather.2.cloned.1.call-start
  11.9 0.5 all-gather.2.cloned.1.call-update
  12.4 0.0 reduce-scatter.7.cloned.1.call-start
  12.5 0.7 compare_convert_fusion
  13.1 1.5 fusion.5
  14.6 116.2 %all-reduce.3.cloned.1.call-done = (f32[192,128]{1,0:T(8,128)}, f32[192,128]{1,0:T(8,128)}) async-done(((f32[192,128]{1,0:T(8,128)}, f32[192,128]{1,0:T(8,128)}), (f32[192,128]{1,0:T(8,128)}, f32[192,128]{1,0:T(8,128)})) %all-reduce.3.cloned.1.call-update) | async-done | bytes 196624 | tf_op jit(solution)/shard_map/psum | solution.py:23
  130.8 1.2 fusion.10
  132.0 0.0 copy-start.2
  132.0 2.7 copy.14
  134.7 0.0 reduce-scatter.7.cloned.1.call-update
  134.7 0.0 copy-start.1
  134.8 0.0 reduce-scatter.9.cloned.1.call-start
  134.8 26.7 %all-gather.2.cloned.1.call-done = bf16[896,8192]{1,0:T(8,128)(2,1)} async-done(((bf16[896,256]{1,0:T(8,128)(2,1)}), bf16[896,8192]{1,0:T(8,128)(2,1)}) %all-gather.2.cloned.1.call-update) | async-done | bytes 14680080 | tf_op jit(solution)/shard_map/all_gather | solution.py:29
  161.5 0.0 copy-done.2
  161.5 10.6 %fusion.1 = f32[192,64]{0,1:T(8,128)S(1)} fusion(bf16[896,64]{0,1:T(8,128)(2,1)S(1)} %copy-done.2, bf16[192,8192]{1,0:T(8,128)(2,1)S(1)} %copy-done, bf16[896,8192]{1,0:T(8,128)(2,1)} %all-gather.2.cloned.1.call-done, bf16[192,896]{1,0:T(8,128)(2,1)} %param.10), kind=kOutput, calls=%fused_computation.2 | convolution fusion | flops 2841796608 | bytes 18333696 | tf_op jit(solution)/shard_map/dot_general | solution.py:34
  172.1 0.0 copy-done.1
  172.1 0.3 fusion.8
  172.4 2.6 copy.15
  175.0 0.0 reduce-scatter.9.cloned.1.call-update
  175.1 23.1 %reduce-scatter.7.cloned.1.call-done = f32[512,2]{1,0:T(8,128)} async-done(((f32[8192,2]{1,0:T(8,128)}), f32[512,2]{1,0:T(8,128)}) %reduce-scatter.7.cloned.1.call-update) | async-done | bytes 4112
  198.1 1.7 copy.11
  199.8 65.2 %reduce-scatter.9.cloned.1.call-done = f32[512,2]{1,0:T(8,128)} async-done(((f32[8192,2]{1,0:T(8,128)}), f32[512,2]{1,0:T(8,128)}) %reduce-scatter.9.cloned.1.call-update) | async-done | bytes 4112
  265.0 1.7 copy.13
Async XLA Ops:
  8.0 2.1 copy-start
  8.0 122.8 %all-reduce.3.cloned.1.call-start = ((), (), s32[]{:S(2)}) async-start(), calls=%async_computation.5 | async-start | bytes 393216 | tf_op jit(solution)/shard_map/psum | solution.py:23
  11.8 149.6 %all-gather.2.cloned.1.call-start = ((), (), s32[]{:S(2)}) async-start(), calls=%async_computation.2 | async-start | bytes 15138816 | tf_op jit(solution)/shard_map/all_gather | solution.py:29
  12.4 185.7 %reduce-scatter.7.cloned.1.call-start = ((), (), s32[]{:S(2)}) async-start(), calls=%async_computation.3 | async-start | bytes 4456448
  132.0 29.5 %copy-start.2 = (bf16[896,64]{0,1:T(8,128)(2,1)S(1)}, bf16[896,64]{0,1:T(8,128)(2,1)}, u32[]{:S(2)}) copy-start(bf16[896,64]{0,1:T(8,128)(2,1)} %param.13) | copy-start | bytes 344068
  134.7 37.4 %copy-start.1 = (f32[192,128]{1,0:T(8,128)S(1)}, f32[192,128]{1,0:T(8,128)}, u32[]{:S(2)}) copy-start(f32[192,128]{1,0:T(8,128)} %get-tuple-element.3) | copy-start | bytes 294916
  134.8 130.3 %reduce-scatter.9.cloned.1.call-start = ((), (), s32[]{:S(2)}) async-start(), calls=%async_computation.4 | async-start | bytes 4456448
Sparse Core Ops, SparseCore 0:
  12.0 118.8 all-reduce.2
  134.9 63.2 reduce-scatter.6
  201.2 63.7 reduce-scatter.8
Sparse Core Ops, SparseCore 1:
  15.8 145.6 all-gather.1
where the time goes:
time: 276 us; the launch traced here: 274 us
  waiting for transfers between devices  232 us (84%)
  matrix products  17.3 us (6%)
  between operations  15.3 us (6%)
  local copies, waits for them, and re-layouts  8.64 us (3%)
    psum x1, waiting for transfers between devices, on_device(): grad_side, input_side = lax.psum((grad_part, input_part), 'blk')  116 us
    unnamed x6, waiting for transfers between devices  88.9 us
    all_gather x1, waiting for transfers between devices, on_device(): lax.all_gather(down_weight, 'fsdp', axis=1, tiled=True)  26.7 us
    dot_general x1, matrix products, on_device(): up_part = jnp.dot(grad_up, proj_hidden, preferred_element_type=jnp.float32)  10.6 us
    unnamed x10, local copies, waits for them, and re-layouts  8.64 us
  transfers between devices with their start and end apart: 4, of which 4 were waited for; matrix products, arithmetic and copies ran while one was open for 8% of the time, Pallas kernels for 0%

commit v1 on v0

v1 whole, which is shorter than its diff:
```python
import jax
import jax.numpy as jnp
from jax import lax
from jax.sharding import Mesh
from jax.sharding import PartitionSpec as P

NY, NX, NZ, NC = 8, 4, 8, 2
NB = NZ * NC
ZC = ("z", "core")
BF16, F32 = jnp.bfloat16, jnp.float32


def turn(n, step):
    return [(i, (i + step) % n) for i in range(n)]


def dot_nt(a, b, **kw):
    return lax.dot_general(a, b, (((1,), (1,)), ((), ())), preferred_element_type=F32, **kw)


def dot_tt(a, b, **kw):
    return lax.dot_general(a, b, (((0,), (1,)), ((), ())), preferred_element_type=F32, **kw)


def on_device(out_grad, layer_input, gate_pre, up_pre, down_weight, proj_hidden, proj_model, example_ids):
    y, x, core = lax.axis_index("y"), lax.axis_index("x"), lax.axis_index("core")
    blk = lax.axis_index(ZC)
    tok, hid = gate_pre.shape
    wide = down_weight.shape[1]
    half = hid // 2

    def cols(shift_y, at_x):
        block = lax.rem(y - shift_y + NY, NY) * NX + at_x
        return lax.dynamic_slice_in_dim(out_grad, block * wide, wide, 1)

    up1 = lax.ppermute(down_weight, "y", turn(NY, 1))
    dn1 = lax.ppermute(down_weight, "y", turn(NY, -1))
    got = []
    for s in (2, 1, 3):
        at_x = lax.rem(x + s, NX)
        piece = jnp.concatenate([gate_pre] + [cols(core * 4 + j, at_x) for j in range(4)], axis=1)
        got.append((s, lax.ppermute(piece, "x", turn(NX, s))))
    got = [g for _, g in sorted(got, key=lambda p: p[0])]
    up2 = lax.ppermute(up1, "y", turn(NY, 1))
    dn2 = lax.ppermute(dn1, "y", turn(NY, -1))
    mine = jnp.stack([g[:, hid:] for g in got])
    other = lax.ppermute(mine, "core", turn(NC, 1))
    up3 = lax.ppermute(up2, "y", turn(NY, 1))
    dn3 = lax.ppermute(dn2, "y", turn(NY, -1))
    far_a = lax.ppermute(up3[:half], "y", turn(NY, 1))
    far_b = lax.ppermute(dn3[half:], "y", turn(NY, -1))

    feat = layer_input.shape[1]
    grad_cols = lax.dynamic_slice_in_dim(out_grad, blk * feat, feat, 1)
    grad_part = dot_tt(proj_model, grad_cols)
    input_part = dot_tt(proj_model, layer_input)
    hidden = (jax.nn.silu(gate_pre.astype(F32)) * up_pre.astype(F32)).astype(BF16)
    hid_part = dot_tt(proj_hidden, hidden)
    early = jnp.concatenate(
        [jnp.concatenate([grad_part, input_part], 0).reshape(NB, -1, tok), hid_part.reshape(NB, -1, tok)], axis=1
    )
    early = jnp.sum(lax.all_to_all(early, ZC, 0, 0), axis=0)
    n_side = 2 * proj_model.shape[1] // NB
    sides = lax.all_to_all(jnp.broadcast_to(early[None, :n_side], (NB, n_side, tok)), ZC, 0, 0).reshape(2, -1, tok)
    hid_side = early[n_side:]

    gates = [gate_pre] + [g[:, :hid] for g in got]
    low = jnp.where(core == 0, mine, other)
    high = jnp.where(core == 0, other, mine)
    grads = [jnp.concatenate([jnp.concatenate([cols(j, x) for j in range(8)], 1)] , 1)]
    grads += [jnp.concatenate([low[i], high[i]], 1) for i in range(3)]
    grads = jnp.concatenate(grads, 0)
    weights = jnp.concatenate(
        [down_weight, up1, up2, up3, jnp.concatenate([far_a, far_b], 0), dn3, dn2, dn1], 1
    )
    grad_hidden = dot_nt(grads, weights)
    silu_gate = jax.nn.silu(jnp.concatenate(gates, 0).astype(F32))
    grad_up = (grad_hidden * silu_gate).astype(BF16)
    up_part = dot_nt(proj_hidden.T, grad_up)
    up_part = [up_part[:, s * tok : (s + 1) * tok] for s in range(NX)]
    back = up_part[0]
    for s in (2, 1, 3):
        back = back + lax.ppermute(up_part[s], "x", turn(NX, -s))
    up_side = jnp.sum(lax.all_to_all(back.reshape(NB, -1, tok), ZC, 0, 0), axis=0)

    picks = (example_ids == jnp.arange(2, dtype=jnp.int32)[:, None]).astype(F32)

    def scores(left, right):
        picked = (picks[:, None, :] * left[None]).reshape(-1, tok)
        return dot_nt(picked, right, precision=lax.Precision.HIGHEST).reshape(2, -1)

    return scores(hid_side, sides[0]), scores(up_side, sides[1])


def solution(mesh):
    fine = Mesh(mesh.devices.reshape(NY, NX, NZ, NC), ("y", "x", "z", "core"))
    yx = ("y", "x")
    in_specs = (P(yx, None), P(yx, ZC), P(yx, ZC), P(yx, ZC), P(ZC, yx), P(ZC, None), P(ZC, None), P(yx, None))
    out_specs = (P(yx, ZC), P(yx, ZC))
    return jax.shard_map(on_device, mesh=fine, in_specs=in_specs, out_specs=out_specs, check_vma=False)
```

time: 276 us -> 157 us (0.57)
  waiting for transfers between devices: 232 us -> 25.1 us
  starting transfers between devices: 0.16 us -> 79.3 us
  local copies, waits for them, and re-layouts: 8.64 us -> 37 us
  between operations: 15.3 us -> 1.19 us
  matrix products: 17.3 us -> 9.39 us
    psum x1 -> x0, waiting for transfers between devices: 116 us -> none  [on_device(): grad_side, input_side = lax.psum((grad_part, input_part), 'blk')]
    unnamed x6 -> x0, waiting for transfers between devices: 88.9 us -> none
    ppermute x0 -> x15, starting transfers between devices: none -> 47 us  [the longest x3 9.32 us: on_device(): got.append((s, lax.ppermute(piece, 'x', turn(NX, s))))]
    all_to_all x0 -> x3, starting transfers between devices: none -> 32.3 us  [the longest x1 12.1 us: on_device(): early = jnp.sum(lax.all_to_all(early, ZC, 0, 0), axis=0)]
    all_gather x1 -> x0, waiting for transfers between devices: 26.7 us -> none  [on_device(): lax.all_gather(down_weight, 'fsdp', axis=1, tiled=True)]
    ppermute x0 -> x15, waiting for transfers between devices: none -> 17.3 us  [the longest x3 9.67 us: on_device(): got.append((s, lax.ppermute(piece, 'x', turn(NX, s))))]
    unnamed x10 -> x35, local copies, waits for them, and re-layouts: 8.64 us -> 23 us
    dot_general x6, matrix products: 17.3 us -> 9.39 us  [the longest x3 6.73 us: dot_nt(): lax.dot_general(a, b, (((1,), (1,)), ((), ())), preferred_element_type=F3...]
  transfers between devices with their start and end apart: 4 -> 18, of which waited for: 4 -> 4; matrix products, arithmetic and copies ran while one was open for 8% -> 30% of each run, Pallas kernels for 0% -> 0%
where the time goes in v1:
time: 157 us; the launch traced here: 155 us
  starting transfers between devices  79.3 us (51%)
  local copies, waits for them, and re-layouts  37 us (24%)
  waiting for transfers between devices  25.1 us (16%)
  matrix products  9.39 us (6%)
  other arithmetic  3.09 us (2%)
    unnamed x35, local copies, waits for them, and re-layouts  23 us
    all_to_all x1, starting transfers between devices, on_device(): early = jnp.sum(lax.all_to_all(early, ZC, 0, 0), axis=0)  12.1 us
    all_to_all x1, starting transfers between devices, on_device(): lax.all_to_all(jnp.broadcast_to(early[None, :n_side], (NB, n_side, tok)),...  10.4 us
    all_to_all x1, starting transfers between devices, on_device(): lax.all_to_all(back.reshape(NB, -1, tok), ZC, 0, 0)  9.74 us
    ppermute x3, waiting for transfers between devices, on_device(): got.append((s, lax.ppermute(piece, 'x', turn(NX, s))))  9.67 us
    ppermute x3, starting transfers between devices, on_device(): got.append((s, lax.ppermute(piece, 'x', turn(NX, s))))  9.32 us
    ppermute x3, starting transfers between devices, on_device(): back = back + lax.ppermute(up_part[s], 'x', turn(NX, -s))  8.41 us
    all_to_all x1, waiting for transfers between devices, on_device(): lax.all_to_all(back.reshape(NB, -1, tok), ZC, 0, 0)  7.79 us
  transfers between devices with their start and end apart: 18, of which 4 were waited for; matrix products, arithmetic and copies ran while one was open for 30% of the time, Pallas kernels for 0%

profile of v1, /device:TPU:1, one launch (start us, length us, event | category | flops | bytes accessed | tf_op | source)
XLA Modules:
  0.0 155.0 jit_solution(7772886696733279380)
XLA Ops:
  0.6 4.2 %collective-permute-start.4 = (bf16[896,256]{1,0:T(8,128)(2,1)}, bf16[896,256]{1,0:T(8,128)(2,1)}, u32[]{:S(2)}, u32[]{:S(2)}) collective-permute-start(bf16[896,256]{1,0:T(8,128)(2,1)} %param.12), channel_id=1, source_target_pairs={{0,64},{64,128},{128,192},{192,256},{256,320},{320,384},{384,448},... | collective-permute-start | bytes 1376264 | tf_op jit(solution)/shard_map/ppermute | solution.py:36
  4.8 3.8 %collective-permute-start.8 = (bf16[896,256]{1,0:T(8,128)(2,1)}, bf16[896,256]{1,0:T(8,128)(2,1)}, u32[]{:S(2)}, u32[]{:S(2)}) collective-permute-start(bf16[896,256]{1,0:T(8,128)(2,1)} %param.12), channel_id=1, source_target_pairs={{0,448},{64,0},{128,64},{192,128},{256,192},{320,256},{384,320},{4... | collective-permute-start | bytes 1376264 | tf_op jit(solution)/shard_map/ppermute | solution.py:37
  18.2 1.8 %dynamic-slice_dynamic-update-slice_fusion.12 = (bf16[192,2048]{1,0:T(8,128)(2,1)S(1)}, bf16[192,1920]{1,0:T(8,128)(2,1)}, bf16[192,1920]{1,0:T(8,128)(2,1)S(1)}, bf16[192,1920]{1,0:T(8,128)(2,1)S(1)}) fusion(bf16[192,2048]{1,0:T(8,128)(2,1)S(1)} %get-tuple-element.6, bf16[192,8192]{1,0:T(8,128)(2,1)} %param.8, s32[]{:T(128)S(6)} %select_n.83, ...), kind=kLoop, calls=%fused_computation.60 | loop fusion | bytes 786448 | tf_op jit(solution)/shard_map/concatenate | solution.py:70
  23.1 4.4 %collective-permute-start.2 = (bf16[192,1920]{1,0:T(8,128)(2,1)}, bf16[192,1920]{1,0:T(8,128)(2,1)S(1)}, u32[]{:S(2)}, u32[]{:S(2)}) collective-permute-start(bf16[192,1920]{1,0:T(8,128)(2,1)} %dynamic-slice_dynamic-update-slice_fusion), channel_id=1, source_target_pairs={{0,48},{16,0},{32,16},{48,32},{1,49},{17,1},{33,17},{49,33},{2,50}... | collective-permute-start | bytes 2211848 | tf_op jit(solution)/shard_map/ppermute | solution.py:42
  27.5 2.4 %collective-permute-start.1 = (bf16[192,1920]{1,0:T(8,128)(2,1)}, bf16[192,1920]{1,0:T(8,128)(2,1)S(1)}, u32[]{:S(2)}, u32[]{:S(2)}) collective-permute-start(bf16[192,1920]{1,0:T(8,128)(2,1)} %copy-done.3), channel_id=1, source_target_pairs={{0,32},{16,48},{32,0},{48,16},{1,33},{17,49},{33,1},{49,17},{2,34}... | collective-permute-start | bytes 2211848 | tf_op jit(solution)/shard_map/ppermute | solution.py:42
  30.0 2.5 %collective-permute-start = (bf16[192,1920]{1,0:T(8,128)(2,1)S(1)}, bf16[192,1920]{1,0:T(8,128)(2,1)}, u32[]{:S(2)}, u32[]{:S(2)}) collective-permute-start(bf16[192,1920]{1,0:T(8,128)(2,1)S(1)} %get-tuple-element.5), channel_id=1, source_target_pairs={{0,16},{16,32},{32,48},{48,0},{1,17},{17,33},{33,49},{49,1},{2,18}... | collective-permute-start | bytes 2211848 | tf_op jit(solution)/shard_map/ppermute | solution.py:42
  36.2 12.1 %all-to-all-start = ((f32[16,20,192]{2,1,0:T(8,128)}), f32[16,20,192]{2,1,0:T(8,128)S(1)}, u32[]{:S(2)}, u32[]{:S(2)}) async-start(f32[16,20,192]{2,1,0:T(8,128)} %pad_maximum_fusion.1), calls=%async_computation | async-start | bytes 786432 | tf_op jit(solution)/shard_map/all_to_all | solution.py:62
  48.3 1.9 %collective-permute-start.5 = (bf16[896,256]{1,0:T(8,128)(2,1)}, bf16[896,256]{1,0:T(8,128)(2,1)}, u32[]{:S(2)}, u32[]{:S(2)}) collective-permute-start(bf16[896,256]{1,0:T(8,128)(2,1)} %collective-permute-done.4), channel_id=1, source_target_pairs={{0,64},{64,128},{128,192},{192,256},{256,320},{320,384},{384,448},... | collective-permute-start | bytes 1376264 | tf_op jit(solution)/shard_map/ppermute | solution.py:44
  50.2 4.6 %collective-permute-start.9 = (bf16[896,256]{1,0:T(8,128)(2,1)}, bf16[896,256]{1,0:T(8,128)(2,1)}, u32[]{:S(2)}, u32[]{:S(2)}) collective-permute-start(bf16[896,256]{1,0:T(8,128)(2,1)} %collective-permute-done.8), channel_id=1, source_target_pairs={{0,448},{64,0},{128,64},{192,128},{256,192},{320,256},{384,320},{4... | collective-permute-start | bytes 1376264 | tf_op jit(solution)/shard_map/ppermute | solution.py:45
  55.8 9.7 %collective-permute-done = bf16[192,1920]{1,0:T(8,128)(2,1)} collective-permute-done((bf16[192,1920]{1,0:T(8,128)(2,1)S(1)}, bf16[192,1920]{1,0:T(8,128)(2,1)}, u32[]{:S(2)}, u32[]{:S(2)}) %collective-permute-start) | collective-permute-done | bytes 737312 | tf_op jit(solution)/shard_map/ppermute | solution.py:42
  66.5 1.9 %collective-permute-start.6 = (bf16[896,256]{1,0:T(8,128)(2,1)}, bf16[896,256]{1,0:T(8,128)(2,1)}, u32[]{:S(2)}, u32[]{:S(2)}) collective-permute-start(bf16[896,256]{1,0:T(8,128)(2,1)} %collective-permute-done.5), channel_id=1, source_target_pairs={{0,64},{64,128},{128,192},{192,256},{256,320},{320,384},{384,448},... | collective-permute-start | bytes 1376264 | tf_op jit(solution)/shard_map/ppermute | solution.py:48
  68.4 4.6 %collective-permute-start.10 = (bf16[896,256]{1,0:T(8,128)(2,1)}, bf16[896,256]{1,0:T(8,128)(2,1)}, u32[]{:S(2)}, u32[]{:S(2)}) collective-permute-start(bf16[896,256]{1,0:T(8,128)(2,1)} %collective-permute-done.9), channel_id=1, source_target_pairs={{0,448},{64,0},{128,64},{192,128},{256,192},{320,256},{384,320},{4... | collective-permute-start | bytes 1376264 | tf_op jit(solution)/shard_map/ppermute | solution.py:49
  74.2 2.9 %collective-permute-start.3 = (bf16[3,192,1024]{2,1,0:T(8,128)(2,1)}, bf16[3,192,1024]{2,1,0:T(8,128)(2,1)S(1)}, u32[]{:S(2)}, u32[]{:S(2)}) collective-permute-start(bf16[3,192,1024]{2,1,0:T(8,128)(2,1)} %pad_maximum_fusion), channel_id=1, source_target_pairs={{0,1},{1,0},{2,3},{3,2},{4,5},{5,4},{6,7},{7,6},{8,9},{9,8},{10,11... | collective-permute-start | bytes 3538952 | tf_op jit(solution)/shard_map/ppermute | solution.py:47
  77.1 1.8 %constant_dynamic-update-slice_fusion.9 = bf16[896,2048]{1,0:T(8,128)(2,1)} fusion(bf16[896,256]{1,0:T(8,128)(2,1)} %param.12), kind=kLoop, calls=%fused_computation.80 | loop fusion | bytes 917504
  79.0 1.9 %constant_dynamic-update-slice_fusion.8 = bf16[896,2048]{1,0:T(8,128)(2,1)} fusion(bf16[896,2048]{1,0:T(8,128)(2,1)} %constant_dynamic-update-slice_fusion.9, bf16[896,256]{1,0:T(8,128)(2,1)} %collective-permute-done.4), kind=kLoop, calls=%fused_computation.79 | loop fusion | bytes 917504
  81.6 10.4 %all-to-all-start.1 = ((f32[16,16,192]{2,1,0:T(8,128)}), f32[16,16,192]{2,1,0:T(8,128)S(1)}, u32[]{:S(2)}, u32[]{:S(2)}) async-start(f32[16,16,192]{2,1,0:T(8,128)} %broadcast_in_dim.2), calls=%async_computation.1 | async-start | bytes 524288 | tf_op jit(solution)/shard_map/all_to_all | solution.py:64
  92.0 1.7 %slice.104 = bf16[192,896]{1,0:T(8,128)(2,1)} slice(bf16[192,1920]{1,0:T(8,128)(2,1)} %collective-permute-done), slice={[0:192], [0:896]} | slice | bytes 688128 | tf_op jit(solution)/shard_map/slice | solution.py:67
  94.7 2.2 %collective-permute-start.11 = (bf16[448,256]{1,0:T(8,128)(2,1)S(1)}, bf16[448,256]{1,0:T(8,128)(2,1)S(1)}, u32[]{:S(2)}, u32[]{:S(2)}) collective-permute-start(bf16[448,256]{1,0:T(8,128)(2,1)S(1)} %slice.103), channel_id=1, source_target_pairs={{0,448},{64,0},{128,64},{192,128},{256,192},{320,256},{384,320},{4... | collective-permute-start | bytes 688136 | tf_op jit(solution)/shard_map/ppermute | solution.py:51
  97.9 3.1 %collective-permute-start.7 = (bf16[448,256]{1,0:T(8,128)(2,1)S(1)}, bf16[448,256]{1,0:T(8,128)(2,1)S(1)}, u32[]{:S(2)}, u32[]{:S(2)}) collective-permute-start(bf16[448,256]{1,0:T(8,128)(2,1)S(1)} %slice.102), channel_id=1, source_target_pairs={{0,64},{64,128},{128,192},{192,256},{256,320},{320,384},{384,448},... | collective-permute-start | bytes 688136 | tf_op jit(solution)/shard_map/ppermute | solution.py:50
  101.0 1.9 %constant_dynamic-update-slice_fusion.7 = bf16[896,2048]{1,0:T(8,128)(2,1)} fusion(bf16[896,2048]{1,0:T(8,128)(2,1)} %constant_dynamic-update-slice_fusion.8, bf16[896,256]{1,0:T(8,128)(2,1)} %collective-permute-done.5), kind=kLoop, calls=%fused_computation.78 | loop fusion | bytes 917504
  102.9 1.9 %constant_dynamic-update-slice_fusion.6 = bf16[896,2048]{1,0:T(8,128)(2,1)} fusion(bf16[896,2048]{1,0:T(8,128)(2,1)} %constant_dynamic-update-slice_fusion.7, bf16[896,256]{1,0:T(8,128)(2,1)} %collective-permute-done.6), kind=kLoop, calls=%fused_computation.77 | loop fusion | bytes 917504
  104.8 3.1 %collective-permute-done.7 = bf16[448,256]{1,0:T(8,128)(2,1)S(1)} collective-permute-done((bf16[448,256]{1,0:T(8,128)(2,1)S(1)}, bf16[448,256]{1,0:T(8,128)(2,1)S(1)}, u32[]{:S(2)}, u32[]{:S(2)}) %collective-permute-start.7) | collective-permute-done | bytes 229408 | tf_op jit(solution)/shard_map/ppermute | solution.py:50
  108.7 1.9 %constant_dynamic-update-slice_fusion.5 = bf16[896,2048]{1,0:T(8,128)(2,1)} fusion(bf16[896,2048]{1,0:T(8,128)(2,1)} %maximum_dynamic-update-slice_fusion, bf16[896,256]{1,0:T(8,128)(2,1)} %collective-permute-done.10), kind=kLoop, calls=%fused_computation.76 | loop fusion | bytes 917504
  110.6 1.8 %constant_dynamic-update-slice_fusion.4 = bf16[896,2048]{1,0:T(8,128)(2,1)} fusion(bf16[896,2048]{1,0:T(8,128)(2,1)} %constant_dynamic-update-slice_fusion.5, bf16[896,256]{1,0:T(8,128)(2,1)} %collective-permute-done.9), kind=kLoop, calls=%fused_computation.75 | loop fusion | bytes 917504
  112.4 1.9 %constant_dynamic-update-slice_fusion.3 = bf16[896,2048]{1,0:T(8,128)(2,1)} fusion(bf16[896,2048]{1,0:T(8,128)(2,1)} %constant_dynamic-update-slice_fusion.4, bf16[896,256]{1,0:T(8,128)(2,1)} %collective-permute-done.8), kind=kLoop, calls=%fused_computation.74 | loop fusion | bytes 917504 | tf_op jit(solution)/shard_map/concatenate | solution.py:73
  115.6 6.4 %fusion.24 = f32[64,768]{1,0:T(8,128)S(1)} fusion(bf16[896,64]{0,1:T(8,128)(2,1)S(1)} %copy-done.8, bf16[896,2048]{1,0:T(8,128)(2,1)} %constant_dynamic-update-slice_fusion.3, bf16[192,1024]{1,0:T(8,128)(2,1)S(1)} %get-tuple-element.23, bf16[192,1024]{1,0:T(8,128)(2,1)S(1)} %get-tuple-element.33, bf16[192,1024]{1,0:T(8,128)(2,1)S(1)} %get-tuple-element.24, ...), kind=kOutput, calls=%fused_computation.25 | convolution fusion | flops 2938306560 | bytes 8503296 | tf_op jit(solution)/shard_map/dot_general | solution.py:18
  122.0 1.9 %collective-permute-start.14 = (f32[64,192]{1,0:T(8,128)S(1)}, f32[64,192]{1,0:T(8,128)S(1)}, u32[]{:S(2)}, u32[]{:S(2)}) collective-permute-start(f32[64,192]{1,0:T(8,128)S(1)} %get-tuple-element.28), channel_id=1, source_target_pairs={{0,16},{16,32},{32,48},{48,0},{1,17},{17,33},{33,49},{49,1},{2,18}... | collective-permute-start | bytes 147464 | tf_op jit(solution)/shard_map/ppermute | solution.py:83
  124.0 4.6 %collective-permute-start.13 = (f32[64,192]{1,0:T(8,128)S(1)}, f32[64,192]{1,0:T(8,128)S(1)}, u32[]{:S(2)}, u32[]{:S(2)}) collective-permute-start(f32[64,192]{1,0:T(8,128)S(1)} %get-tuple-element.29), channel_id=1, source_target_pairs={{0,48},{16,0},{32,16},{48,32},{1,49},{17,1},{33,17},{49,33},{2,50}... | collective-permute-start | bytes 147464 | tf_op jit(solution)/shard_map/ppermute | solution.py:83
  128.6 1.9 %collective-permute-start.12 = (f32[64,192]{1,0:T(8,128)S(1)}, f32[64,192]{1,0:T(8,128)S(1)}, u32[]{:S(2)}, u32[]{:S(2)}) collective-permute-start(f32[64,192]{1,0:T(8,128)S(1)} %get-tuple-element.27), channel_id=1, source_target_pairs={{0,32},{16,48},{32,0},{48,16},{1,33},{17,49},{33,1},{49,17},{2,34}... | collective-permute-start | bytes 147464 | tf_op jit(solution)/shard_map/ppermute | solution.py:83
  130.5 4.5 %collective-permute-done.12 = f32[64,192]{1,0:T(8,128)S(1)} collective-permute-done((f32[64,192]{1,0:T(8,128)S(1)}, f32[64,192]{1,0:T(8,128)S(1)}, u32[]{:S(2)}, u32[]{:S(2)}) %collective-permute-start.12) | collective-permute-done | bytes 49184 | tf_op jit(solution)/shard_map/ppermute | solution.py:83
  135.7 9.7 %all-to-all-start.2 = ((f32[16,4,192]{2,1,0:T(4,128)}), f32[16,4,192]{2,1,0:T(4,128)S(1)}, u32[]{:S(2)}, u32[]{:S(2)}) async-start(f32[16,4,192]{2,1,0:T(4,128)} %reshape.75), calls=%async_computation.2 | async-start | bytes 131072 | tf_op jit(solution)/shard_map/all_to_all | solution.py:84
  145.5 7.8 %all-to-all-done.2 = f32[16,4,192]{2,1,0:T(4,128)S(1)} async-done(((f32[16,4,192]{2,1,0:T(4,128)}), f32[16,4,192]{2,1,0:T(4,128)S(1)}, u32[]{:S(2)}, u32[]{:S(2)}) %all-to-all-start.2) | async-done | bytes 49184 | tf_op jit(solution)/shard_map/all_to_all | solution.py:84
  (81 shorter events, 26.6 us)
Async XLA Ops:
  0.6 33.2 %copy-start = (bf16[192,512]{1,0:T(8,128)(2,1)S(1)}, bf16[192,512]{1,0:T(8,128)(2,1)}, u32[]{:S(2)}) copy-start(bf16[192,512]{1,0:T(8,128)(2,1)} %param.9) | copy-start | bytes 589828
  0.6 47.6 %collective-permute-start.4 = (bf16[896,256]{1,0:T(8,128)(2,1)}, bf16[896,256]{1,0:T(8,128)(2,1)}, u32[]{:S(2)}, u32[]{:S(2)}) collective-permute-start(bf16[896,256]{1,0:T(8,128)(2,1)} %param.12), channel_id=1, source_target_pairs={{0,64},{64,128},{128,192},{192,256},{256,320},{320,384},{384,448},... | collective-permute-start | bytes 1376264 | tf_op jit(solution)/shard_map/ppermute | solution.py:36
  4.8 45.4 %collective-permute-start.8 = (bf16[896,256]{1,0:T(8,128)(2,1)}, bf16[896,256]{1,0:T(8,128)(2,1)}, u32[]{:S(2)}, u32[]{:S(2)}) collective-permute-start(bf16[896,256]{1,0:T(8,128)(2,1)} %param.12), channel_id=1, source_target_pairs={{0,448},{64,0},{128,64},{192,128},{256,192},{320,256},{384,320},{4... | collective-permute-start | bytes 1376264 | tf_op jit(solution)/shard_map/ppermute | solution.py:37
  10.5 21.9 %copy-start.5 = (bf16[192,896]{1,0:T(8,128)(2,1)S(1)}, bf16[192,896]{1,0:T(8,128)(2,1)}, u32[]{:S(2)}) copy-start(bf16[192,896]{1,0:T(8,128)(2,1)} %param.10) | copy-start | bytes 1032196
  10.5 22.0 %copy-start.8 = (bf16[896,64]{0,1:T(8,128)(2,1)S(1)}, bf16[896,64]{0,1:T(8,128)(2,1)}, u32[]{:S(2)}) copy-start(bf16[896,64]{0,1:T(8,128)(2,1)} %param.13) | copy-start | bytes 344068
  15.4 18.5 %copy-start.4 = (bf16[512,128]{1,0:T(8,128)(2,1)S(1)}, bf16[512,128]{1,0:T(8,128)(2,1)}, u32[]{:S(2)}) copy-start(bf16[512,128]{1,0:T(8,128)(2,1)} %param.14) | copy-start | bytes 393220
  19.9 1.6 %copy-start.3 = (bf16[192,1920]{1,0:T(8,128)(2,1)}, bf16[192,1920]{1,0:T(8,128)(2,1)S(1)}, u32[]{:S(2)}) copy-start(bf16[192,1920]{1,0:T(8,128)(2,1)S(1)} %get-tuple-element.4) | copy-start | bytes 2211844
  19.9 1.6 %copy-start.6 = (bf16[192,2048]{1,0:T(8,128)(2,1)}, bf16[192,2048]{1,0:T(8,128)(2,1)S(1)}, u32[]{:S(2)}) copy-start(bf16[192,2048]{1,0:T(8,128)(2,1)S(1)} %get-tuple-element.2) | copy-start | bytes 2359300
  23.1 31.7 %collective-permute-start.2 = (bf16[192,1920]{1,0:T(8,128)(2,1)}, bf16[192,1920]{1,0:T(8,128)(2,1)S(1)}, u32[]{:S(2)}, u32[]{:S(2)}) collective-permute-start(bf16[192,1920]{1,0:T(8,128)(2,1)} %dynamic-slice_dynamic-update-slice_fusion), channel_id=1, source_target_pairs={{0,48},{16,0},{32,16},{48,32},{1,49},{17,1},{33,17},{49,33},{2,50}... | collective-permute-start | bytes 2211848 | tf_op jit(solution)/shard_map/ppermute | solution.py:42
  27.5 28.2 %collective-permute-start.1 = (bf16[192,1920]{1,0:T(8,128)(2,1)}, bf16[192,1920]{1,0:T(8,128)(2,1)S(1)}, u32[]{:S(2)}, u32[]{:S(2)}) collective-permute-start(bf16[192,1920]{1,0:T(8,128)(2,1)} %copy-done.3), channel_id=1, source_target_pairs={{0,32},{16,48},{32,0},{48,16},{1,33},{17,49},{33,1},{49,17},{2,34}... | collective-permute-start | bytes 2211848 | tf_op jit(solution)/shard_map/ppermute | solution.py:42
  30.0 35.5 %collective-permute-start = (bf16[192,1920]{1,0:T(8,128)(2,1)S(1)}, bf16[192,1920]{1,0:T(8,128)(2,1)}, u32[]{:S(2)}, u32[]{:S(2)}) collective-permute-start(bf16[192,1920]{1,0:T(8,128)(2,1)S(1)} %get-tuple-element.5), channel_id=1, source_target_pairs={{0,16},{16,32},{32,48},{48,0},{1,17},{17,33},{33,49},{49,1},{2,18}... | collective-permute-start | bytes 2211848 | tf_op jit(solution)/shard_map/ppermute | solution.py:42
  36.2 44.7 %all-to-all-start = ((f32[16,20,192]{2,1,0:T(8,128)}), f32[16,20,192]{2,1,0:T(8,128)S(1)}, u32[]{:S(2)}, u32[]{:S(2)}) async-start(f32[16,20,192]{2,1,0:T(8,128)} %pad_maximum_fusion.1), calls=%async_computation | async-start | bytes 786432 | tf_op jit(solution)/shard_map/all_to_all | solution.py:62
  48.3 18.2 %collective-permute-start.5 = (bf16[896,256]{1,0:T(8,128)(2,1)}, bf16[896,256]{1,0:T(8,128)(2,1)}, u32[]{:S(2)}, u32[]{:S(2)}) collective-permute-start(bf16[896,256]{1,0:T(8,128)(2,1)} %collective-permute-done.4), channel_id=1, source_target_pairs={{0,64},{64,128},{128,192},{192,256},{256,320},{320,384},{384,448},... | collective-permute-start | bytes 1376264 | tf_op jit(solution)/shard_map/ppermute | solution.py:44
  50.2 18.2 %collective-permute-start.9 = (bf16[896,256]{1,0:T(8,128)(2,1)}, bf16[896,256]{1,0:T(8,128)(2,1)}, u32[]{:S(2)}, u32[]{:S(2)}) collective-permute-start(bf16[896,256]{1,0:T(8,128)(2,1)} %collective-permute-done.8), channel_id=1, source_target_pairs={{0,448},{64,0},{128,64},{192,128},{256,192},{320,256},{384,320},{4... | collective-permute-start | bytes 1376264 | tf_op jit(solution)/shard_map/ppermute | solution.py:45
  54.9 0.9 copy-start.1
  55.7 17.3 %copy-start.2 = (bf16[192,1920]{1,0:T(8,128)(2,1)}, bf16[192,1920]{1,0:T(8,128)(2,1)S(1)}, u32[]{:S(2)}) copy-start(bf16[192,1920]{1,0:T(8,128)(2,1)S(1)} %collective-permute-done.1) | copy-start | bytes 2211844
  66.5 30.5 %collective-permute-start.6 = (bf16[896,256]{1,0:T(8,128)(2,1)}, bf16[896,256]{1,0:T(8,128)(2,1)}, u32[]{:S(2)}, u32[]{:S(2)}) collective-permute-start(bf16[896,256]{1,0:T(8,128)(2,1)} %collective-permute-done.5), channel_id=1, source_target_pairs={{0,64},{64,128},{128,192},{192,256},{256,320},{320,384},{384,448},... | collective-permute-start | bytes 1376264 | tf_op jit(solution)/shard_map/ppermute | solution.py:48
  68.4 25.4 %collective-permute-start.10 = (bf16[896,256]{1,0:T(8,128)(2,1)}, bf16[896,256]{1,0:T(8,128)(2,1)}, u32[]{:S(2)}, u32[]{:S(2)}) collective-permute-start(bf16[896,256]{1,0:T(8,128)(2,1)} %collective-permute-done.9), channel_id=1, source_target_pairs={{0,448},{64,0},{128,64},{192,128},{256,192},{320,256},{384,320},{4... | collective-permute-start | bytes 1376264 | tf_op jit(solution)/shard_map/ppermute | solution.py:49
  74.2 40.1 %collective-permute-start.3 = (bf16[3,192,1024]{2,1,0:T(8,128)(2,1)}, bf16[3,192,1024]{2,1,0:T(8,128)(2,1)S(1)}, u32[]{:S(2)}, u32[]{:S(2)}) collective-permute-start(bf16[3,192,1024]{2,1,0:T(8,128)(2,1)} %pad_maximum_fusion), channel_id=1, source_target_pairs={{0,1},{1,0},{2,3},{3,2},{4,5},{5,4},{6,7},{7,6},{8,9},{9,8},{10,11... | collective-permute-start | bytes 3538952 | tf_op jit(solution)/shard_map/ppermute | solution.py:47
  81.6 54.1 %all-to-all-start.1 = ((f32[16,16,192]{2,1,0:T(8,128)}), f32[16,16,192]{2,1,0:T(8,128)S(1)}, u32[]{:S(2)}, u32[]{:S(2)}) async-start(f32[16,16,192]{2,1,0:T(8,128)} %broadcast_in_dim.2), calls=%async_computation.1 | async-start | bytes 524288 | tf_op jit(solution)/shard_map/all_to_all | solution.py:64
  94.7 10.0 %collective-permute-start.11 = (bf16[448,256]{1,0:T(8,128)(2,1)S(1)}, bf16[448,256]{1,0:T(8,128)(2,1)S(1)}, u32[]{:S(2)}, u32[]{:S(2)}) collective-permute-start(bf16[448,256]{1,0:T(8,128)(2,1)S(1)} %slice.103), channel_id=1, source_target_pairs={{0,448},{64,0},{128,64},{192,128},{256,192},{320,256},{384,320},{4... | collective-permute-start | bytes 688136 | tf_op jit(solution)/shard_map/ppermute | solution.py:51
  97.9 9.9 %collective-permute-start.7 = (bf16[448,256]{1,0:T(8,128)(2,1)S(1)}, bf16[448,256]{1,0:T(8,128)(2,1)S(1)}, u32[]{:S(2)}, u32[]{:S(2)}) collective-permute-start(bf16[448,256]{1,0:T(8,128)(2,1)S(1)} %slice.102), channel_id=1, source_target_pairs={{0,64},{64,128},{128,192},{192,256},{256,320},{320,384},{384,448},... | collective-permute-start | bytes 688136 | tf_op jit(solution)/shard_map/ppermute | solution.py:50
  114.5 1.0 slice-start
  114.5 1.1 slice-start.1
  115.6 14.9 %copy-start.7 = (s32[1,192]{1,0:T(1,128)S(1)}, s32[1,192]{1,0:T(1,128)}, u32[]{:S(2)}) copy-start(s32[1,192]{1,0:T(1,128)} %param.15) | copy-start | bytes 2308
  122.0 8.5 %collective-permute-start.14 = (f32[64,192]{1,0:T(8,128)S(1)}, f32[64,192]{1,0:T(8,128)S(1)}, u32[]{:S(2)}, u32[]{:S(2)}) collective-permute-start(f32[64,192]{1,0:T(8,128)S(1)} %get-tuple-element.28), channel_id=1, source_target_pairs={{0,16},{16,32},{32,48},{48,0},{1,17},{17,33},{33,49},{49,1},{2,18}... | collective-permute-start | bytes 147464 | tf_op jit(solution)/shard_map/ppermute | solution.py:83
  124.0 6.6 %collective-permute-start.13 = (f32[64,192]{1,0:T(8,128)S(1)}, f32[64,192]{1,0:T(8,128)S(1)}, u32[]{:S(2)}, u32[]{:S(2)}) collective-permute-start(f32[64,192]{1,0:T(8,128)S(1)} %get-tuple-element.29), channel_id=1, source_target_pairs={{0,48},{16,0},{32,16},{48,32},{1,49},{17,1},{33,17},{49,33},{2,50}... | collective-permute-start | bytes 147464 | tf_op jit(solution)/shard_map/ppermute | solution.py:83
  128.6 6.5 %collective-permute-start.12 = (f32[64,192]{1,0:T(8,128)S(1)}, f32[64,192]{1,0:T(8,128)S(1)}, u32[]{:S(2)}, u32[]{:S(2)}) collective-permute-start(f32[64,192]{1,0:T(8,128)S(1)} %get-tuple-element.27), channel_id=1, source_target_pairs={{0,32},{16,48},{32,0},{48,16},{1,33},{17,49},{33,1},{49,17},{2,34}... | collective-permute-start | bytes 147464 | tf_op jit(solution)/shard_map/ppermute | solution.py:83
  135.7 17.6 %all-to-all-start.2 = ((f32[16,4,192]{2,1,0:T(4,128)}), f32[16,4,192]{2,1,0:T(4,128)S(1)}, u32[]{:S(2)}, u32[]{:S(2)}) async-start(f32[16,4,192]{2,1,0:T(4,128)} %reshape.75), calls=%async_computation.2 | async-start | bytes 131072 | tf_op jit(solution)/shard_map/all_to_all | solution.py:84

commit v2 on v1

v2 whole, which is shorter than its diff:
```python
import functools

import jax
import jax.numpy as jnp
from jax import lax
from jax.experimental import pallas as pl
from jax.experimental.pallas import tpu as pltpu
from jax.sharding import Mesh
from jax.sharding import PartitionSpec as P

NY, NX, NZ, NC = 8, 4, 8, 2
NB = NZ * NC
ZC = ("z", "core")
BF16, F32 = jnp.bfloat16, jnp.float32
ANY = pl.BlockSpec(memory_space=pl.ANY)
SMEM = pl.BlockSpec(memory_space=pltpu.SMEM)


def turn(n, step):
    return [(i, (i + step) % n) for i in range(n)]


def dot_nt(a, b, **kw):
    return lax.dot_general(a, b, (((1,), (1,)), ((), ())), preferred_element_type=F32, **kw)


def dot_tt(a, b, **kw):
    return lax.dot_general(a, b, (((0,), (1,)), ((), ())), preferred_element_type=F32, **kw)


def pack_kernel(place, grad, gate, *rest):
    outs, sems = rest[:-1], rest[-1]
    hid = gate.shape[1]
    wide = (outs[0].shape[1] - hid) // NY
    y, x = place[0], place[1]
    copies = []
    for s, out in enumerate(outs):
        at = lax.rem(x + s + 1, NX)
        copies.append(pltpu.make_async_copy(gate, out.at[:, pl.ds(0, hid)], sems.at[s, NY]))
        for i in range(NY):
            start = pl.multiple_of((lax.rem(y - i + NY, NY) * NX + at) * wide, wide)
            copies.append(
                pltpu.make_async_copy(
                    grad.at[:, pl.ds(start, wide)], out.at[:, pl.ds(hid + i * wide, wide)], sems.at[s, i]
                )
            )
    for c in copies:
        c.start()
    for c in copies:
        c.wait()


def pack(place, grad, gate, wide):
    tok, hid = gate.shape
    out = jax.ShapeDtypeStruct((tok, hid + NY * wide), BF16)
    return pl.pallas_call(
        pack_kernel,
        out_shape=[out] * (NX - 1),
        in_specs=[SMEM, ANY, ANY],
        out_specs=[ANY] * (NX - 1),
        scratch_shapes=[pltpu.SemaphoreType.DMA((NX - 1, NY + 1))],
        cost_estimate=pl.CostEstimate(flops=0, bytes_accessed=7_000_000, transcendentals=0),
        name="pack",
    )(place, grad, gate)


def main_kernel(place, grad, gates_own, x1, x2, x3, w0, w1, w2, w3, far_a, far_b, w5, w6, w7, proj, out, g, gate, w, g_sem, w_sem):
    y, x = place[0], place[1]
    nx, tok, hid = gate.shape
    wide = w0.shape[1]
    half = hid // 2
    copies = [pltpu.make_async_copy(gates_own, gate.at[0], g_sem.at[0, NY])]
    for i in range(NY):
        start = pl.multiple_of((lax.rem(y - i + NY, NY) * NX + x) * wide, wide)
        copies.append(
            pltpu.make_async_copy(grad.at[:, pl.ds(start, wide)], g.at[0, :, pl.ds(i * wide, wide)], g_sem.at[0, i])
        )
    for s, got in enumerate((x1, x2, x3)):
        copies.append(pltpu.make_async_copy(got.at[:, pl.ds(0, hid)], gate.at[s + 1], g_sem.at[s + 1, 0]))
        copies.append(pltpu.make_async_copy(got.at[:, pl.ds(hid, NY * wide)], g.at[s + 1], g_sem.at[s + 1, 1]))
    for i, src in enumerate((w0, w1, w2, w3, None, w5, w6, w7)):
        if src is None:
            copies.append(
                pltpu.make_async_copy(far_a, w.at[pl.ds(0, half), pl.ds(i * wide, wide)], w_sem.at[i])
            )
            copies.append(
                pltpu.make_async_copy(far_b, w.at[pl.ds(half, half), pl.ds(i * wide, wide)], w_sem.at[NY])
            )
        else:
            copies.append(pltpu.make_async_copy(src, w.at[:, pl.ds(i * wide, wide)], w_sem.at[i]))
    for c in copies:
        c.start()
    for c in copies:
        c.wait()
    grads = g[...].reshape(nx * tok, NY * wide)
    gates = gate[...].reshape(nx * tok, hid)
    total = None
    start = 0
    while start < hid:
        size = min(256, hid - start)
        gh = dot_nt(grads, w[start : start + size, :])
        gp = gates[:, start : start + size].astype(F32)
        gu = gh * (gp / (1.0 + jnp.exp(-gp)))
        hi = gu.astype(BF16)
        lo = (gu - hi.astype(F32)).astype(BF16)
        p = proj[:, start : start + size]
        part = dot_nt(p, hi) + dot_nt(p, lo)
        total = part if total is None else total + part
        start += size
    per = total.shape[0] // NB
    for j in range(nx):
        to = lax.rem(x - j + nx, nx)
        for b in range(NB):
            out[to, b] = total[b * per : (b + 1) * per, j * tok : (j + 1) * tok]


def main(place, grad, gate, got, shards, proj):
    tok, hid = gate.shape
    wide = shards[0].shape[1]
    per = proj.shape[0] // NB
    macs = NX * tok * hid * (NY * wide + proj.shape[0])
    return pl.pallas_call(
        main_kernel,
        out_shape=jax.ShapeDtypeStruct((NX, NB, per, tok), F32),
        in_specs=[SMEM] + [ANY] * 14 + [pl.BlockSpec(memory_space=pltpu.VMEM)],
        out_specs=pl.BlockSpec(memory_space=pltpu.VMEM),
        scratch_shapes=[
            pltpu.VMEM((NX, tok, NY * wide), BF16),
            pltpu.VMEM((NX, tok, hid), BF16),
            pltpu.VMEM((hid, NY * wide), BF16),
            pltpu.SemaphoreType.DMA((NX, NY + 1)),
            pltpu.SemaphoreType.DMA((NY + 1,)),
        ],
        compiler_params=pltpu.CompilerParams(vmem_limit_bytes=32 << 20),
        cost_estimate=pl.CostEstimate(flops=2 * macs, bytes_accessed=10_000_000, transcendentals=NX * tok * hid),
        name="main",
    )(place, grad, gate, *got, *shards, proj)


def on_device(out_grad, layer_input, gate_pre, up_pre, down_weight, proj_hidden, proj_model, example_ids):
    y, x = lax.axis_index("y"), lax.axis_index("x")
    blk = lax.axis_index(ZC)
    place = jnp.stack([y, x]).astype(jnp.int32)
    tok, hid = gate_pre.shape
    half = hid // 2
    feat = layer_input.shape[1]
    grad_cols = lax.dynamic_slice_in_dim(out_grad, blk * feat, feat, 1)
    grad_part = dot_tt(proj_model, grad_cols)
    input_part = dot_tt(proj_model, layer_input)
    hidden = (jax.nn.silu(gate_pre.astype(F32)) * up_pre.astype(F32)).astype(BF16)
    hid_part = dot_tt(proj_hidden, hidden)
    early = jnp.concatenate(
        [jnp.concatenate([grad_part, input_part], 0).reshape(NB, -1, tok), hid_part.reshape(NB, -1, tok)], axis=1
    )

    up1 = lax.ppermute(down_weight, "y", turn(NY, 1))
    dn1 = lax.ppermute(down_weight, "y", turn(NY, -1))
    p1, p2, p3 = pack(place, out_grad, gate_pre, down_weight.shape[1])
    up1, dn1, early = lax.optimization_barrier((up1, dn1, early))
    x1, x2, x3 = [lax.ppermute(p, "x", turn(NX, s + 1)) for s, p in enumerate((p1, p2, p3))]
    up2 = lax.ppermute(up1, "y", turn(NY, 1))
    dn2 = lax.ppermute(dn1, "y", turn(NY, -1))
    early = jnp.sum(lax.all_to_all(early, ZC, 0, 0), axis=0)
    n_side = 2 * proj_model.shape[1] // NB
    up3 = lax.ppermute(up2, "y", turn(NY, 1))
    dn3 = lax.ppermute(dn2, "y", turn(NY, -1))
    sides = lax.all_to_all(jnp.broadcast_to(early[None, :n_side], (NB, n_side, tok)), ZC, 0, 0).reshape(2, -1, tok)
    hid_side = early[n_side:]
    up3, dn3, early, x1, x3 = lax.optimization_barrier((up3, dn3, early, x1, x3))
    far_a = lax.ppermute(up3[:half], "y", turn(NY, 1))
    far_b = lax.ppermute(dn3[half:], "y", turn(NY, -1))
    x2, far_a, far_b, sides = lax.optimization_barrier((x2, far_a, far_b, sides))

    up_part = main(place, out_grad, gate_pre, (x1, x2, x3), (down_weight, up1, up2, up3, far_a, far_b, dn3, dn2, dn1), proj_hidden.T)
    up_part = jnp.sum(lax.all_to_all(up_part, "x", 0, 0), axis=0)
    up_side = jnp.sum(lax.all_to_all(up_part, ZC, 0, 0), axis=0)

    picks = (example_ids == jnp.arange(2, dtype=jnp.int32)[:, None]).astype(F32)

    def scores(left, right):
        picked = (picks[:, None, :] * left[None]).reshape(-1, tok)
        return dot_nt(picked, right, precision=lax.Precision.HIGHEST).reshape(2, -1)

    return scores(hid_side, sides[0]), scores(up_side, sides[1])


def solution(mesh):
    fine = Mesh(mesh.devices.reshape(NY, NX, NZ, NC), ("y", "x", "z", "core"))
    yx = ("y", "x")
    in_specs = (P(yx, None), P(yx, ZC), P(yx, ZC), P(yx, ZC), P(ZC, yx), P(ZC, None), P(ZC, None), P(yx, None))
    out_specs = (P(yx, ZC), P(yx, ZC))
    return jax.shard_map(on_device, mesh=fine, in_specs=in_specs, out_specs=out_specs, check_vma=False)
```

time: 157 us -> 234 us (1.49)
  Pallas kernels: 0 us -> 115 us
  local copies, waits for them, and re-layouts: 37 us -> 9.77 us
  starting transfers between devices: 79.3 us -> 64.2 us
  blocking collectives: 0 us -> 8.21 us
  waiting for transfers between devices: 25.1 us -> 21.6 us
  matrix products: 9.39 us -> 5.94 us
    pallas_call x0 -> x2, Pallas kernels: none -> 115 us  [the longest x1 105 us: pack(): pl.pallas_call(pack_kernel, out_shape=[out] * (NX - 1), in_specs=[SMEM, A...]
    unnamed x35 -> x14, local copies, waits for them, and re-layouts: 23 us -> 2.02 us
    ppermute x7 -> x3, waiting for transfers between devices: 14.2 us -> 0.01 us  [on_device(): lax.ppermute(p, 'x', turn(NX, s + 1))]
    ppermute x7 -> x3, starting transfers between devices: 20.7 us -> 9.94 us  [on_device(): lax.ppermute(p, 'x', turn(NX, s + 1))]
    all_to_all x0 -> x1, blocking collectives: none -> 8.21 us  [on_device(): up_part = jnp.sum(lax.all_to_all(up_part, 'x', 0, 0), axis=0)]
    all_to_all x1, waiting for transfers between devices: 0.01 us -> 8.12 us  [on_device(): early = jnp.sum(lax.all_to_all(early, ZC, 0, 0), axis=0)]
    all_to_all x1, starting transfers between devices: 10.4 us -> 4.1 us  [on_device(): lax.all_to_all(jnp.broadcast_to(early[None, :n_side], (NB, n_side, tok)),...]
    concatenate x3 -> x0, local copies, waits for them, and re-layouts: 5.16 us -> none  [the longest x1 1.85 us: on_device(): jnp.concatenate([down_weight, up1, up2, up3, jnp.concatenate([far_a, far_...]
  transfers between devices with their start and end apart: 18 -> 14, of which waited for: 4 -> 5; matrix products, arithmetic and copies ran while one was open for 30% -> 6% of each run, Pallas kernels for 0% -> 45%
where the time goes in v2:
time: 234 us; the launch traced here: 231 us
  Pallas kernels  115 us (49%)
  starting transfers between devices  64.2 us (27%)
  waiting for transfers between devices  21.6 us (9%)
  local copies, waits for them, and re-layouts  9.77 us (4%)
  blocking collectives  8.21 us (4%)
  matrix products  5.94 us (3%)
  other arithmetic  4.91 us (2%)
    pallas_call x1, Pallas kernels, pack(): pl.pallas_call(pack_kernel, out_shape=[out] * (NX - 1), in_specs=[SMEM, A...  105 us
    all_to_all x1, starting transfers between devices, on_device(): early = jnp.sum(lax.all_to_all(early, ZC, 0, 0), axis=0)  12.7 us
    pallas_call x1, Pallas kernels, main(): pl.pallas_call(main_kernel, out_shape=jax.ShapeDtypeStruct((NX, NB, per,...  10.6 us
    all_to_all x1, starting transfers between devices, on_device(): up_side = jnp.sum(lax.all_to_all(up_part, ZC, 0, 0), axis=0)  10 us
    ppermute x3, starting transfers between devices, on_device(): lax.ppermute(p, 'x', turn(NX, s + 1))  9.94 us
    all_to_all x1, blocking collectives, on_device(): up_part = jnp.sum(lax.all_to_all(up_part, 'x', 0, 0), axis=0)  8.21 us
    all_to_all x1, waiting for transfers between devices, on_device(): early = jnp.sum(lax.all_to_all(early, ZC, 0, 0), axis=0)  8.12 us
    all_to_all x1, waiting for transfers between devices, on_device(): up_side = jnp.sum(lax.all_to_all(up_part, ZC, 0, 0), axis=0)  7.78 us
  transfers between devices with their start and end apart: 14, of which 5 were waited for; matrix products, arithmetic and copies ran while one was open for 6% of the time, Pallas kernels for 45%

profile of v2, /device:TPU:1, one launch (start us, length us, event | category | flops | bytes accessed | tf_op | source)
XLA Modules:
  0.0 231.0 jit_solution(8695211167674111915)
XLA Ops:
  0.6 4.2 %collective-permute-start = (bf16[896,256]{1,0:T(8,128)(2,1)}, bf16[896,256]{1,0:T(8,128)(2,1)}, u32[]{:S(2)}, u32[]{:S(2)}) collective-permute-start(bf16[896,256]{1,0:T(8,128)(2,1)} %w0.1), channel_id=1, source_target_pairs={{0,64},{64,128},{128,192},{192,256},{256,320},{320,384},{384,448},... | collective-permute-start | bytes 1376264 | tf_op jit(solution)/shard_map/ppermute | solution.py:156
  4.8 3.8 %collective-permute-start.1 = (bf16[896,256]{1,0:T(8,128)(2,1)}, bf16[896,256]{1,0:T(8,128)(2,1)}, u32[]{:S(2)}, u32[]{:S(2)}) collective-permute-start(bf16[896,256]{1,0:T(8,128)(2,1)} %w0.1), channel_id=1, source_target_pairs={{0,448},{64,0},{128,64},{192,128},{256,192},{320,256},{384,320},{4... | collective-permute-start | bytes 1376264 | tf_op jit(solution)/shard_map/ppermute | solution.py:157
  9.3 104.9 %pack.1 = (bf16[192,2944]{1,0:T(8,128)(2,1)}, bf16[192,2944]{1,0:T(8,128)(2,1)}, bf16[192,2944]{1,0:T(8,128)(2,1)}) custom-call(s32[2]{0:T(128)} %pad_add_fusion.place, bf16[192,8192]{1,0:T(8,128)(2,1)} %grad.3, bf16[192,896]{1,0:T(8,128)(2,1)} %gates_own.1), custom_call_target="tpu_custom_call" | custom-call | bytes 7000000 | tf_op jit(solution)/shard_map/pack/pallas_call | solution.py:56
  114.2 3.1 %collective-permute-start.7 = (bf16[192,2944]{1,0:T(8,128)(2,1)}, bf16[192,2944]{1,0:T(8,128)(2,1)}, u32[]{:S(2)}, u32[]{:S(2)}) collective-permute-start(bf16[192,2944]{1,0:T(8,128)(2,1)} %get-tuple-element.20), channel_id=1, source_target_pairs={{0,16},{16,32},{32,48},{48,0},{1,17},{17,33},{33,49},{49,1},{2,18}... | collective-permute-start | bytes 3391496 | tf_op jit(solution)/shard_map/ppermute | solution.py:160
  117.3 3.4 %collective-permute-start.8 = (bf16[192,2944]{1,0:T(8,128)(2,1)}, bf16[192,2944]{1,0:T(8,128)(2,1)}, u32[]{:S(2)}, u32[]{:S(2)}) collective-permute-start(bf16[192,2944]{1,0:T(8,128)(2,1)} %get-tuple-element.21), channel_id=1, source_target_pairs={{0,48},{16,0},{32,16},{48,32},{1,49},{17,1},{33,17},{49,33},{2,50}... | collective-permute-start | bytes 3391496 | tf_op jit(solution)/shard_map/ppermute | solution.py:160
  120.7 1.6 convolution_bitcast_fusion.1
  123.0 1.1 fusion.15
  124.1 1.1 convolution_bitcast_fusion
  125.9 1.8 copy.13
  127.7 1.8 pad_maximum_fusion
  129.4 1.9 collective-permute-start.3
  131.4 4.6 %collective-permute-start.5 = (bf16[896,256]{1,0:T(8,128)(2,1)}, bf16[896,256]{1,0:T(8,128)(2,1)}, u32[]{:S(2)}, u32[]{:S(2)}) collective-permute-start(bf16[896,256]{1,0:T(8,128)(2,1)} %collective-permute-done.1.w7), channel_id=1, source_target_pairs={{0,448},{64,0},{128,64},{192,128},{256,192},{320,256},{384,320},{4... | collective-permute-start | bytes 1376264 | tf_op jit(solution)/shard_map/ppermute | solution.py:162
  136.0 3.4 %collective-permute-start.2 = (bf16[192,2944]{1,0:T(8,128)(2,1)}, bf16[192,2944]{1,0:T(8,128)(2,1)}, u32[]{:S(2)}, u32[]{:S(2)}) collective-permute-start(bf16[192,2944]{1,0:T(8,128)(2,1)} %get-tuple-element.17), channel_id=1, source_target_pairs={{0,32},{16,48},{32,0},{48,16},{1,33},{17,49},{33,1},{49,17},{2,34}... | collective-permute-start | bytes 3391496 | tf_op jit(solution)/shard_map/ppermute | solution.py:160
  139.4 12.7 %all-to-all-start = ((f32[16,20,192]{2,1,0:T(8,128)}), f32[16,20,192]{2,1,0:T(8,128)}, u32[]{:S(2)}, u32[]{:S(2)}) async-start(f32[16,20,192]{2,1,0:T(8,128)} %pad_maximum_fusion), calls=%async_computation | async-start | bytes 786432 | tf_op jit(solution)/shard_map/all_to_all | solution.py:163
  152.1 1.9 collective-permute-start.4
  154.1 4.6 %collective-permute-start.6 = (bf16[896,256]{1,0:T(8,128)(2,1)}, bf16[896,256]{1,0:T(8,128)(2,1)}, u32[]{:S(2)}, u32[]{:S(2)}) collective-permute-start(bf16[896,256]{1,0:T(8,128)(2,1)} %collective-permute-done.5.w6), channel_id=1, source_target_pairs={{0,448},{64,0},{128,64},{192,128},{256,192},{320,256},{384,320},{4... | collective-permute-start | bytes 1376264 | tf_op jit(solution)/shard_map/ppermute | solution.py:166
  158.6 8.1 %all-to-all-done = f32[16,20,192]{2,1,0:T(8,128)} async-done(((f32[16,20,192]{2,1,0:T(8,128)}), f32[16,20,192]{2,1,0:T(8,128)}, u32[]{:S(2)}, u32[]{:S(2)}) %all-to-all-start) | async-done | bytes 245792 | tf_op jit(solution)/shard_map/all_to_all | solution.py:163
  166.8 1.0 reduce_sum.27
  168.5 4.1 %all-to-all-start.1 = ((f32[16,16,192]{2,1,0:T(8,128)}), f32[16,16,192]{2,1,0:T(8,128)}, u32[]{:S(2)}, u32[]{:S(2)}) async-start(f32[16,16,192]{2,1,0:T(8,128)} %broadcast_in_dim.2), calls=%async_computation.1 | async-start | bytes 524288 | tf_op jit(solution)/shard_map/all_to_all | solution.py:167
  172.7 1.6 slice.19
  174.3 1.9 collective-permute-start.9
  176.2 1.7 slice.20
  177.9 4.6 %collective-permute-start.10 = (bf16[448,256]{1,0:T(8,128)(2,1)}, bf16[448,256]{1,0:T(8,128)(2,1)}, u32[]{:S(2)}, u32[]{:S(2)}) collective-permute-start(bf16[448,256]{1,0:T(8,128)(2,1)} %slice.20), channel_id=1, source_target_pairs={{0,448},{64,0},{128,64},{192,128},{256,192},{320,256},{384,320},{4... | collective-permute-start | bytes 688136 | tf_op jit(solution)/shard_map/ppermute | solution.py:171
  183.4 1.5 collective-permute-done.9.far_a
  184.9 3.2 %collective-permute-done.10.far_b = bf16[448,256]{1,0:T(8,128)(2,1)} collective-permute-done((bf16[448,256]{1,0:T(8,128)(2,1)}, bf16[448,256]{1,0:T(8,128)(2,1)}, u32[]{:S(2)}, u32[]{:S(2)}) %collective-permute-start.10) | collective-permute-done | bytes 229408 | tf_op jit(solution)/shard_map/ppermute | solution.py:171
  189.1 1.0 copy-done.3
  190.1 10.6 %main.1 = f32[4,16,4,192]{3,2,1,0:T(4,128)S(1)} custom-call(s32[2]{0:T(128)S(1)} %copy-done.5, bf16[192,8192]{1,0:T(8,128)(2,1)S(1)} %copy-done.1, bf16[192,896]{1,0:T(8,128)(2,1)S(1)} %copy-done.2, bf16[192,2944]{1,0:T(8,128)(2,1)} %collective-permute-done.7.x1, bf16[192,2944]{1,0:T(8,128)(2,1)} %collective-permute-done.2.x2, ...), custom_call_target="tpu_custom_call" | custom-call | flops 2906652672 | bytes 10000000 | tf_op jit(solution)/shard_map/main/pallas_call | solution.py:122
  200.7 8.2 %all_to_all.20 = f32[4,16,4,192]{3,2,1,0:T(4,128)S(1)} all-to-all(f32[4,16,4,192]{3,2,1,0:T(4,128)S(1)} %main.1), channel_id=1, replica_groups=mesh['y'=8,'x'=4,'z'=8,'core'=2] {'x'}, dimensions={0} | all-to-all | bytes 393216 | tf_op jit(solution)/shard_map/all_to_all | solution.py:175
  209.6 10.0 %all-to-all-start.3 = ((f32[16,4,192]{2,1,0:T(4,128)}), f32[16,4,192]{2,1,0:T(4,128)S(1)}, u32[]{:S(2)}, u32[]{:S(2)}) async-start(f32[16,4,192]{2,1,0:T(4,128)} %reduce_sum.28), calls=%async_computation.3 | async-start | bytes 131072 | tf_op jit(solution)/shard_map/all_to_all | solution.py:176
  219.7 7.8 %all-to-all-done.3 = f32[16,4,192]{2,1,0:T(4,128)S(1)} async-done(((f32[16,4,192]{2,1,0:T(4,128)}), f32[16,4,192]{2,1,0:T(4,128)S(1)}, u32[]{:S(2)}, u32[]{:S(2)}) %all-to-all-start.3) | async-done | bytes 49184 | tf_op jit(solution)/shard_map/all_to_all | solution.py:176
  227.5 1.1 fusion.9
  229.2 1.1 fusion.7
  (37 shorter events, 6.8 us)
Async XLA Ops:
  0.6 122.4 %copy-start = (bf16[192,512]{1,0:T(8,128)(2,1)S(1)}, bf16[192,512]{1,0:T(8,128)(2,1)}, u32[]{:S(2)}) copy-start(bf16[192,512]{1,0:T(8,128)(2,1)} %param.9) | copy-start | bytes 589828
  0.6 128.8 %collective-permute-start = (bf16[896,256]{1,0:T(8,128)(2,1)}, bf16[896,256]{1,0:T(8,128)(2,1)}, u32[]{:S(2)}, u32[]{:S(2)}) collective-permute-start(bf16[896,256]{1,0:T(8,128)(2,1)} %w0.1), channel_id=1, source_target_pairs={{0,64},{64,128},{128,192},{192,256},{256,320},{320,384},{384,448},... | collective-permute-start | bytes 1376264 | tf_op jit(solution)/shard_map/ppermute | solution.py:156
  4.8 124.6 %collective-permute-start.1 = (bf16[896,256]{1,0:T(8,128)(2,1)}, bf16[896,256]{1,0:T(8,128)(2,1)}, u32[]{:S(2)}, u32[]{:S(2)}) collective-permute-start(bf16[896,256]{1,0:T(8,128)(2,1)} %w0.1), channel_id=1, source_target_pairs={{0,448},{64,0},{128,64},{192,128},{256,192},{320,256},{384,320},{4... | collective-permute-start | bytes 1376264 | tf_op jit(solution)/shard_map/ppermute | solution.py:157
  9.3 111.4 %copy-start.4 = (bf16[896,64]{0,1:T(8,128)(2,1)S(1)}, bf16[896,64]{0,1:T(8,128)(2,1)}, u32[]{:S(2)}) copy-start(bf16[896,64]{0,1:T(8,128)(2,1)} %param.13) | copy-start | bytes 344068
  114.2 58.4 %collective-permute-start.7 = (bf16[192,2944]{1,0:T(8,128)(2,1)}, bf16[192,2944]{1,0:T(8,128)(2,1)}, u32[]{:S(2)}, u32[]{:S(2)}) collective-permute-start(bf16[192,2944]{1,0:T(8,128)(2,1)} %get-tuple-element.20), channel_id=1, source_target_pairs={{0,16},{16,32},{32,48},{48,0},{1,17},{17,33},{33,49},{49,1},{2,18}... | collective-permute-start | bytes 3391496 | tf_op jit(solution)/shard_map/ppermute | solution.py:160
  117.3 55.3 %collective-permute-start.8 = (bf16[192,2944]{1,0:T(8,128)(2,1)}, bf16[192,2944]{1,0:T(8,128)(2,1)}, u32[]{:S(2)}, u32[]{:S(2)}) collective-permute-start(bf16[192,2944]{1,0:T(8,128)(2,1)} %get-tuple-element.21), channel_id=1, source_target_pairs={{0,48},{16,0},{32,16},{48,32},{1,49},{17,1},{33,17},{49,33},{2,50}... | collective-permute-start | bytes 3391496 | tf_op jit(solution)/shard_map/ppermute | solution.py:160
  120.7 3.4 %copy-start.1 = (bf16[192,8192]{1,0:T(8,128)(2,1)S(1)}, bf16[192,8192]{1,0:T(8,128)(2,1)}, u32[]{:S(2)}) copy-start(bf16[192,8192]{1,0:T(8,128)(2,1)} %grad.3) | copy-start | bytes 9437188
  129.4 22.7 %collective-permute-start.3 = (bf16[896,256]{1,0:T(8,128)(2,1)}, bf16[896,256]{1,0:T(8,128)(2,1)}, u32[]{:S(2)}, u32[]{:S(2)}) collective-permute-start(bf16[896,256]{1,0:T(8,128)(2,1)} %collective-permute-done.w1), channel_id=1, source_target_pairs={{0,64},{64,128},{128,192},{192,256},{256,320},{320,384},{384,448},... | collective-permute-start | bytes 1376264 | tf_op jit(solution)/shard_map/ppermute | solution.py:161
  131.4 22.7 %collective-permute-start.5 = (bf16[896,256]{1,0:T(8,128)(2,1)}, bf16[896,256]{1,0:T(8,128)(2,1)}, u32[]{:S(2)}, u32[]{:S(2)}) collective-permute-start(bf16[896,256]{1,0:T(8,128)(2,1)} %collective-permute-done.1.w7), channel_id=1, source_target_pairs={{0,448},{64,0},{128,64},{192,128},{256,192},{320,256},{384,320},{4... | collective-permute-start | bytes 1376264 | tf_op jit(solution)/shard_map/ppermute | solution.py:162
  136.0 46.5 %collective-permute-start.2 = (bf16[192,2944]{1,0:T(8,128)(2,1)}, bf16[192,2944]{1,0:T(8,128)(2,1)}, u32[]{:S(2)}, u32[]{:S(2)}) collective-permute-start(bf16[192,2944]{1,0:T(8,128)(2,1)} %get-tuple-element.17), channel_id=1, source_target_pairs={{0,32},{16,48},{32,0},{48,16},{1,33},{17,49},{33,1},{49,17},{2,34}... | collective-permute-start | bytes 3391496 | tf_op jit(solution)/shard_map/ppermute | solution.py:160
  139.4 27.3 %all-to-all-start = ((f32[16,20,192]{2,1,0:T(8,128)}), f32[16,20,192]{2,1,0:T(8,128)}, u32[]{:S(2)}, u32[]{:S(2)}) async-start(f32[16,20,192]{2,1,0:T(8,128)} %pad_maximum_fusion), calls=%async_computation | async-start | bytes 786432 | tf_op jit(solution)/shard_map/all_to_all | solution.py:163
  152.1 36.0 %copy-start.5 = (s32[2]{0:T(128)S(1)}, s32[2]{0:T(128)}, u32[]{:S(2)}) copy-start(s32[2]{0:T(128)} %pad_add_fusion.place) | copy-start | bytes 28
  152.1 20.5 %collective-permute-start.4 = (bf16[896,256]{1,0:T(8,128)(2,1)}, bf16[896,256]{1,0:T(8,128)(2,1)}, u32[]{:S(2)}, u32[]{:S(2)}) collective-permute-start(bf16[896,256]{1,0:T(8,128)(2,1)} %collective-permute-done.3.w2), channel_id=1, source_target_pairs={{0,64},{64,128},{128,192},{192,256},{256,320},{320,384},{384,448},... | collective-permute-start | bytes 1376264 | tf_op jit(solution)/shard_map/ppermute | solution.py:165
  154.1 18.6 %collective-permute-start.6 = (bf16[896,256]{1,0:T(8,128)(2,1)}, bf16[896,256]{1,0:T(8,128)(2,1)}, u32[]{:S(2)}, u32[]{:S(2)}) collective-permute-start(bf16[896,256]{1,0:T(8,128)(2,1)} %collective-permute-done.5.w6), channel_id=1, source_target_pairs={{0,448},{64,0},{128,64},{192,128},{256,192},{320,256},{384,320},{4... | collective-permute-start | bytes 1376264 | tf_op jit(solution)/shard_map/ppermute | solution.py:166
  168.5 14.9 %all-to-all-start.1 = ((f32[16,16,192]{2,1,0:T(8,128)}), f32[16,16,192]{2,1,0:T(8,128)}, u32[]{:S(2)}, u32[]{:S(2)}) async-start(f32[16,16,192]{2,1,0:T(8,128)} %broadcast_in_dim.2), calls=%async_computation.1 | async-start | bytes 524288 | tf_op jit(solution)/shard_map/all_to_all | solution.py:167
  174.3 10.6 %collective-permute-start.9 = (bf16[448,256]{1,0:T(8,128)(2,1)}, bf16[448,256]{1,0:T(8,128)(2,1)}, u32[]{:S(2)}, u32[]{:S(2)}) collective-permute-start(bf16[448,256]{1,0:T(8,128)(2,1)} %slice.19), channel_id=1, source_target_pairs={{0,64},{64,128},{128,192},{192,256},{256,320},{320,384},{384,448},... | collective-permute-start | bytes 688136 | tf_op jit(solution)/shard_map/ppermute | solution.py:170
  177.9 10.2 %collective-permute-start.10 = (bf16[448,256]{1,0:T(8,128)(2,1)}, bf16[448,256]{1,0:T(8,128)(2,1)}, u32[]{:S(2)}, u32[]{:S(2)}) collective-permute-start(bf16[448,256]{1,0:T(8,128)(2,1)} %slice.20), channel_id=1, source_target_pairs={{0,448},{64,0},{128,64},{192,128},{256,192},{320,256},{384,320},{4... | collective-permute-start | bytes 688136 | tf_op jit(solution)/shard_map/ppermute | solution.py:171
  188.1 1.0 copy-start.2
  189.1 1.0 copy-start.3
  190.1 29.5 %copy-start.6 = (s32[1,192]{1,0:T(1,128)S(1)}, s32[1,192]{1,0:T(1,128)}, u32[]{:S(2)}) copy-start(s32[1,192]{1,0:T(1,128)} %param.15) | copy-start | bytes 2308
  209.6 17.8 %all-to-all-start.3 = ((f32[16,4,192]{2,1,0:T(4,128)}), f32[16,4,192]{2,1,0:T(4,128)S(1)}, u32[]{:S(2)}, u32[]{:S(2)}) async-start(f32[16,4,192]{2,1,0:T(4,128)} %reduce_sum.28), calls=%async_computation.3 | async-start | bytes 131072 | tf_op jit(solution)/shard_map/all_to_all | solution.py:176

commit v3 on v1

v3 whole, which is shorter than its diff:
```python
import jax
import jax.numpy as jnp
from jax import lax
from jax.experimental import pallas as pl
from jax.experimental.pallas import tpu as pltpu
from jax.sharding import Mesh
from jax.sharding import PartitionSpec as P

NY, NX, NZ, NC = 8, 4, 8, 2
NB = NZ * NC
FAR = NY // 2
ZC = ("z", "core")
BF16, F32 = jnp.bfloat16, jnp.float32
HBM = pl.BlockSpec(memory_space=pltpu.HBM)
VMEM = pl.BlockSpec(memory_space=pltpu.VMEM)
SMEM = pl.BlockSpec(memory_space=pltpu.SMEM)
PARAMS = pltpu.CompilerParams(vmem_limit_bytes=40 << 20)


def turn(n, step):
    return [(i, (i + step) % n) for i in range(n)]


def dot_nt(a, b, **kw):
    return lax.dot_general(a, b, (((1,), (1,)), ((), ())), preferred_element_type=F32, **kw)


def silu(v):
    return v / (1.0 + jnp.exp(-v))


def columns(y, back, x, wide):
    return pl.multiple_of((lax.rem(y - back + NY, NY) * NX + x) * wide, wide)


def prepare_kernel(place, grad, gate, up, inp, model, hproj, p1, p2, p3, early, buf, gate_v, up_v, inp_v, gcols, model_v, hproj_v, in_sem, out_sem, side_sem):
    outs = (p1, p2, p3)
    tok, hid = gate.shape
    wide = (p1.shape[1] - hid) // NY
    feat = inp.shape[1]
    y, x, blk = place[0], place[1], place[2]
    fills, sends = [], []
    for s, out in enumerate(outs):
        at = lax.rem(x + s + 1, NX)
        fill = [pltpu.make_async_copy(gate, buf.at[s, :, pl.ds(0, hid)], in_sem.at[s, NY])]
        for i in range(NY):
            fill.append(
                pltpu.make_async_copy(
                    grad.at[:, pl.ds(columns(y, i, at, wide), wide)],
                    buf.at[s, :, pl.ds(hid + i * wide, wide)],
                    in_sem.at[s, i],
                )
            )
        fills.append(fill)
        sends.append(pltpu.make_async_copy(buf.at[s], out, out_sem.at[s]))
        for c in fill:
            c.start()
    loads = [
        pltpu.make_async_copy(gate, gate_v, side_sem.at[0]),
        pltpu.make_async_copy(up, up_v, side_sem.at[1]),
        pltpu.make_async_copy(inp, inp_v, side_sem.at[2]),
        pltpu.make_async_copy(grad.at[:, pl.ds(pl.multiple_of(blk * feat, feat), feat)], gcols, side_sem.at[3]),
        pltpu.make_async_copy(model, model_v, side_sem.at[4]),
        pltpu.make_async_copy(hproj, hproj_v, side_sem.at[5]),
    ]
    for c in loads:
        c.start()
    for fill, send in zip(fills, sends):
        for c in fill:
            c.wait()
        send.start()
    for c in loads:
        c.wait()
    hidden = (silu(gate_v[...].astype(F32)) * up_v[...].astype(F32)).astype(BF16)
    hid_side = dot_nt(hproj_v[...], hidden)
    m = model_v[...]
    parts = [jnp.dot(v[...], m, preferred_element_type=F32).T for v in (gcols, inp_v)]
    side = 2 * model.shape[1] // NB
    per = hproj.shape[0] // NB
    for b in range(NB):
        part = parts[b // (NB // 2)]
        r = (b % (NB // 2)) * side
        early[b, 0:side, :] = part[r : r + side, :]
        early[b, side : side + per, :] = hid_side[b * per : (b + 1) * per, :]
    for c in sends:
        c.wait()


def prepare(place, grad, gate, up, inp, model, hproj, wide):
    tok, hid = gate.shape
    feat = inp.shape[1]
    out = jax.ShapeDtypeStruct((tok, hid + NY * wide), BF16)
    rows = 2 * model.shape[1] // NB + hproj.shape[0] // NB
    return pl.pallas_call(
        prepare_kernel,
        out_shape=[out] * 3 + [jax.ShapeDtypeStruct((NB, rows, tok), F32)],
        in_specs=[SMEM] + [HBM] * 6,
        out_specs=[HBM] * 3 + [VMEM],
        scratch_shapes=[
            pltpu.VMEM((NX - 1, tok, hid + NY * wide), BF16),
            pltpu.VMEM((tok, hid), BF16),
            pltpu.VMEM((tok, hid), BF16),
            pltpu.VMEM((tok, feat), BF16),
            pltpu.VMEM((tok, feat), BF16),
            pltpu.VMEM(model.shape, BF16),
            pltpu.VMEM(hproj.shape, BF16),
            pltpu.SemaphoreType.DMA((NX - 1, NY + 1)),
            pltpu.SemaphoreType.DMA((NX - 1,)),
            pltpu.SemaphoreType.DMA((6,)),
        ],
        compiler_params=pltpu.CompilerParams(vmem_limit_bytes=60 << 20),
        cost_estimate=pl.CostEstimate(flops=80_000_000, bytes_accessed=8_000_000, transcendentals=tok * hid),
        name="prepare",
    )(place, grad, gate, up, inp, model, hproj)


def share_kernel(got, out, hid_side):
    total = got[0]
    for b in range(1, NB):
        total = total + got[b]
    side = out.shape[1]
    for b in range(NB):
        out[b] = total[:side]
    hid_side[...] = total[side:]


def share(got):
    _, rows, tok = got.shape
    per = rows - NB
    return pl.pallas_call(
        share_kernel,
        out_shape=[jax.ShapeDtypeStruct((NB, rows - per, tok), F32), jax.ShapeDtypeStruct((per, tok), F32)],
        in_specs=[VMEM],
        out_specs=[VMEM, VMEM],
        name="share",
    )(got)


def near_kernel(place, grad, x1, x2, x3, w0, w1, w2, w3, w5, w6, w7, acc, g, w, g_sem, w_sem):
    y, x = place[0], place[1]
    nx, tok, hid = acc.shape
    wide = w0.shape[1]
    shards = (w0, w1, w2, w3, None, w5, w6, w7)
    live = [i for i in range(NY) if i != FAR]
    copies = []
    for k, i in enumerate(live):
        copies.append(pltpu.make_async_copy(shards[i], w.at[:, pl.ds(k * wide, wide)], w_sem.at[k]))
        copies.append(
            pltpu.make_async_copy(
                grad.at[:, pl.ds(columns(y, i, x, wide), wide)], g.at[0, :, pl.ds(k * wide, wide)], g_sem.at[0, k]
            )
        )
    low = FAR * wide
    high = (NY - 1 - FAR) * wide
    for s, got in enumerate((x1, x2, x3)):
        copies.append(pltpu.make_async_copy(got.at[:, pl.ds(hid, low)], g.at[s + 1, :, pl.ds(0, low)], g_sem.at[s + 1, 0]))
        copies.append(
            pltpu.make_async_copy(
                got.at[:, pl.ds(hid + low + wide, high)], g.at[s + 1, :, pl.ds(low, high)], g_sem.at[s + 1, 1]
            )
        )
    for c in copies:
        c.start()
    for c in copies:
        c.wait()
    grads = g[...].reshape(nx * tok, len(live) * wide)
    start = 0
    while start < hid:
        size = min(256, hid - start)
        acc[:, :, start : start + size] = dot_nt(grads, w[start : start + size, :]).reshape(nx, tok, size)
        start += size


def near(place, grad, got, shards):
    tok = grad.shape[0]
    hid, wide = shards[0].shape
    k = (NY - 1) * wide
    return pl.pallas_call(
        near_kernel,
        out_shape=jax.ShapeDtypeStruct((NX, tok, hid), F32),
        in_specs=[SMEM] + [HBM] * 11,
        out_specs=VMEM,
        scratch_shapes=[
            pltpu.VMEM((NX, tok, k), BF16),
            pltpu.VMEM((hid, k), BF16),
            pltpu.SemaphoreType.DMA((NX, NY - 1)),
            pltpu.SemaphoreType.DMA((NY - 1,)),
        ],
        compiler_params=PARAMS,
        cost_estimate=pl.CostEstimate(flops=2 * NX * tok * hid * k, bytes_accessed=9_000_000, transcendentals=0),
        name="near",
    )(place, grad, *got, *shards)


def far_kernel(place, acc, grad, gate_own, x1, x2, x3, w4, proj, out, a_v, g, gate, w, p, sems):
    y, x = place[0], place[1]
    nx, tok, hid = acc.shape
    wide = w4.shape[1]
    per = proj.shape[0] // NB
    heads = [pltpu.make_async_copy(w4, w, sems.at[nx, 0]), pltpu.make_async_copy(proj, p, sems.at[nx, 1])]
    for c in heads:
        c.start()
    waits = []
    for s, got in enumerate((None, x1, x2, x3)):
        if got is None:
            mine = [
                pltpu.make_async_copy(grad.at[:, pl.ds(columns(y, FAR, x, wide), wide)], g.at[s], sems.at[s, 0]),
                pltpu.make_async_copy(gate_own, gate.at[s], sems.at[s, 1]),
            ]
        else:
            mine = [
                pltpu.make_async_copy(got.at[:, pl.ds(hid + FAR * wide, wide)], g.at[s], sems.at[s, 0]),
                pltpu.make_async_copy(got.at[:, pl.ds(0, hid)], gate.at[s], sems.at[s, 1]),
            ]
        mine.append(pltpu.make_async_copy(acc.at[s], a_v.at[s], sems.at[s, 2]))
        for c in mine:
            c.start()
        waits.append(mine)
    for c in heads:
        c.wait()
    for s in range(nx):
        for c in waits[s]:
            c.wait()
        gh = a_v[s] + dot_nt(g[s], w[...])
        gu = gh * silu(gate[s].astype(F32))
        hi = gu.astype(BF16)
        lo = (gu - hi.astype(F32)).astype(BF16)
        part = dot_nt(p[...], hi) + dot_nt(p[...], lo)
        to = lax.rem(x - s + nx, nx)
        for b in range(NB):
            out[to, b] = part[b * per : (b + 1) * per, :]


def far(place, acc, grad, gate, got, w4, proj):
    nx, tok, hid = acc.shape
    wide = w4.shape[1]
    per = proj.shape[0] // NB
    return pl.pallas_call(
        far_kernel,
        out_shape=jax.ShapeDtypeStruct((nx, NB, per, tok), F32),
        in_specs=[SMEM] + [HBM] * 8,
        out_specs=VMEM,
        scratch_shapes=[
            pltpu.VMEM((nx, tok, hid), F32),
            pltpu.VMEM((nx, tok, wide), BF16),
            pltpu.VMEM((nx, tok, hid), BF16),
            pltpu.VMEM((hid, wide), BF16),
            pltpu.VMEM(proj.shape, BF16),
            pltpu.SemaphoreType.DMA((nx + 1, 3)),
        ],
        compiler_params=PARAMS,
        cost_estimate=pl.CostEstimate(
            flops=2 * nx * tok * hid * (wide + 128), bytes_accessed=6_000_000, transcendentals=nx * tok * hid
        ),
        name="far",
    )(place, acc, grad, gate, *got, w4, proj)


def finish_kernel(got, hid_side, sides, ids, down, up):
    up_side = got[0]
    for b in range(1, got.shape[0]):
        up_side = up_side + got[b]
    half = NB // 2
    tok = ids.shape[1]
    which = ids[...]
    for left, first, out in ((hid_side[...], 0, down), (up_side, half, up)):
        right = sides[first : first + half].reshape(-1, tok)
        picked = jnp.concatenate([jnp.where(which == e, left, 0.0) for e in range(2)], axis=0)
        res = dot_nt(picked, right, precision=lax.Precision.HIGHEST)
        per, width = left.shape[0], right.shape[0]
        for e in range(2):
            for k in range(per):
                r = e * per + k
                out[e : e + 1, k * width : (k + 1) * width] = res[r : r + 1, :]


def finish(got, hid_side, sides, ids):
    per = hid_side.shape[0]
    width = sides.shape[1] * NB // 2
    out = jax.ShapeDtypeStruct((2, per * width), F32)
    return pl.pallas_call(
        finish_kernel, out_shape=[out, out], in_specs=[VMEM] * 4, out_specs=[VMEM, VMEM], name="finish"
    )(got, hid_side, sides, ids)


def on_device(out_grad, layer_input, gate_pre, up_pre, down_weight, proj_hidden, proj_model, example_ids):
    place = jnp.stack([lax.axis_index("y"), lax.axis_index("x"), lax.axis_index(ZC)]).astype(jnp.int32)
    hproj = proj_hidden.T
    up1 = lax.ppermute(down_weight, "y", turn(NY, 1))
    dn1 = lax.ppermute(down_weight, "y", turn(NY, -1))
    p1, p2, p3, early = prepare(
        place, out_grad, gate_pre, up_pre, layer_input, proj_model, hproj, down_weight.shape[1]
    )
    up1, dn1, early = lax.optimization_barrier((up1, dn1, early))
    x1, x2, x3 = [lax.ppermute(p, "x", turn(NX, s + 1)) for s, p in enumerate((p1, p2, p3))]
    up2 = lax.ppermute(up1, "y", turn(NY, 1))
    dn2 = lax.ppermute(dn1, "y", turn(NY, -1))
    early = lax.all_to_all(early, ZC, 0, 0)
    wide_sides, hid_side = share(early)
    up3 = lax.ppermute(up2, "y", turn(NY, 1))
    dn3 = lax.ppermute(dn2, "y", turn(NY, -1))
    sides = lax.all_to_all(wide_sides, ZC, 0, 0)
    up3, dn3, hid_side, x1, x3 = lax.optimization_barrier((up3, dn3, hid_side, x1, x3))
    w4 = lax.ppermute(up3, "y", turn(NY, 1))
    x2, sides = lax.optimization_barrier((x2, sides))
    acc = near(place, out_grad, (x1, x2, x3), (down_weight, up1, up2, up3, dn3, dn2, dn1))
    up_part = far(place, acc, out_grad, gate_pre, (x1, x2, x3), w4, hproj)
    up_side = lax.all_to_all(up_part.reshape((NX * NB,) + up_part.shape[2:]), ("x",) + ZC, 0, 0)
    return tuple(finish(up_side, hid_side, sides, example_ids))


def solution(mesh):
    fine = Mesh(mesh.devices.reshape(NY, NX, NZ, NC), ("y", "x", "z", "core"))
    yx = ("y", "x")
    in_specs = (P(yx, None), P(yx, ZC), P(yx, ZC), P(yx, ZC), P(ZC, yx), P(ZC, None), P(ZC, None), P(yx, None))
    out_specs = (P(yx, ZC), P(yx, ZC))
    return jax.shard_map(on_device, mesh=fine, in_specs=in_specs, out_specs=out_specs, check_vma=False)
```

time: 157 us -> 117 us (0.75)
  local copies, waits for them, and re-layouts: 37 us -> 1.04 us
  starting transfers between devices: 79.3 us -> 49.7 us
  blocking collectives: 0 us -> 26.2 us
  Pallas kernels: 0 us -> 21 us
  matrix products: 9.39 us -> 0 us
  waiting for transfers between devices: 25.1 us -> 16.8 us
  other arithmetic: 3.09 us -> 0.66 us
    all_to_all x0 -> x1, blocking collectives: none -> 26.2 us  [on_device(): lax.all_to_all(up_part.reshape((NX * NB,) + up_part.shape[2:]), ('x',) +...]
    unnamed x35 -> x10, local copies, waits for them, and re-layouts: 23 us -> 1.04 us
    pallas_call x0 -> x5, Pallas kernels: none -> 21 us  [the longest x1 6.3 us: near(): pl.pallas_call(near_kernel, out_shape=jax.ShapeDtypeStruct((NX, tok, hid)...]
    all_to_all x3 -> x2, starting transfers between devices: 32.3 us -> 16.8 us  [the longest x1 12.7 us: on_device(): early = lax.all_to_all(early, ZC, 0, 0)]
    ppermute x9 -> x4, waiting for transfers between devices: 17.3 us -> 2.26 us  [the longest x3 2.26 us: on_device(): lax.ppermute(p, 'x', turn(NX, s + 1))]
    ppermute x9 -> x4, starting transfers between devices: 26 us -> 12 us  [the longest x3 9.97 us: on_device(): lax.ppermute(p, 'x', turn(NX, s + 1))]
    dot_general x6 -> x0, matrix products: 9.39 us -> none  [the longest x3 6.73 us: dot_nt(): lax.dot_general(a, b, (((1,), (1,)), ((), ())), preferred_element_type=F3...]
    all_to_all x3 -> x2, waiting for transfers between devices: 7.79 us -> 14.6 us  [the longest x1 8.13 us: on_device(): early = lax.all_to_all(early, ZC, 0, 0)]
  transfers between devices with their start and end apart: 18 -> 12, of which waited for: 4 -> 3; matrix products, arithmetic and copies ran while one was open for 30% -> 1% of each run, Pallas kernels for 0% -> 12%
where the time goes in v3:
time: 117 us; the launch traced here: 116 us
  starting transfers between devices  49.7 us (42%)
  blocking collectives  26.2 us (22%)
  Pallas kernels  21 us (18%)
  waiting for transfers between devices  16.8 us (14%)
    all_to_all x1, blocking collectives, on_device(): lax.all_to_all(up_part.reshape((NX * NB,) + up_part.shape[2:]), ('x',) +...  26.2 us
    all_to_all x1, starting transfers between devices, on_device(): early = lax.all_to_all(early, ZC, 0, 0)  12.7 us
    ppermute x3, starting transfers between devices, on_device(): lax.ppermute(p, 'x', turn(NX, s + 1))  9.97 us
    all_to_all x1, waiting for transfers between devices, on_device(): early = lax.all_to_all(early, ZC, 0, 0)  8.13 us
    all_to_all x1, waiting for transfers between devices, on_device(): sides = lax.all_to_all(wide_sides, ZC, 0, 0)  6.42 us
    pallas_call x1, Pallas kernels, near(): pl.pallas_call(near_kernel, out_shape=jax.ShapeDtypeStruct((NX, tok, hid)...  6.3 us
    pallas_call x1, Pallas kernels, prepare(): pl.pallas_call(prepare_kernel, out_shape=[out] * 3 + [jax.ShapeDtypeStruc...  5.71 us
    pallas_call x1, Pallas kernels, far(): pl.pallas_call(far_kernel, out_shape=jax.ShapeDtypeStruct((nx, NB, per, t...  5.2 us
  transfers between devices with their start and end apart: 12, of which 3 were waited for; matrix products, arithmetic and copies ran while one was open for 1% of the time, Pallas kernels for 12%

profile of v3, /device:TPU:1, one launch (start us, length us, event | category | flops | bytes accessed | tf_op | source)
XLA Modules:
  0.0 116.3 jit_solution(7591697003476940894)
XLA Ops:
  0.6 4.0 %collective-permute-start = (bf16[896,256]{1,0:T(8,128)(2,1)}, bf16[896,256]{1,0:T(8,128)(2,1)}, u32[]{:S(2)}, u32[]{:S(2)}) collective-permute-start(bf16[896,256]{1,0:T(8,128)(2,1)} %w0.1), channel_id=1, source_target_pairs={{0,64},{64,128},{128,192},{192,256},{256,320},{320,384},{384,448},... | collective-permute-start | bytes 1376264 | tf_op jit(solution)/shard_map/ppermute | solution.py:289
  4.7 3.8 %collective-permute-start.1 = (bf16[896,256]{1,0:T(8,128)(2,1)}, bf16[896,256]{1,0:T(8,128)(2,1)}, u32[]{:S(2)}, u32[]{:S(2)}) collective-permute-start(bf16[896,256]{1,0:T(8,128)(2,1)} %w0.1), channel_id=1, source_target_pairs={{0,448},{64,0},{128,64},{192,128},{256,192},{320,256},{384,320},{4... | collective-permute-start | bytes 1376264 | tf_op jit(solution)/shard_map/ppermute | solution.py:290
  8.5 0.7 pad_add_fusion.place
  9.2 5.7 %prepare.1 = (bf16[192,2944]{1,0:T(8,128)(2,1)}, bf16[192,2944]{1,0:T(8,128)(2,1)}, bf16[192,2944]{1,0:T(8,128)(2,1)}, f32[16,20,192]{2,1,0:T(8,128)}) custom-call(s32[3]{0:T(128)} %pad_add_fusion.place, bf16[192,8192]{1,0:T(8,128)(2,1)} %grad.5, bf16[192,896]{1,0:T(8,128)(2,1)} %gate_own.1, bf16[192,896]{1,0:T(8,128)(2,1)} %up.1, bf16[192,512]{1,0:T(8,128)(2,1)} %inp.1, ...), custom_call_target="tpu_custom_call" | custom-call | flops 80000000 | bytes 8000000 | tf_op jit(solution)/shard_map/prepare/pallas_call | solution.py:94
  14.9 3.2 %collective-permute-start.6 = (bf16[192,2944]{1,0:T(8,128)(2,1)}, bf16[192,2944]{1,0:T(8,128)(2,1)}, u32[]{:S(2)}, u32[]{:S(2)}) collective-permute-start(bf16[192,2944]{1,0:T(8,128)(2,1)} %get-tuple-element.23), channel_id=1, source_target_pairs={{0,16},{16,32},{32,48},{48,0},{1,17},{17,33},{33,49},{49,1},{2,18}... | collective-permute-start | bytes 3391496 | tf_op jit(solution)/shard_map/ppermute | solution.py:295
  18.1 3.3 %collective-permute-start.7 = (bf16[192,2944]{1,0:T(8,128)(2,1)}, bf16[192,2944]{1,0:T(8,128)(2,1)}, u32[]{:S(2)}, u32[]{:S(2)}) collective-permute-start(bf16[192,2944]{1,0:T(8,128)(2,1)} %get-tuple-element.24), channel_id=1, source_target_pairs={{0,48},{16,0},{32,16},{48,32},{1,49},{17,1},{33,17},{49,33},{2,50}... | collective-permute-start | bytes 3391496 | tf_op jit(solution)/shard_map/ppermute | solution.py:295
  21.4 0.0 collective-permute-done.w1
  21.4 0.0 collective-permute-done.1.w7
  21.4 1.9 %collective-permute-start.2 = (bf16[896,256]{1,0:T(8,128)(2,1)}, bf16[896,256]{1,0:T(8,128)(2,1)}, u32[]{:S(2)}, u32[]{:S(2)}) collective-permute-start(bf16[896,256]{1,0:T(8,128)(2,1)} %collective-permute-done.w1), channel_id=1, source_target_pairs={{0,64},{64,128},{128,192},{192,256},{256,320},{320,384},{384,448},... | collective-permute-start | bytes 1376264 | tf_op jit(solution)/shard_map/ppermute | solution.py:296
  23.4 4.6 %collective-permute-start.4 = (bf16[896,256]{1,0:T(8,128)(2,1)}, bf16[896,256]{1,0:T(8,128)(2,1)}, u32[]{:S(2)}, u32[]{:S(2)}) collective-permute-start(bf16[896,256]{1,0:T(8,128)(2,1)} %collective-permute-done.1.w7), channel_id=1, source_target_pairs={{0,448},{64,0},{128,64},{192,128},{256,192},{320,256},{384,320},{4... | collective-permute-start | bytes 1376264 | tf_op jit(solution)/shard_map/ppermute | solution.py:297
  27.9 3.5 %collective-permute-start.8 = (bf16[192,2944]{1,0:T(8,128)(2,1)}, bf16[192,2944]{1,0:T(8,128)(2,1)}, u32[]{:S(2)}, u32[]{:S(2)}) collective-permute-start(bf16[192,2944]{1,0:T(8,128)(2,1)} %get-tuple-element.26), channel_id=1, source_target_pairs={{0,32},{16,48},{32,0},{48,16},{1,33},{17,49},{33,1},{49,17},{2,34}... | collective-permute-start | bytes 3391496 | tf_op jit(solution)/shard_map/ppermute | solution.py:295
  31.4 12.7 %all-to-all-start = ((f32[16,20,192]{2,1,0:T(8,128)}), f32[16,20,192]{2,1,0:T(8,128)}, u32[]{:S(2)}, u32[]{:S(2)}) async-start(f32[16,20,192]{2,1,0:T(8,128)} %get-tuple-element.21), calls=%async_computation | async-start | bytes 786432 | tf_op jit(solution)/shard_map/all_to_all | solution.py:298
  44.1 0.0 collective-permute-done.2.w2
  44.1 1.9 %collective-permute-start.3 = (bf16[896,256]{1,0:T(8,128)(2,1)}, bf16[896,256]{1,0:T(8,128)(2,1)}, u32[]{:S(2)}, u32[]{:S(2)}) collective-permute-start(bf16[896,256]{1,0:T(8,128)(2,1)} %collective-permute-done.2.w2), channel_id=1, source_target_pairs={{0,64},{64,128},{128,192},{192,256},{256,320},{320,384},{384,448},... | collective-permute-start | bytes 1376264 | tf_op jit(solution)/shard_map/ppermute | solution.py:300
  46.1 0.0 collective-permute-done.4.w6
  46.1 4.6 %collective-permute-start.5 = (bf16[896,256]{1,0:T(8,128)(2,1)}, bf16[896,256]{1,0:T(8,128)(2,1)}, u32[]{:S(2)}, u32[]{:S(2)}) collective-permute-start(bf16[896,256]{1,0:T(8,128)(2,1)} %collective-permute-done.4.w6), channel_id=1, source_target_pairs={{0,448},{64,0},{128,64},{192,128},{256,192},{320,256},{384,320},{4... | collective-permute-start | bytes 1376264 | tf_op jit(solution)/shard_map/ppermute | solution.py:301
  50.7 8.1 %all-to-all-done.got = f32[16,20,192]{2,1,0:T(8,128)} async-done(((f32[16,20,192]{2,1,0:T(8,128)}), f32[16,20,192]{2,1,0:T(8,128)}, u32[]{:S(2)}, u32[]{:S(2)}) %all-to-all-start) | async-done | bytes 245792 | tf_op jit(solution)/shard_map/all_to_all | solution.py:298
  58.8 1.7 %share.1 = (f32[16,16,192]{2,1,0:T(8,128)}, f32[4,192]{1,0:T(4,128)}) custom-call(f32[16,20,192]{2,1,0:T(8,128)} %all-to-all-done.got), custom_call_target="tpu_custom_call" | custom-call | tf_op jit(solution)/shard_map/share/pallas_call | solution.py:130
  60.5 4.1 %all-to-all-start.1 = ((f32[16,16,192]{2,1,0:T(8,128)}), f32[16,16,192]{2,1,0:T(8,128)}, u32[]{:S(2)}, u32[]{:S(2)}) async-start(f32[16,16,192]{2,1,0:T(8,128)} %get-tuple-element.27), calls=%async_computation.1 | async-start | bytes 524288 | tf_op jit(solution)/shard_map/all_to_all | solution.py:302
  64.6 0.0 collective-permute-done.6.x1
  64.7 0.0 collective-permute-done.3.w3
  64.7 0.0 collective-permute-done.5.w5
  64.7 0.0 copy-start.1
  64.7 2.1 %collective-permute-start.9 = (bf16[896,256]{1,0:T(8,128)(2,1)}, bf16[896,256]{1,0:T(8,128)(2,1)}, u32[]{:S(2)}, u32[]{:S(2)}) collective-permute-start(bf16[896,256]{1,0:T(8,128)(2,1)} %collective-permute-done.3.w3), channel_id=1, source_target_pairs={{0,64},{64,128},{128,192},{192,256},{256,320},{320,384},{384,448},... | collective-permute-start | bytes 1376264 | tf_op jit(solution)/shard_map/ppermute | solution.py:304
  66.7 2.3 %collective-permute-done.8.x2 = bf16[192,2944]{1,0:T(8,128)(2,1)} collective-permute-done((bf16[192,2944]{1,0:T(8,128)(2,1)}, bf16[192,2944]{1,0:T(8,128)(2,1)}, u32[]{:S(2)}, u32[]{:S(2)}) %collective-permute-start.8) | collective-permute-done | bytes 1130528 | tf_op jit(solution)/shard_map/ppermute | solution.py:295
  69.0 6.4 %all-to-all-done.1.sides = f32[16,16,192]{2,1,0:T(8,128)} async-done(((f32[16,16,192]{2,1,0:T(8,128)}), f32[16,16,192]{2,1,0:T(8,128)}, u32[]{:S(2)}, u32[]{:S(2)}) %all-to-all-start.1) | async-done | bytes 196640 | tf_op jit(solution)/shard_map/all_to_all | solution.py:302
  75.4 1.0 copy-done.3
  76.5 6.3 %near.1.acc = f32[4,192,896]{2,1,0:T(8,128)S(1)} custom-call(s32[3]{0:T(128)S(1)} %copy-done.4, bf16[192,8192]{1,0:T(8,128)(2,1)S(1)} %copy-done, bf16[192,2944]{1,0:T(8,128)(2,1)} %collective-permute-done.6.x1, bf16[192,2944]{1,0:T(8,128)(2,1)} %collective-permute-done.8.x2, bf16[192,2944]{1,0:T(8,128)(2,1)} %collective-permute-done.7.x3, ...), custom_call_target="tpu_custom_call" | custom-call | flops 2466250752 | bytes 9000000 | tf_op jit(solution)/shard_map/near/pallas_call | solution.py:178
  82.8 0.0 collective-permute-done.9.w4
  82.8 5.2 %far.1 = f32[4,16,4,192]{3,2,1,0:T(4,128)S(1)} custom-call(s32[3]{0:T(128)S(1)} %copy-done.4, f32[4,192,896]{2,1,0:T(8,128)S(1)} %near.1.acc, bf16[192,8192]{1,0:T(8,128)(2,1)S(1)} %copy-done, bf16[192,896]{1,0:T(8,128)(2,1)S(1)} %copy-done.1, bf16[192,2944]{1,0:T(8,128)(2,1)} %collective-permute-done.6.x1, bf16[192,2944]{1,0:T(8,128)(2,1)} %collective-permute-done.8.x2, ...), custom_call_target="tpu_custom_call" | custom-call | flops 528482304 | bytes 6000000 | tf_op jit(solution)/shard_map/far/pallas_call | solution.py:238
  88.0 26.2 %all_to_all.15.got = f32[64,4,192]{2,1,0:T(4,128)} all-to-all(f32[64,4,192]{2,1,0:T(4,128)S(1)} %bitcast.5), channel_id=1, replica_groups=mesh['y'=8,'x'=4,'z'=8,'core'=2] {'x','z','core'}, dimensions={0} | all-to-all | bytes 393216 | tf_op jit(solution)/shard_map/all_to_all | solution.py:308
  114.2 2.0 %finish.1 = (f32[2,512]{1,0:T(2,128)}, f32[2,512]{1,0:T(2,128)}) custom-call(f32[64,4,192]{2,1,0:T(4,128)} %all_to_all.15.got, f32[4,192]{1,0:T(4,128)} %get-tuple-element.32.hid_side, f32[16,16,192]{2,1,0:T(8,128)} %all-to-all-done.1.sides, s32[1,192]{1,0:T(1,128)} %ids.1), custom_call_target="tpu_custom_call" | custom-call | tf_op jit(solution)/shard_map/finish/pallas_call | solution.py:281
  (9 shorter events, 0.0 us)
Async XLA Ops:
  0.6 20.8 %collective-permute-start = (bf16[896,256]{1,0:T(8,128)(2,1)}, bf16[896,256]{1,0:T(8,128)(2,1)}, u32[]{:S(2)}, u32[]{:S(2)}) collective-permute-start(bf16[896,256]{1,0:T(8,128)(2,1)} %w0.1), channel_id=1, source_target_pairs={{0,64},{64,128},{128,192},{192,256},{256,320},{320,384},{384,448},... | collective-permute-start | bytes 1376264 | tf_op jit(solution)/shard_map/ppermute | solution.py:289
  4.7 16.7 %collective-permute-start.1 = (bf16[896,256]{1,0:T(8,128)(2,1)}, bf16[896,256]{1,0:T(8,128)(2,1)}, u32[]{:S(2)}, u32[]{:S(2)}) collective-permute-start(bf16[896,256]{1,0:T(8,128)(2,1)} %w0.1), channel_id=1, source_target_pairs={{0,448},{64,0},{128,64},{192,128},{256,192},{320,256},{384,320},{4... | collective-permute-start | bytes 1376264 | tf_op jit(solution)/shard_map/ppermute | solution.py:290
  9.2 66.3 %copy-start = (bf16[192,8192]{1,0:T(8,128)(2,1)S(1)}, bf16[192,8192]{1,0:T(8,128)(2,1)}, u32[]{:S(2)}) copy-start(bf16[192,8192]{1,0:T(8,128)(2,1)} %grad.5) | copy-start | bytes 9437188
  14.9 60.5 %copy-start.4 = (s32[3]{0:T(128)S(1)}, s32[3]{0:T(128)}, u32[]{:S(2)}) copy-start(s32[3]{0:T(128)} %pad_add_fusion.place) | copy-start | bytes 40
  14.9 49.7 %collective-permute-start.6 = (bf16[192,2944]{1,0:T(8,128)(2,1)}, bf16[192,2944]{1,0:T(8,128)(2,1)}, u32[]{:S(2)}, u32[]{:S(2)}) collective-permute-start(bf16[192,2944]{1,0:T(8,128)(2,1)} %get-tuple-element.23), channel_id=1, source_target_pairs={{0,16},{16,32},{32,48},{48,0},{1,17},{17,33},{33,49},{49,1},{2,18}... | collective-permute-start | bytes 3391496 | tf_op jit(solution)/shard_map/ppermute | solution.py:295
  18.1 46.5 %collective-permute-start.7 = (bf16[192,2944]{1,0:T(8,128)(2,1)}, bf16[192,2944]{1,0:T(8,128)(2,1)}, u32[]{:S(2)}, u32[]{:S(2)}) collective-permute-start(bf16[192,2944]{1,0:T(8,128)(2,1)} %get-tuple-element.24), channel_id=1, source_target_pairs={{0,48},{16,0},{32,16},{48,32},{1,49},{17,1},{33,17},{49,33},{2,50}... | collective-permute-start | bytes 3391496 | tf_op jit(solution)/shard_map/ppermute | solution.py:295
  21.4 22.7 %collective-permute-start.2 = (bf16[896,256]{1,0:T(8,128)(2,1)}, bf16[896,256]{1,0:T(8,128)(2,1)}, u32[]{:S(2)}, u32[]{:S(2)}) collective-permute-start(bf16[896,256]{1,0:T(8,128)(2,1)} %collective-permute-done.w1), channel_id=1, source_target_pairs={{0,64},{64,128},{128,192},{192,256},{256,320},{320,384},{384,448},... | collective-permute-start | bytes 1376264 | tf_op jit(solution)/shard_map/ppermute | solution.py:296
  23.4 22.7 %collective-permute-start.4 = (bf16[896,256]{1,0:T(8,128)(2,1)}, bf16[896,256]{1,0:T(8,128)(2,1)}, u32[]{:S(2)}, u32[]{:S(2)}) collective-permute-start(bf16[896,256]{1,0:T(8,128)(2,1)} %collective-permute-done.1.w7), channel_id=1, source_target_pairs={{0,448},{64,0},{128,64},{192,128},{256,192},{320,256},{384,320},{4... | collective-permute-start | bytes 1376264 | tf_op jit(solution)/shard_map/ppermute | solution.py:297
  27.9 41.1 %collective-permute-start.8 = (bf16[192,2944]{1,0:T(8,128)(2,1)}, bf16[192,2944]{1,0:T(8,128)(2,1)}, u32[]{:S(2)}, u32[]{:S(2)}) collective-permute-start(bf16[192,2944]{1,0:T(8,128)(2,1)} %get-tuple-element.26), channel_id=1, source_target_pairs={{0,32},{16,48},{32,0},{48,16},{1,33},{17,49},{33,1},{49,17},{2,34}... | collective-permute-start | bytes 3391496 | tf_op jit(solution)/shard_map/ppermute | solution.py:295
  31.4 27.4 %all-to-all-start = ((f32[16,20,192]{2,1,0:T(8,128)}), f32[16,20,192]{2,1,0:T(8,128)}, u32[]{:S(2)}, u32[]{:S(2)}) async-start(f32[16,20,192]{2,1,0:T(8,128)} %get-tuple-element.21), calls=%async_computation | async-start | bytes 786432 | tf_op jit(solution)/shard_map/all_to_all | solution.py:298
  44.1 20.5 %collective-permute-start.3 = (bf16[896,256]{1,0:T(8,128)(2,1)}, bf16[896,256]{1,0:T(8,128)(2,1)}, u32[]{:S(2)}, u32[]{:S(2)}) collective-permute-start(bf16[896,256]{1,0:T(8,128)(2,1)} %collective-permute-done.2.w2), channel_id=1, source_target_pairs={{0,64},{64,128},{128,192},{192,256},{256,320},{320,384},{384,448},... | collective-permute-start | bytes 1376264 | tf_op jit(solution)/shard_map/ppermute | solution.py:300
  46.1 18.6 %collective-permute-start.5 = (bf16[896,256]{1,0:T(8,128)(2,1)}, bf16[896,256]{1,0:T(8,128)(2,1)}, u32[]{:S(2)}, u32[]{:S(2)}) collective-permute-start(bf16[896,256]{1,0:T(8,128)(2,1)} %collective-permute-done.4.w6), channel_id=1, source_target_pairs={{0,448},{64,0},{128,64},{192,128},{256,192},{320,256},{384,320},{4... | collective-permute-start | bytes 1376264 | tf_op jit(solution)/shard_map/ppermute | solution.py:301
  60.5 14.9 %all-to-all-start.1 = ((f32[16,16,192]{2,1,0:T(8,128)}), f32[16,16,192]{2,1,0:T(8,128)}, u32[]{:S(2)}, u32[]{:S(2)}) async-start(f32[16,16,192]{2,1,0:T(8,128)} %get-tuple-element.27), calls=%async_computation.1 | async-start | bytes 524288 | tf_op jit(solution)/shard_map/all_to_all | solution.py:302
  64.7 18.1 %copy-start.1 = (bf16[192,896]{1,0:T(8,128)(2,1)S(1)}, bf16[192,896]{1,0:T(8,128)(2,1)}, u32[]{:S(2)}) copy-start(bf16[192,896]{1,0:T(8,128)(2,1)} %gate_own.1) | copy-start | bytes 1032196
  64.7 18.1 %collective-permute-start.9 = (bf16[896,256]{1,0:T(8,128)(2,1)}, bf16[896,256]{1,0:T(8,128)(2,1)}, u32[]{:S(2)}, u32[]{:S(2)}) collective-permute-start(bf16[896,256]{1,0:T(8,128)(2,1)} %collective-permute-done.3.w3), channel_id=1, source_target_pairs={{0,64},{64,128},{128,192},{192,256},{256,320},{320,384},{384,448},... | collective-permute-start | bytes 1376264 | tf_op jit(solution)/shard_map/ppermute | solution.py:304
  75.4 1.0 copy-start.3
  76.5 6.3 %copy-start.2 = (bf16[896,64]{0,1:T(8,128)(2,1)S(1)}, bf16[896,64]{0,1:T(8,128)(2,1)}, u32[]{:S(2)}) copy-start(bf16[896,64]{0,1:T(8,128)(2,1)} %param.13) | copy-start | bytes 344068

commit v4 on v1

v4 whole, which is shorter than its diff:
```python
import jax
import jax.numpy as jnp
from jax import lax
from jax.experimental import pallas as pl
from jax.experimental.pallas import tpu as pltpu
from jax.sharding import Mesh
from jax.sharding import PartitionSpec as P

NY, NX, NZ, NC = 8, 4, 8, 2
NB = NZ * NC
FAR = NY // 2
EXTRA = 16
CHUNK = 256
ZC = ("z", "core")
BF16, F32 = jnp.bfloat16, jnp.float32
HBM = pl.BlockSpec(memory_space=pltpu.HBM)
VMEM = pl.BlockSpec(memory_space=pltpu.VMEM)
WIDE = pltpu.CompilerParams(vmem_limit_bytes=60 << 20)


def turn(n, step):
    return [(i, (i + step) % n) for i in range(n)]


def dot_nt(a, b, **kw):
    return lax.dot_general(a, b, (((1,), (1,)), ((), ())), preferred_element_type=F32, **kw)


def silu(v):
    return v / (1.0 + jnp.exp(-v))


def columns(y, back, x, wide):
    return pl.multiple_of((lax.rem(y - back + NY, NY) * NX + x) * wide, wide)


def here():
    return lax.axis_index("y"), lax.axis_index("x"), lax.axis_index("z") * NC + lax.axis_index("core")


def prepare_kernel(grad, gate, up, inp, model, hproj, p1, p2, p3, early, buf, gate_v, up_v, inp_v, gcols, model_v, hproj_v, in_sem, out_sem, side_sem):
    outs = (p1, p2, p3)
    tok, hid = gate.shape
    wide = (p1.shape[1] - hid) // NY
    feat = inp.shape[1]
    y, x, blk = here()
    fills, sends = [], []
    for s, out in enumerate(outs):
        at = lax.rem(x + s + 1, NX)
        fill = [pltpu.make_async_copy(gate, buf.at[s, :, pl.ds(0, hid)], in_sem.at[s, NY])]
        for i in range(NY):
            fill.append(
                pltpu.make_async_copy(
                    grad.at[:, pl.ds(columns(y, i, at, wide), wide)],
                    buf.at[s, :, pl.ds(hid + i * wide, wide)],
                    in_sem.at[s, i],
                )
            )
        fills.append(fill)
        sends.append(pltpu.make_async_copy(buf.at[s], out, out_sem.at[s]))
        for c in fill:
            c.start()
    loads = [
        pltpu.make_async_copy(gate, gate_v, side_sem.at[0]),
        pltpu.make_async_copy(up, up_v, side_sem.at[1]),
        pltpu.make_async_copy(inp, inp_v, side_sem.at[2]),
        pltpu.make_async_copy(grad.at[:, pl.ds(pl.multiple_of(blk * feat, feat), feat)], gcols, side_sem.at[3]),
        pltpu.make_async_copy(model, model_v, side_sem.at[4]),
        pltpu.make_async_copy(hproj, hproj_v, side_sem.at[5]),
    ]
    for c in loads:
        c.start()
    for fill, send in zip(fills, sends):
        for c in fill:
            c.wait()
        send.start()
    for c in loads:
        c.wait()
    hidden = (silu(gate_v[...].astype(F32)) * up_v[...].astype(F32)).astype(BF16)
    hid_side = dot_nt(hproj_v[...], hidden)
    high = hid_side.astype(BF16).astype(F32)
    low = hid_side - high
    m = model_v[...]
    side = jnp.concatenate(
        [jnp.dot(v[...], m, preferred_element_type=F32) for v in (gcols, inp_v)], axis=1
    ).astype(BF16)
    width = side.shape[1]
    per = hproj.shape[0] // NB
    for b in range(NB):
        early[b, 0:tok, :] = side
        rows = jnp.concatenate(
            [high[b * per : (b + 1) * per], low[b * per : (b + 1) * per], jnp.zeros((EXTRA - 2 * per, tok), F32)], axis=0
        )
        early[b, tok : tok + EXTRA, :] = jnp.concatenate(
            [rows, jnp.zeros((EXTRA, width - tok), F32)], axis=1
        ).astype(BF16)
    for c in sends:
        c.wait()


def prepare(grad, gate, up, inp, model, hproj, wide):
    tok, hid = gate.shape
    feat = inp.shape[1]
    out = jax.ShapeDtypeStruct((tok, hid + NY * wide), BF16)
    return pl.pallas_call(
        prepare_kernel,
        out_shape=[out] * 3 + [jax.ShapeDtypeStruct((NB, tok + EXTRA, 2 * model.shape[1]), BF16)],
        in_specs=[HBM] * 6,
        out_specs=[HBM] * 3 + [VMEM],
        scratch_shapes=[
            pltpu.VMEM((NX - 1, tok, hid + NY * wide), BF16),
            pltpu.VMEM((tok, hid), BF16),
            pltpu.VMEM((tok, hid), BF16),
            pltpu.VMEM((tok, feat), BF16),
            pltpu.VMEM((tok, feat), BF16),
            pltpu.VMEM(model.shape, BF16),
            pltpu.VMEM(hproj.shape, BF16),
            pltpu.SemaphoreType.DMA((NX - 1, NY + 1)),
            pltpu.SemaphoreType.DMA((NX - 1,)),
            pltpu.SemaphoreType.DMA((6,)),
        ],
        compiler_params=WIDE,
        cost_estimate=pl.CostEstimate(flops=80_000_000, bytes_accessed=8_000_000, transcendentals=tok * hid),
        name="prepare",
    )(grad, gate, up, inp, model, hproj)


def main_kernel(grad, own, x1, x2, x3, w0, w1, w2, w3, w4, w5, w6, w7, proj, out, g, gate, w, p, g_sem, w_sem):
    y, x, _ = here()
    nx, tok, hid = gate.shape
    wide = w0.shape[1]
    per = proj.shape[0] // NB
    chunks = [(c, min(CHUNK, hid - c)) for c in range(0, hid, CHUNK)]
    firsts = []
    for i in range(NY):
        firsts.append(
            pltpu.make_async_copy(
                grad.at[:, pl.ds(columns(y, i, x, wide), wide)], g.at[0, :, pl.ds(i * wide, wide)], g_sem.at[0, i]
            )
        )
    for s, got in enumerate((x1, x2, x3)):
        firsts.append(pltpu.make_async_copy(got.at[:, pl.ds(hid, NY * wide)], g.at[s + 1], g_sem.at[s + 1, 0]))
    loads = []
    for k, (c, n) in enumerate(chunks):
        loads.append(
            [
                pltpu.make_async_copy(src.at[pl.ds(c, n)], w.at[pl.ds(c, n), pl.ds(i * wide, wide)], w_sem.at[k, i])
                for i, src in enumerate((w0, w1, w2, w3, w4, w5, w6, w7))
            ]
        )
    seconds = [pltpu.make_async_copy(own, gate.at[0], g_sem.at[0, NY]), pltpu.make_async_copy(proj, p, g_sem.at[1, NY])]
    for s, got in enumerate((x1, x2, x3)):
        seconds.append(pltpu.make_async_copy(got.at[:, pl.ds(0, hid)], gate.at[s + 1], g_sem.at[s + 1, 1]))
    for c in loads[0] + firsts + loads[1] + seconds:
        c.start()
    for load in loads[2:]:
        for c in load:
            c.start()
    for c in firsts:
        c.wait()
    grads = g[...].reshape(nx * tok, NY * wide)
    total = [None] * nx
    for k, (c, n) in enumerate(chunks):
        for cp in loads[k]:
            cp.wait()
        gh = dot_nt(grads, w[c : c + n, :])
        if k == 0:
            for cp in seconds:
                cp.wait()
        gu = gh * silu(gate[:, :, c : c + n].reshape(nx * tok, n).astype(F32))
        hi = gu.astype(BF16)
        lo = (gu - hi.astype(F32)).astype(BF16)
        ps = p[:, c : c + n]
        for s in range(nx):
            rows = slice(s * tok, (s + 1) * tok)
            part = dot_nt(ps, hi[rows]) + dot_nt(ps, lo[rows])
            total[s] = part if k == 0 else total[s] + part
    for s in range(nx):
        to = lax.rem(x - s + nx, nx)
        for b in range(NB):
            out[to, b] = total[s][b * per : (b + 1) * per, :]


def main(grad, own, got, shards, proj):
    tok = grad.shape[0]
    hid, wide = shards[0].shape
    per = proj.shape[0] // NB
    n_chunk = -(-hid // CHUNK)
    return pl.pallas_call(
        main_kernel,
        out_shape=jax.ShapeDtypeStruct((NX, NB, per, tok), F32),
        in_specs=[HBM] * 14,
        out_specs=VMEM,
        scratch_shapes=[
            pltpu.VMEM((NX, tok, NY * wide), BF16),
            pltpu.VMEM((NX, tok, hid), BF16),
            pltpu.VMEM((hid, NY * wide), BF16),
            pltpu.VMEM(proj.shape, BF16),
            pltpu.SemaphoreType.DMA((NX, NY + 1)),
            pltpu.SemaphoreType.DMA((n_chunk, NY)),
        ],
        compiler_params=pltpu.CompilerParams(vmem_limit_bytes=32 << 20),
        cost_estimate=pl.CostEstimate(
            flops=16 * NX * tok * hid * (NY * wide + 128), bytes_accessed=9_000_000, transcendentals=NX * tok * hid
        ),
        name="main",
    )(grad, own, *got, *shards, proj)


def score(left, right, which, out):
    picked = jnp.concatenate([jnp.where(which == e, left, 0.0) for e in range(2)], axis=0)
    res = jnp.dot(picked, right, precision=lax.Precision.HIGHEST, preferred_element_type=F32)
    per, width = left.shape[0], right.shape[1]
    for e in range(2):
        for k in range(per):
            out[e : e + 1, k * width : (k + 1) * width] = res[e * per + k : e * per + k + 1, :]


def settle_kernel(got, ids, down, side):
    tok = ids.shape[1]
    total = got[0].astype(F32)
    for b in range(1, NB):
        total = total + got[b].astype(F32)
    width = side.shape[1]
    per = down.shape[1] // width
    hid_side = total[tok : tok + per, 0:tok] + total[tok + per : tok + 2 * per, 0:tok]
    score(hid_side, total[0:tok, 0:width], ids[...], down)
    side[...] = total[0:tok, width:]


def settle(got, ids, per):
    tok, width = ids.shape[1], got.shape[2] // 2
    return pl.pallas_call(
        settle_kernel,
        out_shape=[jax.ShapeDtypeStruct((2, per * width), F32), jax.ShapeDtypeStruct((tok, width), F32)],
        in_specs=[VMEM, VMEM],
        out_specs=[VMEM, VMEM],
        name="settle",
    )(got, ids)


def finish_kernel(got, side, ids, up):
    parts = [got[b] for b in range(got.shape[0])]
    while len(parts) > 1:
        parts = [parts[i] + parts[i + 1] for i in range(0, len(parts), 2)]
    score(parts[0], side[...], ids[...], up)


def finish(got, side, ids):
    return pl.pallas_call(
        finish_kernel,
        out_shape=jax.ShapeDtypeStruct((2, got.shape[1] * side.shape[1]), F32),
        in_specs=[VMEM] * 3,
        out_specs=VMEM,
        name="finish",
    )(got, side, ids)


def on_device(out_grad, layer_input, gate_pre, up_pre, down_weight, proj_hidden, proj_model, example_ids):
    hproj = proj_hidden.T
    up1 = lax.ppermute(down_weight, "y", turn(NY, 1))
    dn1 = lax.ppermute(down_weight, "y", turn(NY, -1))
    p1, p2, p3, early = prepare(out_grad, gate_pre, up_pre, layer_input, proj_model, hproj, down_weight.shape[1])
    up1, dn1, early = lax.optimization_barrier((up1, dn1, early))
    x1, x2, x3 = [lax.ppermute(p, "x", turn(NX, s + 1)) for s, p in enumerate((p1, p2, p3))]
    up2 = lax.ppermute(up1, "y", turn(NY, 1))
    dn2 = lax.ppermute(dn1, "y", turn(NY, -1))
    got = lax.all_to_all(early, ZC, 0, 0)
    up3 = lax.ppermute(up2, "y", turn(NY, 1))
    dn3 = lax.ppermute(dn2, "y", turn(NY, -1))
    up3, dn3, x1, x3 = lax.optimization_barrier((up3, dn3, x1, x3))
    w4 = lax.ppermute(up3, "y", turn(NY, 1))
    x2, w4 = lax.optimization_barrier((x2, w4))
    up_part = main(out_grad, gate_pre, (x1, x2, x3), (down_weight, up1, up2, up3, w4, dn3, dn2, dn1), hproj)
    up_part, got = lax.optimization_barrier((up_part, got))
    up_side = lax.all_to_all(up_part.reshape((NX * NB,) + up_part.shape[2:]), ("x",) + ZC, 0, 0)
    down_scores, side = settle(got, example_ids, up_part.shape[2])
    return down_scores, finish(up_side, side, example_ids)


def solution(mesh):
    fine = Mesh(mesh.devices.reshape(NY, NX, NZ, NC), ("y", "x", "z", "core"))
    yx = ("y", "x")
    in_specs = (P(yx, None), P(yx, ZC), P(yx, ZC), P(yx, ZC), P(ZC, yx), P(ZC, None), P(ZC, None), P(yx, None))
    out_specs = (P(yx, ZC), P(yx, ZC))
    return jax.shard_map(on_device, mesh=fine, in_specs=in_specs, out_specs=out_specs, check_vma=False)
```

time: 157 us -> 124 us (0.79)
  local copies, waits for them, and re-layouts: 37 us -> 3.31 us
  Pallas kernels: 0 us -> 20.2 us
  starting transfers between devices: 79.3 us -> 68.1 us
  matrix products: 9.39 us -> 0 us
  waiting for transfers between devices: 25.1 us -> 30.9 us
  other arithmetic: 3.09 us -> 0 us
    pallas_call x0 -> x4, Pallas kernels: none -> 20.2 us  [the longest x1 10.6 us: main(): pl.pallas_call(main_kernel, out_shape=jax.ShapeDtypeStruct((NX, NB, per,...]
    unnamed x35 -> x12, local copies, waits for them, and re-layouts: 23 us -> 3.31 us
    ppermute x9 -> x4, starting transfers between devices: 26 us -> 13.8 us  [the longest x3 10.1 us: on_device(): lax.ppermute(p, 'x', turn(NX, s + 1))]
    dot_general x6 -> x0, matrix products: 9.39 us -> none  [the longest x3 6.73 us: dot_nt(): lax.dot_general(a, b, (((1,), (1,)), ((), ())), preferred_element_type=F3...]
    ppermute x1, waiting for transfers between devices: 0.01 us -> 8.85 us  [on_device(): up3 = lax.ppermute(up2, 'y', turn(NY, 1))]
    ppermute x9 -> x4, waiting for transfers between devices: 17.3 us -> 10.7 us  [the longest x1 6.79 us: on_device(): w4 = lax.ppermute(up3, 'y', turn(NY, 1))]
    concatenate x4 -> x0, local copies, waits for them, and re-layouts: 5.29 us -> none  [the longest x1 1.85 us: on_device(): jnp.concatenate([down_weight, up1, up2, up3, jnp.concatenate([far_a, far_...]
    slice x11 -> x0, local copies, waits for them, and re-layouts: 3.87 us -> none  [the longest x5 1.85 us: on_device(): gates = [gate_pre] + [g[:, :hid] for g in got]]
  transfers between devices with their start and end apart: 18 -> 12, of which waited for: 4 -> 5; matrix products, arithmetic and copies ran while one was open for 30% -> 0% of each run, Pallas kernels for 0% -> 15%
where the time goes in v4:
time: 124 us; the launch traced here: 123 us
  starting transfers between devices  68.1 us (55%)
  waiting for transfers between devices  30.9 us (25%)
  Pallas kernels  20.2 us (16%)
  local copies, waits for them, and re-layouts  3.31 us (3%)
    all_to_all x1, starting transfers between devices, on_device(): lax.all_to_all(up_part.reshape((NX * NB,) + up_part.shape[2:]), ('x',) +...  20.8 us
    all_to_all x1, starting transfers between devices, on_device(): got = lax.all_to_all(early, ZC, 0, 0)  12.7 us
    pallas_call x1, Pallas kernels, main(): pl.pallas_call(main_kernel, out_shape=jax.ShapeDtypeStruct((NX, NB, per,...  10.6 us
    ppermute x3, starting transfers between devices, on_device(): lax.ppermute(p, 'x', turn(NX, s + 1))  10.1 us
    all_to_all x1, waiting for transfers between devices, on_device(): lax.all_to_all(up_part.reshape((NX * NB,) + up_part.shape[2:]), ('x',) +...  9.54 us
    ppermute x1, waiting for transfers between devices, on_device(): up3 = lax.ppermute(up2, 'y', turn(NY, 1))  8.85 us
    ppermute x1, waiting for transfers between devices, on_device(): w4 = lax.ppermute(up3, 'y', turn(NY, 1))  6.79 us
    pallas_call x1, Pallas kernels, prepare(): pl.pallas_call(prepare_kernel, out_shape=[out] * 3 + [jax.ShapeDtypeStruc...  5.39 us
  transfers between devices with their start and end apart: 12, of which 5 were waited for; matrix products, arithmetic and copies ran while one was open for 0% of the time, Pallas kernels for 15%

profile of v4, /device:TPU:1, one launch (start us, length us, event | category | flops | bytes accessed | tf_op | source)
XLA Modules:
  0.0 123.4 jit_solution(17618878651833369004)
XLA Ops:
  0.6 4.0 %collective-permute-start = (bf16[896,256]{1,0:T(8,128)(2,1)}, bf16[896,256]{1,0:T(8,128)(2,1)}, u32[]{:S(2)}, u32[]{:S(2)}) collective-permute-start(bf16[896,256]{1,0:T(8,128)(2,1)} %w0.1), channel_id=1, source_target_pairs={{0,64},{64,128},{128,192},{192,256},{256,320},{320,384},{384,448},... | collective-permute-start | bytes 1376264 | tf_op jit(solution)/shard_map/ppermute | solution.py:261
  4.7 3.8 %collective-permute-start.1 = (bf16[896,256]{1,0:T(8,128)(2,1)}, bf16[896,256]{1,0:T(8,128)(2,1)}, u32[]{:S(2)}, u32[]{:S(2)}) collective-permute-start(bf16[896,256]{1,0:T(8,128)(2,1)} %w0.1), channel_id=1, source_target_pairs={{0,448},{64,0},{128,64},{192,128},{256,192},{320,256},{384,320},{4... | collective-permute-start | bytes 1376264 | tf_op jit(solution)/shard_map/ppermute | solution.py:262
  8.5 5.4 %prepare.1 = (bf16[192,2944]{1,0:T(8,128)(2,1)}, bf16[192,2944]{1,0:T(8,128)(2,1)}, bf16[192,2944]{1,0:T(8,128)(2,1)}, bf16[16,208,256]{2,1,0:T(8,128)(2,1)}) custom-call(bf16[192,8192]{1,0:T(8,128)(2,1)} %grad.3, bf16[192,896]{1,0:T(8,128)(2,1)} %own.1, bf16[192,896]{1,0:T(8,128)(2,1)} %up.1, bf16[192,512]{1,0:T(8,128)(2,1)} %inp.1, ...), custom_call_target="tpu_custom_call" | custom-call | flops 80000000 | bytes 8000000 | tf_op jit(solution)/shard_map/prepare/pallas_call | solution.py:105
  13.9 3.1 %collective-permute-start.6 = (bf16[192,2944]{1,0:T(8,128)(2,1)}, bf16[192,2944]{1,0:T(8,128)(2,1)}, u32[]{:S(2)}, u32[]{:S(2)}) collective-permute-start(bf16[192,2944]{1,0:T(8,128)(2,1)} %get-tuple-element.22), channel_id=1, source_target_pairs={{0,16},{16,32},{32,48},{48,0},{1,17},{17,33},{33,49},{49,1},{2,18}... | collective-permute-start | bytes 3391496 | tf_op jit(solution)/shard_map/ppermute | solution.py:265
  17.0 3.4 %collective-permute-start.7 = (bf16[192,2944]{1,0:T(8,128)(2,1)}, bf16[192,2944]{1,0:T(8,128)(2,1)}, u32[]{:S(2)}, u32[]{:S(2)}) collective-permute-start(bf16[192,2944]{1,0:T(8,128)(2,1)} %get-tuple-element.23), channel_id=1, source_target_pairs={{0,48},{16,0},{32,16},{48,32},{1,49},{17,1},{33,17},{49,33},{2,50}... | collective-permute-start | bytes 3391496 | tf_op jit(solution)/shard_map/ppermute | solution.py:265
  20.4 0.0 collective-permute-done.w1
  20.4 0.0 collective-permute-done.1.w7
  20.4 1.9 %collective-permute-start.2 = (bf16[896,256]{1,0:T(8,128)(2,1)}, bf16[896,256]{1,0:T(8,128)(2,1)}, u32[]{:S(2)}, u32[]{:S(2)}) collective-permute-start(bf16[896,256]{1,0:T(8,128)(2,1)} %collective-permute-done.w1), channel_id=1, source_target_pairs={{0,64},{64,128},{128,192},{192,256},{256,320},{320,384},{384,448},... | collective-permute-start | bytes 1376264 | tf_op jit(solution)/shard_map/ppermute | solution.py:266
  22.4 4.6 %collective-permute-start.4 = (bf16[896,256]{1,0:T(8,128)(2,1)}, bf16[896,256]{1,0:T(8,128)(2,1)}, u32[]{:S(2)}, u32[]{:S(2)}) collective-permute-start(bf16[896,256]{1,0:T(8,128)(2,1)} %collective-permute-done.1.w7), channel_id=1, source_target_pairs={{0,448},{64,0},{128,64},{192,128},{256,192},{320,256},{384,320},{4... | collective-permute-start | bytes 1376264 | tf_op jit(solution)/shard_map/ppermute | solution.py:267
  27.0 0.0 copy-start
  27.0 3.7 %collective-permute-start.8 = (bf16[192,2944]{1,0:T(8,128)(2,1)}, bf16[192,2944]{1,0:T(8,128)(2,1)}, u32[]{:S(2)}, u32[]{:S(2)}) collective-permute-start(bf16[192,2944]{1,0:T(8,128)(2,1)} %get-tuple-element.25), channel_id=1, source_target_pairs={{0,32},{16,48},{32,0},{48,16},{1,33},{17,49},{33,1},{49,17},{2,34}... | collective-permute-start | bytes 3391496 | tf_op jit(solution)/shard_map/ppermute | solution.py:265
  30.6 12.7 %all-to-all-start = ((bf16[16,208,256]{2,1,0:T(8,128)(2,1)}), bf16[16,208,256]{2,1,0:T(8,128)(2,1)}, u32[]{:S(2)}, u32[]{:S(2)}) async-start(bf16[16,208,256]{2,1,0:T(8,128)(2,1)} %get-tuple-element.31), calls=%async_computation | async-start | bytes 3407872 | tf_op jit(solution)/shard_map/all_to_all | solution.py:268
  43.3 0.0 collective-permute-done.2.w2
  43.3 1.9 %collective-permute-start.3 = (bf16[896,256]{1,0:T(8,128)(2,1)}, bf16[896,256]{1,0:T(8,128)(2,1)S(1)}, u32[]{:S(2)}, u32[]{:S(2)}) collective-permute-start(bf16[896,256]{1,0:T(8,128)(2,1)} %collective-permute-done.2.w2), channel_id=1, source_target_pairs={{0,64},{64,128},{128,192},{192,256},{256,320},{320,384},{384,448},... | collective-permute-start | bytes 1376264 | tf_op jit(solution)/shard_map/ppermute | solution.py:269
  45.3 0.0 collective-permute-done.4.w6
  45.3 4.6 %collective-permute-start.5 = (bf16[896,256]{1,0:T(8,128)(2,1)}, bf16[896,256]{1,0:T(8,128)(2,1)S(1)}, u32[]{:S(2)}, u32[]{:S(2)}) collective-permute-start(bf16[896,256]{1,0:T(8,128)(2,1)} %collective-permute-done.4.w6), channel_id=1, source_target_pairs={{0,448},{64,0},{128,64},{192,128},{256,192},{320,256},{384,320},{4... | collective-permute-start | bytes 1376264 | tf_op jit(solution)/shard_map/ppermute | solution.py:270
  49.9 0.0 collective-permute-done.6.x1
  49.9 8.8 %collective-permute-done.3.w3 = bf16[896,256]{1,0:T(8,128)(2,1)S(1)} collective-permute-done((bf16[896,256]{1,0:T(8,128)(2,1)}, bf16[896,256]{1,0:T(8,128)(2,1)S(1)}, u32[]{:S(2)}, u32[]{:S(2)}) %collective-permute-start.3) | collective-permute-done | bytes 458784 | tf_op jit(solution)/shard_map/ppermute | solution.py:269
  58.7 1.8 %collective-permute-done.5.w5 = bf16[896,256]{1,0:T(8,128)(2,1)S(1)} collective-permute-done((bf16[896,256]{1,0:T(8,128)(2,1)}, bf16[896,256]{1,0:T(8,128)(2,1)S(1)}, u32[]{:S(2)}, u32[]{:S(2)}) %collective-permute-start.5) | collective-permute-done | bytes 458784 | tf_op jit(solution)/shard_map/ppermute | solution.py:270
  60.5 3.6 %collective-permute-start.9 = (bf16[896,256]{1,0:T(8,128)(2,1)S(1)}, bf16[896,256]{1,0:T(8,128)(2,1)S(1)}, u32[]{:S(2)}, u32[]{:S(2)}) collective-permute-start(bf16[896,256]{1,0:T(8,128)(2,1)S(1)} %collective-permute-done.3.w3), channel_id=1, source_target_pairs={{0,64},{64,128},{128,192},{192,256},{256,320},{320,384},{384,448},... | collective-permute-start | bytes 1376264 | tf_op jit(solution)/shard_map/ppermute | solution.py:272
  64.1 3.9 %collective-permute-done.8.x2 = bf16[192,2944]{1,0:T(8,128)(2,1)} collective-permute-done((bf16[192,2944]{1,0:T(8,128)(2,1)}, bf16[192,2944]{1,0:T(8,128)(2,1)}, u32[]{:S(2)}, u32[]{:S(2)}) %collective-permute-start.8) | collective-permute-done | bytes 1130528 | tf_op jit(solution)/shard_map/ppermute | solution.py:265
  68.1 6.8 %collective-permute-done.9.w4 = bf16[896,256]{1,0:T(8,128)(2,1)S(1)} collective-permute-done((bf16[896,256]{1,0:T(8,128)(2,1)S(1)}, bf16[896,256]{1,0:T(8,128)(2,1)S(1)}, u32[]{:S(2)}, u32[]{:S(2)}) %collective-permute-start.9) | collective-permute-done | bytes 458784 | tf_op jit(solution)/shard_map/ppermute | solution.py:272
  74.9 0.9 copy-done.3
  75.8 1.0 copy-done.4
  76.8 10.6 %main.1 = f32[4,16,4,192]{3,2,1,0:T(4,128)S(1)} custom-call(bf16[192,8192]{1,0:T(8,128)(2,1)S(1)} %copy-done, bf16[192,896]{1,0:T(8,128)(2,1)S(1)} %copy-done.1, bf16[192,2944]{1,0:T(8,128)(2,1)} %collective-permute-done.6.x1, bf16[192,2944]{1,0:T(8,128)(2,1)} %collective-permute-done.8.x2, bf16[192,2944]{1,0:T(8,128)(2,1)} %collective-permute-done.7.x3, ...), custom_call_target="tpu_custom_call" | custom-call | flops 23957864448 | bytes 9000000 | tf_op jit(solution)/shard_map/main/pallas_call | solution.py:189
  87.4 0.7 copy-done.2
  88.1 0.0 all-to-all-done.got
  88.1 20.8 %all-to-all-start.1 = ((f32[64,4,192]{2,1,0:T(4,128)}), f32[64,4,192]{2,1,0:T(4,128)S(1)}, u32[]{:S(2)}, u32[]{:S(2)}) async-start(f32[64,4,192]{2,1,0:T(4,128)} %bitcast.2), calls=%async_computation.1 | async-start | bytes 524288 | tf_op jit(solution)/shard_map/all_to_all | solution.py:276
  108.9 2.5 %settle.1 = (f32[2,512]{1,0:T(2,128)}, f32[192,128]{1,0:T(8,128)}) custom-call(bf16[16,208,256]{2,1,0:T(8,128)(2,1)} %all-to-all-done.got, s32[1,192]{1,0:T(1,128)} %ids.3), custom_call_target="tpu_custom_call" | custom-call | tf_op jit(solution)/shard_map/settle/pallas_call | solution.py:233
  111.3 9.5 %all-to-all-done.1.got = f32[64,4,192]{2,1,0:T(4,128)S(1)} async-done(((f32[64,4,192]{2,1,0:T(4,128)}), f32[64,4,192]{2,1,0:T(4,128)S(1)}, u32[]{:S(2)}, u32[]{:S(2)}) %all-to-all-start.1) | async-done | bytes 196640 | tf_op jit(solution)/shard_map/all_to_all | solution.py:276
  120.9 0.7 copy-done.5
  121.6 1.8 %finish.1 = f32[2,512]{1,0:T(2,128)} custom-call(f32[64,4,192]{2,1,0:T(4,128)} %copy-done.5, f32[192,128]{1,0:T(8,128)} %get-tuple-element.35.side, s32[1,192]{1,0:T(1,128)} %ids.3), custom_call_target="tpu_custom_call" | custom-call | tf_op jit(solution)/shard_map/finish/pallas_call | solution.py:250
  (8 shorter events, 0.0 us)
Async XLA Ops:
  0.6 19.8 %collective-permute-start = (bf16[896,256]{1,0:T(8,128)(2,1)}, bf16[896,256]{1,0:T(8,128)(2,1)}, u32[]{:S(2)}, u32[]{:S(2)}) collective-permute-start(bf16[896,256]{1,0:T(8,128)(2,1)} %w0.1), channel_id=1, source_target_pairs={{0,64},{64,128},{128,192},{192,256},{256,320},{320,384},{384,448},... | collective-permute-start | bytes 1376264 | tf_op jit(solution)/shard_map/ppermute | solution.py:261
  4.7 15.8 %collective-permute-start.1 = (bf16[896,256]{1,0:T(8,128)(2,1)}, bf16[896,256]{1,0:T(8,128)(2,1)}, u32[]{:S(2)}, u32[]{:S(2)}) collective-permute-start(bf16[896,256]{1,0:T(8,128)(2,1)} %w0.1), channel_id=1, source_target_pairs={{0,448},{64,0},{128,64},{192,128},{256,192},{320,256},{384,320},{4... | collective-permute-start | bytes 1376264 | tf_op jit(solution)/shard_map/ppermute | solution.py:262
  8.5 66.3 %copy-start.1 = (bf16[192,896]{1,0:T(8,128)(2,1)S(1)}, bf16[192,896]{1,0:T(8,128)(2,1)}, u32[]{:S(2)}) copy-start(bf16[192,896]{1,0:T(8,128)(2,1)} %own.1) | copy-start | bytes 1032196
  13.9 35.9 %collective-permute-start.6 = (bf16[192,2944]{1,0:T(8,128)(2,1)}, bf16[192,2944]{1,0:T(8,128)(2,1)}, u32[]{:S(2)}, u32[]{:S(2)}) collective-permute-start(bf16[192,2944]{1,0:T(8,128)(2,1)} %get-tuple-element.22), channel_id=1, source_target_pairs={{0,16},{16,32},{32,48},{48,0},{1,17},{17,33},{33,49},{49,1},{2,18}... | collective-permute-start | bytes 3391496 | tf_op jit(solution)/shard_map/ppermute | solution.py:265
  17.0 32.8 %collective-permute-start.7 = (bf16[192,2944]{1,0:T(8,128)(2,1)}, bf16[192,2944]{1,0:T(8,128)(2,1)}, u32[]{:S(2)}, u32[]{:S(2)}) collective-permute-start(bf16[192,2944]{1,0:T(8,128)(2,1)} %get-tuple-element.23), channel_id=1, source_target_pairs={{0,48},{16,0},{32,16},{48,32},{1,49},{17,1},{33,17},{49,33},{2,50}... | collective-permute-start | bytes 3391496 | tf_op jit(solution)/shard_map/ppermute | solution.py:265
  20.4 22.9 %collective-permute-start.2 = (bf16[896,256]{1,0:T(8,128)(2,1)}, bf16[896,256]{1,0:T(8,128)(2,1)}, u32[]{:S(2)}, u32[]{:S(2)}) collective-permute-start(bf16[896,256]{1,0:T(8,128)(2,1)} %collective-permute-done.w1), channel_id=1, source_target_pairs={{0,64},{64,128},{128,192},{192,256},{256,320},{320,384},{384,448},... | collective-permute-start | bytes 1376264 | tf_op jit(solution)/shard_map/ppermute | solution.py:266
  22.4 22.9 %collective-permute-start.4 = (bf16[896,256]{1,0:T(8,128)(2,1)}, bf16[896,256]{1,0:T(8,128)(2,1)}, u32[]{:S(2)}, u32[]{:S(2)}) collective-permute-start(bf16[896,256]{1,0:T(8,128)(2,1)} %collective-permute-done.1.w7), channel_id=1, source_target_pairs={{0,448},{64,0},{128,64},{192,128},{256,192},{320,256},{384,320},{4... | collective-permute-start | bytes 1376264 | tf_op jit(solution)/shard_map/ppermute | solution.py:267
  27.0 47.9 %copy-start = (bf16[192,8192]{1,0:T(8,128)(2,1)S(1)}, bf16[192,8192]{1,0:T(8,128)(2,1)}, u32[]{:S(2)}) copy-start(bf16[192,8192]{1,0:T(8,128)(2,1)} %grad.3) | copy-start | bytes 9437188
  27.0 41.1 %collective-permute-start.8 = (bf16[192,2944]{1,0:T(8,128)(2,1)}, bf16[192,2944]{1,0:T(8,128)(2,1)}, u32[]{:S(2)}, u32[]{:S(2)}) collective-permute-start(bf16[192,2944]{1,0:T(8,128)(2,1)} %get-tuple-element.25), channel_id=1, source_target_pairs={{0,32},{16,48},{32,0},{48,16},{1,33},{17,49},{33,1},{49,17},{2,34}... | collective-permute-start | bytes 3391496 | tf_op jit(solution)/shard_map/ppermute | solution.py:265
  30.6 57.4 %all-to-all-start = ((bf16[16,208,256]{2,1,0:T(8,128)(2,1)}), bf16[16,208,256]{2,1,0:T(8,128)(2,1)}, u32[]{:S(2)}, u32[]{:S(2)}) async-start(bf16[16,208,256]{2,1,0:T(8,128)(2,1)} %get-tuple-element.31), calls=%async_computation | async-start | bytes 3407872 | tf_op jit(solution)/shard_map/all_to_all | solution.py:268
  43.3 15.4 %collective-permute-start.3 = (bf16[896,256]{1,0:T(8,128)(2,1)}, bf16[896,256]{1,0:T(8,128)(2,1)S(1)}, u32[]{:S(2)}, u32[]{:S(2)}) collective-permute-start(bf16[896,256]{1,0:T(8,128)(2,1)} %collective-permute-done.2.w2), channel_id=1, source_target_pairs={{0,64},{64,128},{128,192},{192,256},{256,320},{320,384},{384,448},... | collective-permute-start | bytes 1376264 | tf_op jit(solution)/shard_map/ppermute | solution.py:269
  45.3 15.2 %collective-permute-start.5 = (bf16[896,256]{1,0:T(8,128)(2,1)}, bf16[896,256]{1,0:T(8,128)(2,1)S(1)}, u32[]{:S(2)}, u32[]{:S(2)}) collective-permute-start(bf16[896,256]{1,0:T(8,128)(2,1)} %collective-permute-done.4.w6), channel_id=1, source_target_pairs={{0,448},{64,0},{128,64},{192,128},{256,192},{320,256},{384,320},{4... | collective-permute-start | bytes 1376264 | tf_op jit(solution)/shard_map/ppermute | solution.py:270
  60.5 14.4 %collective-permute-start.9 = (bf16[896,256]{1,0:T(8,128)(2,1)S(1)}, bf16[896,256]{1,0:T(8,128)(2,1)S(1)}, u32[]{:S(2)}, u32[]{:S(2)}) collective-permute-start(bf16[896,256]{1,0:T(8,128)(2,1)S(1)} %collective-permute-done.3.w3), channel_id=1, source_target_pairs={{0,64},{64,128},{128,192},{192,256},{256,320},{320,384},{384,448},... | collective-permute-start | bytes 1376264 | tf_op jit(solution)/shard_map/ppermute | solution.py:272
  74.9 0.9 copy-start.3
  75.8 1.0 copy-start.4
  87.4 0.7 copy-start.2
  88.1 32.8 %all-to-all-start.1 = ((f32[64,4,192]{2,1,0:T(4,128)}), f32[64,4,192]{2,1,0:T(4,128)S(1)}, u32[]{:S(2)}, u32[]{:S(2)}) async-start(f32[64,4,192]{2,1,0:T(4,128)} %bitcast.2), calls=%async_computation.1 | async-start | bytes 524288 | tf_op jit(solution)/shard_map/all_to_all | solution.py:276
  120.9 0.7 copy-start.5

commit v5 on v4

--- a/solution.py
+++ b/solution.py
@@ -10,7 +10,6 @@
 NB = NZ * NC
 FAR = NY // 2
 EXTRA = 16
-CHUNK = 256
 ZC = ("z", "core")
 BF16, F32 = jnp.bfloat16, jnp.float32
 HBM = pl.BlockSpec(memory_space=pltpu.HBM)
@@ -86,12 +85,13 @@
     ).astype(BF16)
     width = side.shape[1]
     per = hproj.shape[0] // NB
+    half = tok // NC
     for b in range(NB):
-        early[b, 0:tok, :] = side
+        early[b, 0:half, :] = side[(b % NC) * half : (b % NC + 1) * half]
         rows = jnp.concatenate(
             [high[b * per : (b + 1) * per], low[b * per : (b + 1) * per], jnp.zeros((EXTRA - 2 * per, tok), F32)], axis=0
         )
-        early[b, tok : tok + EXTRA, :] = jnp.concatenate(
+        early[b, half : half + EXTRA, :] = jnp.concatenate(
             [rows, jnp.zeros((EXTRA, width - tok), F32)], axis=1
         ).astype(BF16)
     for c in sends:
@@ -104,7 +104,7 @@
     out = jax.ShapeDtypeStruct((tok, hid + NY * wide), BF16)
     return pl.pallas_call(
         prepare_kernel,
-        out_shape=[out] * 3 + [jax.ShapeDtypeStruct((NB, tok + EXTRA, 2 * model.shape[1]), BF16)],
+        out_shape=[out] * 3 + [jax.ShapeDtypeStruct((NB, tok // NC + EXTRA, 2 * model.shape[1]), BF16)],
         in_specs=[HBM] * 6,
         out_specs=[HBM] * 3 + [VMEM],
         scratch_shapes=[
@@ -130,7 +130,6 @@
     nx, tok, hid = gate.shape
     wide = w0.shape[1]
     per = proj.shape[0] // NB
-    chunks = [(c, min(CHUNK, hid - c)) for c in range(0, hid, CHUNK)]
     firsts = []
     for i in range(NY):
         firsts.append(
@@ -140,52 +139,33 @@
         )
     for s, got in enumerate((x1, x2, x3)):
         firsts.append(pltpu.make_async_copy(got.at[:, pl.ds(hid, NY * wide)], g.at[s + 1], g_sem.at[s + 1, 0]))
-    loads = []
-    for k, (c, n) in enumerate(chunks):
-        loads.append(
-            [
-                pltpu.make_async_copy(src.at[pl.ds(c, n)], w.at[pl.ds(c, n), pl.ds(i * wide, wide)], w_sem.at[k, i])
-                for i, src in enumerate((w0, w1, w2, w3, w4, w5, w6, w7))
-            ]
-        )
+    for i, src in enumerate((w0, w1, w2, w3, w4, w5, w6, w7)):
+        firsts.append(pltpu.make_async_copy(src, w.at[:, pl.ds(i * wide, wide)], w_sem.at[i]))
     seconds = [pltpu.make_async_copy(own, gate.at[0], g_sem.at[0, NY]), pltpu.make_async_copy(proj, p, g_sem.at[1, NY])]
     for s, got in enumerate((x1, x2, x3)):
         seconds.append(pltpu.make_async_copy(got.at[:, pl.ds(0, hid)], gate.at[s + 1], g_sem.at[s + 1, 1]))
-    for c in loads[0] + firsts + loads[1] + seconds:
+    for c in firsts + seconds:
         c.start()
-    for load in loads[2:]:
-        for c in load:
-            c.start()
     for c in firsts:
         c.wait()
-    grads = g[...].reshape(nx * tok, NY * wide)
-    total = [None] * nx
-    for k, (c, n) in enumerate(chunks):
-        for cp in loads[k]:
-            cp.wait()
-        gh = dot_nt(grads, w[c : c + n, :])
-        if k == 0:
-            for cp in seconds:
-                cp.wait()
-        gu = gh * silu(gate[:, :, c : c + n].reshape(nx * tok, n).astype(F32))
-        hi = gu.astype(BF16)
-        lo = (gu - hi.astype(F32)).astype(BF16)
-        ps = p[:, c : c + n]
-        for s in range(nx):
-            rows = slice(s * tok, (s + 1) * tok)
-            part = dot_nt(ps, hi[rows]) + dot_nt(ps, lo[rows])
-            total[s] = part if k == 0 else total[s] + part
+    gh = dot_nt(g[...].reshape(nx * tok, NY * wide), w[...])
+    for c in seconds:
+        c.wait()
+    gu = gh * silu(gate[...].reshape(nx * tok, hid).astype(F32))
+    hi = gu.astype(BF16)
+    lo = (gu - hi.astype(F32)).astype(BF16)
     for s in range(nx):
+        rows = slice(s * tok, (s + 1) * tok)
+        total = dot_nt(p[...], hi[rows]) + dot_nt(p[...], lo[rows])
         to = lax.rem(x - s + nx, nx)
         for b in range(NB):
-            out[to, b] = total[s][b * per : (b + 1) * per, :]
+            out[to, b] = total[b * per : (b + 1) * per, :]
 
 
 def main(grad, own, got, shards, proj):
     tok = grad.shape[0]
     hid, wide = shards[0].shape
     per = proj.shape[0] // NB
-    n_chunk = -(-hid // CHUNK)
     return pl.pallas_call(
         main_kernel,
         out_shape=jax.ShapeDtypeStruct((NX, NB, per, tok), F32),
@@ -197,11 +177,11 @@
             pltpu.VMEM((hid, NY * wide), BF16),
             pltpu.VMEM(proj.shape, BF16),
             pltpu.SemaphoreType.DMA((NX, NY + 1)),
-            pltpu.SemaphoreType.DMA((n_chunk, NY)),
+            pltpu.SemaphoreType.DMA((NY,)),
         ],
         compiler_params=pltpu.CompilerParams(vmem_limit_bytes=32 << 20),
         cost_estimate=pl.CostEstimate(
-            flops=16 * NX * tok * hid * (NY * wide + 128), bytes_accessed=9_000_000, transcendentals=NX * tok * hid
+            flops=7 * NX * tok * hid * (NY * wide + 128), bytes_accessed=9_000_000, transcendentals=NX * tok * hid
         ),
         name="main",
     )(grad, own, *got, *shards, proj)
@@ -216,44 +196,46 @@
             out[e : e + 1, k * width : (k + 1) * width] = res[e * per + k : e * per + k + 1, :]
 
 
-def settle_kernel(got, ids, down, side):
-    tok = ids.shape[1]
+def settle_kernel(got, side, hid_side):
     total = got[0].astype(F32)
     for b in range(1, NB):
         total = total + got[b].astype(F32)
-    width = side.shape[1]
-    per = down.shape[1] // width
-    hid_side = total[tok : tok + per, 0:tok] + total[tok + per : tok + 2 * per, 0:tok]
-    score(hid_side, total[0:tok, 0:width], ids[...], down)
-    side[...] = total[0:tok, width:]
-
-
-def settle(got, ids, per):
-    tok, width = ids.shape[1], got.shape[2] // 2
+    half = side.shape[0]
+    per, tok = hid_side.shape
+    side[...] = total[:half]
+    hid_side[...] = total[half : half + per, 0:tok] + total[half + per : half + 2 * per, 0:tok]
+
+
+def settle(got, per):
+    _, rows, width = got.shape
+    half = rows - EXTRA
     return pl.pallas_call(
         settle_kernel,
-        out_shape=[jax.ShapeDtypeStruct((2, per * width), F32), jax.ShapeDtypeStruct((tok, width), F32)],
-        in_specs=[VMEM, VMEM],
+        out_shape=[jax.ShapeDtypeStruct((half, width), F32), jax.ShapeDtypeStruct((per, half * NC), F32)],
+        in_specs=[VMEM],
         out_specs=[VMEM, VMEM],
         name="settle",
-    )(got, ids)
-
-
-def finish_kernel(got, side, ids, up):
+    )(got)
+
+
+def finish_kernel(got, hid_side, mine, other, ids, down, up):
+    first = lax.axis_index("core") == 0
+    side = jnp.concatenate(
+        [jnp.where(first, mine[...], other[...]), jnp.where(first, other[...], mine[...])], axis=0
+    )
+    width = side.shape[1] // 2
     parts = [got[b] for b in range(got.shape[0])]
     while len(parts) > 1:
         parts = [parts[i] + parts[i + 1] for i in range(0, len(parts), 2)]
-    score(parts[0], side[...], ids[...], up)
-
-
-def finish(got, side, ids):
-    return pl.pallas_call(
-        finish_kernel,
-        out_shape=jax.ShapeDtypeStruct((2, got.shape[1] * side.shape[1]), F32),
-        in_specs=[VMEM] * 3,
-        out_specs=VMEM,
-        name="finish",
-    )(got, side, ids)
+    score(hid_side[...], side[:, :width], ids[...], down)
+    score(parts[0], side[:, width:], ids[...], up)
+
+
+def finish(got, hid_side, mine, other, ids):
+    out = jax.ShapeDtypeStruct((2, got.shape[1] * mine.shape[1] // 2), F32)
+    return pl.pallas_call(
+        finish_kernel, out_shape=[out, out], in_specs=[VMEM] * 5, out_specs=[VMEM, VMEM], name="finish"
+    )(got, hid_side, mine, other, ids)
 
 
 def on_device(out_grad, layer_input, gate_pre, up_pre, down_weight, proj_hidden, proj_model, example_ids):
@@ -268,14 +250,15 @@
     got = lax.all_to_all(early, ZC, 0, 0)
     up3 = lax.ppermute(up2, "y", turn(NY, 1))
     dn3 = lax.ppermute(dn2, "y", turn(NY, -1))
-    up3, dn3, x1, x3 = lax.optimization_barrier((up3, dn3, x1, x3))
+    up3, dn3, x1 = lax.optimization_barrier((up3, dn3, x1))
     w4 = lax.ppermute(up3, "y", turn(NY, 1))
-    x2, w4 = lax.optimization_barrier((x2, w4))
+    x2, x3, w4 = lax.optimization_barrier((x2, x3, w4))
     up_part = main(out_grad, gate_pre, (x1, x2, x3), (down_weight, up1, up2, up3, w4, dn3, dn2, dn1), hproj)
     up_part, got = lax.optimization_barrier((up_part, got))
     up_side = lax.all_to_all(up_part.reshape((NX * NB,) + up_part.shape[2:]), ("x",) + ZC, 0, 0)
-    down_scores, side = settle(got, example_ids, up_part.shape[2])
-    return down_scores, finish(up_side, side, example_ids)
+    mine, hid_side = settle(got, up_part.shape[2])
+    other = lax.ppermute(mine, "core", turn(NC, 1))
+    return tuple(finish(up_side, hid_side, mine, other, example_ids))
 
 
 def solution(mesh):

time: 124 us -> 121 us (0.976)
  Pallas kernels: 20.2 us -> 16.9 us
  starting transfers between devices: 68.1 us -> 65.6 us
  local copies, waits for them, and re-layouts: 3.31 us -> 5.1 us
    ppermute x3, waiting for transfers between devices: 3.95 us -> 24.4 us  [on_device(): lax.ppermute(p, 'x', turn(NX, s + 1))]
    ppermute x1, waiting for transfers between devices: 8.85 us -> 0.01 us  [on_device(): up3 = lax.ppermute(up2, 'y', turn(NY, 1))]
    ppermute x1, waiting for transfers between devices: 6.79 us -> 0.01 us  [on_device(): w4 = lax.ppermute(up3, 'y', turn(NY, 1))]
    all_to_all x1, starting transfers between devices: 20.8 us -> 14.5 us  [on_device(): lax.all_to_all(up_part.reshape((NX * NB,) + up_part.shape[2:]), ('x',) +...]
    all_to_all x1, waiting for transfers between devices: 9.54 us -> 6.57 us  [on_device(): lax.all_to_all(up_part.reshape((NX * NB,) + up_part.shape[2:]), ('x',) +...]
    pallas_call x1, Pallas kernels: 10.6 us -> 7.89 us  [main(): pl.pallas_call(main_kernel, out_shape=jax.ShapeDtypeStruct((NX, NB, per,...]
    ppermute x0 -> x1, starting transfers between devices: none -> 2.35 us  [on_device(): other = lax.ppermute(mine, 'core', turn(NC, 1))]
    ppermute x3, starting transfers between devices: 10.1 us -> 12.4 us  [on_device(): lax.ppermute(p, 'x', turn(NX, s + 1))]
  transfers between devices with their start and end apart: 12 -> 13, of which waited for: 5 -> 4; matrix products, arithmetic and copies ran while one was open for 0% -> 0% of each run, Pallas kernels for 15% -> 12%
where the time goes in v5:
time: 121 us
  starting transfers between devices  65.6 us (54%)
  waiting for transfers between devices  32.1 us (27%)
  Pallas kernels  16.9 us (14%)
  local copies, waits for them, and re-layouts  5.1 us (4%)
    ppermute x3, waiting for transfers between devices, on_device(): lax.ppermute(p, 'x', turn(NX, s + 1))  24.4 us
    all_to_all x1, starting transfers between devices, on_device(): lax.all_to_all(up_part.reshape((NX * NB,) + up_part.shape[2:]), ('x',) +...  14.5 us
    all_to_all x1, starting transfers between devices, on_device(): got = lax.all_to_all(early, ZC, 0, 0)  13.3 us
    ppermute x3, starting transfers between devices, on_device(): lax.ppermute(p, 'x', turn(NX, s + 1))  12.4 us
    pallas_call x1, Pallas kernels, main(): pl.pallas_call(main_kernel, out_shape=jax.ShapeDtypeStruct((NX, NB, per,...  7.89 us
    all_to_all x1, waiting for transfers between devices, on_device(): lax.all_to_all(up_part.reshape((NX * NB,) + up_part.shape[2:]), ('x',) +...  6.57 us
    pallas_call x1, Pallas kernels, prepare(): pl.pallas_call(prepare_kernel, out_shape=[out] * 3 + [jax.ShapeDtypeStruc...  5.15 us
    unnamed x18, local copies, waits for them, and re-layouts  5.1 us
  transfers between devices with their start and end apart: 13, of which 4 were waited for; matrix products, arithmetic and copies ran while one was open for 0% of the time, Pallas kernels for 12%

profile of v5, /device:TPU:1, one launch (start us, length us, event | category | flops | bytes accessed | tf_op | source)
XLA Modules:
  0.0 120.5 jit_solution(7881413983117307001)
XLA Ops:
  0.6 4.0 %collective-permute-start = (bf16[896,256]{1,0:T(8,128)(2,1)}, bf16[896,256]{1,0:T(8,128)(2,1)S(1)}, u32[]{:S(2)}, u32[]{:S(2)}) collective-permute-start(bf16[896,256]{1,0:T(8,128)(2,1)} %w0.1), channel_id=1, source_target_pairs={{0,64},{64,128},{128,192},{192,256},{256,320},{320,384},{384,448},... | collective-permute-start | bytes 1376264 | tf_op jit(solution)/shard_map/ppermute | solution.py:243
  4.7 3.8 %collective-permute-start.1 = (bf16[896,256]{1,0:T(8,128)(2,1)}, bf16[896,256]{1,0:T(8,128)(2,1)}, u32[]{:S(2)}, u32[]{:S(2)}) collective-permute-start(bf16[896,256]{1,0:T(8,128)(2,1)} %w0.1), channel_id=1, source_target_pairs={{0,448},{64,0},{128,64},{192,128},{256,192},{320,256},{384,320},{4... | collective-permute-start | bytes 1376264 | tf_op jit(solution)/shard_map/ppermute | solution.py:244
  8.5 5.2 %prepare.1 = (bf16[192,2944]{1,0:T(8,128)(2,1)}, bf16[192,2944]{1,0:T(8,128)(2,1)}, bf16[192,2944]{1,0:T(8,128)(2,1)}, bf16[16,112,256]{2,1,0:T(8,128)(2,1)}) custom-call(bf16[192,8192]{1,0:T(8,128)(2,1)} %grad.3, bf16[192,896]{1,0:T(8,128)(2,1)} %own.1, bf16[192,896]{1,0:T(8,128)(2,1)} %up.1, bf16[192,512]{1,0:T(8,128)(2,1)} %inp.1, ...), custom_call_target="tpu_custom_call" | custom-call | flops 80000000 | bytes 8000000 | tf_op jit(solution)/shard_map/prepare/pallas_call | solution.py:105
  13.7 0.0 copy-start.1
  13.7 3.3 %collective-permute-start.6 = (bf16[192,2944]{1,0:T(8,128)(2,1)}, bf16[192,2944]{1,0:T(8,128)(2,1)}, u32[]{:S(2)}, u32[]{:S(2)}) collective-permute-start(bf16[192,2944]{1,0:T(8,128)(2,1)} %get-tuple-element.22), channel_id=1, source_target_pairs={{0,16},{16,32},{32,48},{48,0},{1,17},{17,33},{33,49},{49,1},{2,18}... | collective-permute-start | bytes 3391496 | tf_op jit(solution)/shard_map/ppermute | solution.py:247
  17.0 0.0 collective-permute-done.w1
  17.0 0.0 collective-permute-done.1.w7
  17.0 4.2 %collective-permute-start.2 = (bf16[896,256]{1,0:T(8,128)(2,1)S(1)}, bf16[896,256]{1,0:T(8,128)(2,1)}, u32[]{:S(2)}, u32[]{:S(2)}) collective-permute-start(bf16[896,256]{1,0:T(8,128)(2,1)S(1)} %collective-permute-done.w1), channel_id=1, source_target_pairs={{0,64},{64,128},{128,192},{192,256},{256,320},{320,384},{384,448},... | collective-permute-start | bytes 1376264 | tf_op jit(solution)/shard_map/ppermute | solution.py:248
  21.2 0.8 copy-done.5
  21.9 2.3 %collective-permute-start.4 = (bf16[896,256]{1,0:T(8,128)(2,1)}, bf16[896,256]{1,0:T(8,128)(2,1)}, u32[]{:S(2)}, u32[]{:S(2)}) collective-permute-start(bf16[896,256]{1,0:T(8,128)(2,1)} %collective-permute-done.1.w7), channel_id=1, source_target_pairs={{0,448},{64,0},{128,64},{192,128},{256,192},{320,256},{384,320},{4... | collective-permute-start | bytes 1376264 | tf_op jit(solution)/shard_map/ppermute | solution.py:249
  24.2 6.4 %collective-permute-start.7 = (bf16[192,2944]{1,0:T(8,128)(2,1)}, bf16[192,2944]{1,0:T(8,128)(2,1)}, u32[]{:S(2)}, u32[]{:S(2)}) collective-permute-start(bf16[192,2944]{1,0:T(8,128)(2,1)} %get-tuple-element.24), channel_id=1, source_target_pairs={{0,32},{16,48},{32,0},{48,16},{1,33},{17,49},{33,1},{49,17},{2,34}... | collective-permute-start | bytes 3391496 | tf_op jit(solution)/shard_map/ppermute | solution.py:247
  30.6 2.8 %collective-permute-start.8 = (bf16[192,2944]{1,0:T(8,128)(2,1)}, bf16[192,2944]{1,0:T(8,128)(2,1)}, u32[]{:S(2)}, u32[]{:S(2)}) collective-permute-start(bf16[192,2944]{1,0:T(8,128)(2,1)} %get-tuple-element.25), channel_id=1, source_target_pairs={{0,48},{16,0},{32,16},{48,32},{1,49},{17,1},{33,17},{49,33},{2,50}... | collective-permute-start | bytes 3391496 | tf_op jit(solution)/shard_map/ppermute | solution.py:247
  33.4 0.0 collective-permute-done.2.w2
  33.4 2.4 %collective-permute-start.3 = (bf16[896,256]{1,0:T(8,128)(2,1)}, bf16[896,256]{1,0:T(8,128)(2,1)}, u32[]{:S(2)}, u32[]{:S(2)}) collective-permute-start(bf16[896,256]{1,0:T(8,128)(2,1)} %collective-permute-done.2.w2), channel_id=1, source_target_pairs={{0,64},{64,128},{128,192},{192,256},{256,320},{320,384},{384,448},... | collective-permute-start | bytes 1376264 | tf_op jit(solution)/shard_map/ppermute | solution.py:251
  35.9 0.0 collective-permute-done.4.w6
  35.9 4.1 %collective-permute-start.5 = (bf16[896,256]{1,0:T(8,128)(2,1)}, bf16[896,256]{1,0:T(8,128)(2,1)}, u32[]{:S(2)}, u32[]{:S(2)}) collective-permute-start(bf16[896,256]{1,0:T(8,128)(2,1)} %collective-permute-done.4.w6), channel_id=1, source_target_pairs={{0,448},{64,0},{128,64},{192,128},{256,192},{320,256},{384,320},{4... | collective-permute-start | bytes 1376264 | tf_op jit(solution)/shard_map/ppermute | solution.py:252
  40.0 13.3 %all-to-all-start = ((bf16[16,112,256]{2,1,0:T(8,128)(2,1)}), bf16[16,112,256]{2,1,0:T(8,128)(2,1)}, u32[]{:S(2)}, u32[]{:S(2)}) async-start(bf16[16,112,256]{2,1,0:T(8,128)(2,1)} %get-tuple-element.31), calls=%async_computation | async-start | bytes 1835008 | tf_op jit(solution)/shard_map/all_to_all | solution.py:250
  53.3 2.2 %collective-permute-start.9 = (bf16[896,256]{1,0:T(8,128)(2,1)}, bf16[896,256]{1,0:T(8,128)(2,1)S(1)}, u32[]{:S(2)}, u32[]{:S(2)}) collective-permute-start(bf16[896,256]{1,0:T(8,128)(2,1)} %collective-permute-done.3.w3), channel_id=1, source_target_pairs={{0,64},{64,128},{128,192},{192,256},{256,320},{320,384},{384,448},... | collective-permute-start | bytes 1376264 | tf_op jit(solution)/shard_map/ppermute | solution.py:254
  55.4 12.5 %collective-permute-done.7.x2 = bf16[192,2944]{1,0:T(8,128)(2,1)} collective-permute-done((bf16[192,2944]{1,0:T(8,128)(2,1)}, bf16[192,2944]{1,0:T(8,128)(2,1)}, u32[]{:S(2)}, u32[]{:S(2)}) %collective-permute-start.7) | collective-permute-done | bytes 1130528 | tf_op jit(solution)/shard_map/ppermute | solution.py:247
  68.0 11.9 %collective-permute-done.8.x3 = bf16[192,2944]{1,0:T(8,128)(2,1)} collective-permute-done((bf16[192,2944]{1,0:T(8,128)(2,1)}, bf16[192,2944]{1,0:T(8,128)(2,1)}, u32[]{:S(2)}, u32[]{:S(2)}) %collective-permute-start.8) | collective-permute-done | bytes 1130528 | tf_op jit(solution)/shard_map/ppermute | solution.py:247
  79.8 0.9 copy-done.3
  80.7 1.0 copy-done.4
  81.8 1.0 copy-done.6
  82.8 7.9 %main.1 = f32[4,16,4,192]{3,2,1,0:T(4,128)S(1)} custom-call(bf16[192,8192]{1,0:T(8,128)(2,1)S(1)} %copy-done, bf16[192,896]{1,0:T(8,128)(2,1)S(1)} %copy-done.1, bf16[192,2944]{1,0:T(8,128)(2,1)} %collective-permute-done.6.x1, bf16[192,2944]{1,0:T(8,128)(2,1)} %collective-permute-done.7.x2, bf16[192,2944]{1,0:T(8,128)(2,1)} %collective-permute-done.8.x3, ...), custom_call_target="tpu_custom_call" | custom-call | flops 10481565696 | bytes 9000000 | tf_op jit(solution)/shard_map/main/pallas_call | solution.py:169
  90.7 0.7 copy-done.2
  91.4 14.5 %all-to-all-start.1 = ((f32[64,4,192]{2,1,0:T(4,128)}), f32[64,4,192]{2,1,0:T(4,128)S(1)}, u32[]{:S(2)}, u32[]{:S(2)}) async-start(f32[64,4,192]{2,1,0:T(4,128)} %bitcast.2), calls=%async_computation.1 | async-start | bytes 524288 | tf_op jit(solution)/shard_map/all_to_all | solution.py:258
  105.9 1.9 %settle.1 = (f32[96,256]{1,0:T(8,128)}, f32[4,192]{1,0:T(4,128)}) custom-call(bf16[16,112,256]{2,1,0:T(8,128)(2,1)} %all-to-all-done.got), custom_call_target="tpu_custom_call" | custom-call | tf_op jit(solution)/shard_map/settle/pallas_call | solution.py:212
  107.8 2.4 %collective-permute-start.10 = (f32[96,256]{1,0:T(8,128)}, f32[96,256]{1,0:T(8,128)S(1)}, u32[]{:S(2)}, u32[]{:S(2)}) collective-permute-start(f32[96,256]{1,0:T(8,128)} %get-tuple-element.35.mine), channel_id=1, source_target_pairs={{0,1},{1,0},{2,3},{3,2},{4,5},{5,4},{6,7},{7,6},{8,9},{9,8},{10,11... | collective-permute-start | bytes 294920 | tf_op jit(solution)/shard_map/ppermute | solution.py:260
  110.2 1.1 collective-permute-done.10.other
  111.3 6.6 %all-to-all-done.1.got = f32[64,4,192]{2,1,0:T(4,128)S(1)} async-done(((f32[64,4,192]{2,1,0:T(4,128)}), f32[64,4,192]{2,1,0:T(4,128)S(1)}, u32[]{:S(2)}, u32[]{:S(2)}) %all-to-all-start.1) | async-done | bytes 196640 | tf_op jit(solution)/shard_map/all_to_all | solution.py:258
  117.9 0.7 copy-done.7
  118.6 1.9 %finish.1 = (f32[2,512]{1,0:T(2,128)}, f32[2,512]{1,0:T(2,128)}) custom-call(f32[64,4,192]{2,1,0:T(4,128)} %copy-done.7, f32[4,192]{1,0:T(4,128)} %get-tuple-element.34.hid_side, f32[96,256]{1,0:T(8,128)} %get-tuple-element.35.mine, f32[96,256]{1,0:T(8,128)} %copy-done.8, s32[1,192]{1,0:T(1,128)} %ids.1), custom_call_target="tpu_custom_call" | custom-call | tf_op jit(solution)/shard_map/finish/pallas_call | solution.py:236
  (16 shorter events, 0.0 us)
Async XLA Ops:
  0.6 16.3 %collective-permute-start = (bf16[896,256]{1,0:T(8,128)(2,1)}, bf16[896,256]{1,0:T(8,128)(2,1)S(1)}, u32[]{:S(2)}, u32[]{:S(2)}) collective-permute-start(bf16[896,256]{1,0:T(8,128)(2,1)} %w0.1), channel_id=1, source_target_pairs={{0,64},{64,128},{128,192},{192,256},{256,320},{320,384},{384,448},... | collective-permute-start | bytes 1376264 | tf_op jit(solution)/shard_map/ppermute | solution.py:243
  4.7 12.3 %collective-permute-start.1 = (bf16[896,256]{1,0:T(8,128)(2,1)}, bf16[896,256]{1,0:T(8,128)(2,1)}, u32[]{:S(2)}, u32[]{:S(2)}) collective-permute-start(bf16[896,256]{1,0:T(8,128)(2,1)} %w0.1), channel_id=1, source_target_pairs={{0,448},{64,0},{128,64},{192,128},{256,192},{320,256},{384,320},{4... | collective-permute-start | bytes 1376264 | tf_op jit(solution)/shard_map/ppermute | solution.py:244
  8.5 71.3 %copy-start = (bf16[192,8192]{1,0:T(8,128)(2,1)S(1)}, bf16[192,8192]{1,0:T(8,128)(2,1)}, u32[]{:S(2)}) copy-start(bf16[192,8192]{1,0:T(8,128)(2,1)} %grad.3) | copy-start | bytes 9437188
  13.7 66.2 %copy-start.1 = (bf16[192,896]{1,0:T(8,128)(2,1)S(1)}, bf16[192,896]{1,0:T(8,128)(2,1)}, u32[]{:S(2)}) copy-start(bf16[192,896]{1,0:T(8,128)(2,1)} %own.1) | copy-start | bytes 1032196
  13.7 39.6 %collective-permute-start.6 = (bf16[192,2944]{1,0:T(8,128)(2,1)}, bf16[192,2944]{1,0:T(8,128)(2,1)}, u32[]{:S(2)}, u32[]{:S(2)}) collective-permute-start(bf16[192,2944]{1,0:T(8,128)(2,1)} %get-tuple-element.22), channel_id=1, source_target_pairs={{0,16},{16,32},{32,48},{48,0},{1,17},{17,33},{33,49},{49,1},{2,18}... | collective-permute-start | bytes 3391496 | tf_op jit(solution)/shard_map/ppermute | solution.py:247
  17.0 16.4 %collective-permute-start.2 = (bf16[896,256]{1,0:T(8,128)(2,1)S(1)}, bf16[896,256]{1,0:T(8,128)(2,1)}, u32[]{:S(2)}, u32[]{:S(2)}) collective-permute-start(bf16[896,256]{1,0:T(8,128)(2,1)S(1)} %collective-permute-done.w1), channel_id=1, source_target_pairs={{0,64},{64,128},{128,192},{192,256},{256,320},{320,384},{384,448},... | collective-permute-start | bytes 1376264 | tf_op jit(solution)/shard_map/ppermute | solution.py:248
  21.2 0.8 copy-start.5
  21.9 14.0 %collective-permute-start.4 = (bf16[896,256]{1,0:T(8,128)(2,1)}, bf16[896,256]{1,0:T(8,128)(2,1)}, u32[]{:S(2)}, u32[]{:S(2)}) collective-permute-start(bf16[896,256]{1,0:T(8,128)(2,1)} %collective-permute-done.1.w7), channel_id=1, source_target_pairs={{0,448},{64,0},{128,64},{192,128},{256,192},{320,256},{384,320},{4... | collective-permute-start | bytes 1376264 | tf_op jit(solution)/shard_map/ppermute | solution.py:249
  24.2 43.7 %collective-permute-start.7 = (bf16[192,2944]{1,0:T(8,128)(2,1)}, bf16[192,2944]{1,0:T(8,128)(2,1)}, u32[]{:S(2)}, u32[]{:S(2)}) collective-permute-start(bf16[192,2944]{1,0:T(8,128)(2,1)} %get-tuple-element.24), channel_id=1, source_target_pairs={{0,32},{16,48},{32,0},{48,16},{1,33},{17,49},{33,1},{49,17},{2,34}... | collective-permute-start | bytes 3391496 | tf_op jit(solution)/shard_map/ppermute | solution.py:247
  30.6 49.2 %collective-permute-start.8 = (bf16[192,2944]{1,0:T(8,128)(2,1)}, bf16[192,2944]{1,0:T(8,128)(2,1)}, u32[]{:S(2)}, u32[]{:S(2)}) collective-permute-start(bf16[192,2944]{1,0:T(8,128)(2,1)} %get-tuple-element.25), channel_id=1, source_target_pairs={{0,48},{16,0},{32,16},{48,32},{1,49},{17,1},{33,17},{49,33},{2,50}... | collective-permute-start | bytes 3391496 | tf_op jit(solution)/shard_map/ppermute | solution.py:247
  33.4 19.8 %collective-permute-start.3 = (bf16[896,256]{1,0:T(8,128)(2,1)}, bf16[896,256]{1,0:T(8,128)(2,1)}, u32[]{:S(2)}, u32[]{:S(2)}) collective-permute-start(bf16[896,256]{1,0:T(8,128)(2,1)} %collective-permute-done.2.w2), channel_id=1, source_target_pairs={{0,64},{64,128},{128,192},{192,256},{256,320},{320,384},{384,448},... | collective-permute-start | bytes 1376264 | tf_op jit(solution)/shard_map/ppermute | solution.py:251
  35.9 17.4 %collective-permute-start.5 = (bf16[896,256]{1,0:T(8,128)(2,1)}, bf16[896,256]{1,0:T(8,128)(2,1)}, u32[]{:S(2)}, u32[]{:S(2)}) collective-permute-start(bf16[896,256]{1,0:T(8,128)(2,1)} %collective-permute-done.4.w6), channel_id=1, source_target_pairs={{0,448},{64,0},{128,64},{192,128},{256,192},{320,256},{384,320},{4... | collective-permute-start | bytes 1376264 | tf_op jit(solution)/shard_map/ppermute | solution.py:252
  40.0 51.4 %all-to-all-start = ((bf16[16,112,256]{2,1,0:T(8,128)(2,1)}), bf16[16,112,256]{2,1,0:T(8,128)(2,1)}, u32[]{:S(2)}, u32[]{:S(2)}) async-start(bf16[16,112,256]{2,1,0:T(8,128)(2,1)} %get-tuple-element.31), calls=%async_computation | async-start | bytes 1835008 | tf_op jit(solution)/shard_map/all_to_all | solution.py:250
  53.3 26.6 %collective-permute-start.9 = (bf16[896,256]{1,0:T(8,128)(2,1)}, bf16[896,256]{1,0:T(8,128)(2,1)S(1)}, u32[]{:S(2)}, u32[]{:S(2)}) collective-permute-start(bf16[896,256]{1,0:T(8,128)(2,1)} %collective-permute-done.3.w3), channel_id=1, source_target_pairs={{0,64},{64,128},{128,192},{192,256},{256,320},{320,384},{384,448},... | collective-permute-start | bytes 1376264 | tf_op jit(solution)/shard_map/ppermute | solution.py:254
  79.8 0.9 copy-start.3
  80.7 1.0 copy-start.4
  81.8 1.0 copy-start.6
  90.7 0.7 copy-start.2
  91.4 26.5 %all-to-all-start.1 = ((f32[64,4,192]{2,1,0:T(4,128)}), f32[64,4,192]{2,1,0:T(4,128)S(1)}, u32[]{:S(2)}, u32[]{:S(2)}) async-start(f32[64,4,192]{2,1,0:T(4,128)} %bitcast.2), calls=%async_computation.1 | async-start | bytes 524288 | tf_op jit(solution)/shard_map/all_to_all | solution.py:258
  107.8 3.5 %collective-permute-start.10 = (f32[96,256]{1,0:T(8,128)}, f32[96,256]{1,0:T(8,128)S(1)}, u32[]{:S(2)}, u32[]{:S(2)}) collective-permute-start(f32[96,256]{1,0:T(8,128)} %get-tuple-element.35.mine), channel_id=1, source_target_pairs={{0,1},{1,0},{2,3},{3,2},{4,5},{5,4},{6,7},{7,6},{8,9},{9,8},{10,11... | collective-permute-start | bytes 294920 | tf_op jit(solution)/shard_map/ppermute | solution.py:260
  111.3 6.6 %copy-start.8 = (f32[96,256]{1,0:T(8,128)}, f32[96,256]{1,0:T(8,128)S(1)}, u32[]{:S(2)}) copy-start(f32[96,256]{1,0:T(8,128)S(1)} %collective-permute-done.10.other) | copy-start | bytes 294916
  117.9 0.7 copy-start.7

commit v6 on v5

--- a/solution.py
+++ b/solution.py
@@ -8,7 +8,7 @@
 
 NY, NX, NZ, NC = 8, 4, 8, 2
 NB = NZ * NC
-FAR = NY // 2
+HALF = NY // NC
 EXTRA = 16
 ZC = ("z", "core")
 BF16, F32 = jnp.bfloat16, jnp.float32
@@ -40,17 +40,18 @@
 def prepare_kernel(grad, gate, up, inp, model, hproj, p1, p2, p3, early, buf, gate_v, up_v, inp_v, gcols, model_v, hproj_v, in_sem, out_sem, side_sem):
     outs = (p1, p2, p3)
     tok, hid = gate.shape
-    wide = (p1.shape[1] - hid) // NY
+    wide = (p1.shape[1] - hid) // HALF
+    core = lax.axis_index("core")
     feat = inp.shape[1]
     y, x, blk = here()
     fills, sends = [], []
     for s, out in enumerate(outs):
         at = lax.rem(x + s + 1, NX)
-        fill = [pltpu.make_async_copy(gate, buf.at[s, :, pl.ds(0, hid)], in_sem.at[s, NY])]
-        for i in range(NY):
+        fill = [pltpu.make_async_copy(gate, buf.at[s, :, pl.ds(0, hid)], in_sem.at[s, HALF])]
+        for i in range(HALF):
             fill.append(
                 pltpu.make_async_copy(
-                    grad.at[:, pl.ds(columns(y, i, at, wide), wide)],
+                    grad.at[:, pl.ds(columns(y, core * HALF + i, at, wide), wide)],
                     buf.at[s, :, pl.ds(hid + i * wide, wide)],
                     in_sem.at[s, i],
                 )
@@ -101,21 +102,21 @@
 def prepare(grad, gate, up, inp, model, hproj, wide):
     tok, hid = gate.shape
     feat = inp.shape[1]
-    out = jax.ShapeDtypeStruct((tok, hid + NY * wide), BF16)
+    out = jax.ShapeDtypeStruct((tok, hid + HALF * wide), BF16)
     return pl.pallas_call(
         prepare_kernel,
         out_shape=[out] * 3 + [jax.ShapeDtypeStruct((NB, tok // NC + EXTRA, 2 * model.shape[1]), BF16)],
         in_specs=[HBM] * 6,
         out_specs=[HBM] * 3 + [VMEM],
         scratch_shapes=[
-            pltpu.VMEM((NX - 1, tok, hid + NY * wide), BF16),
+            pltpu.VMEM((NX - 1, tok, hid + HALF * wide), BF16),
             pltpu.VMEM((tok, hid), BF16),
             pltpu.VMEM((tok, hid), BF16),
             pltpu.VMEM((tok, feat), BF16),
             pltpu.VMEM((tok, feat), BF16),
             pltpu.VMEM(model.shape, BF16),
             pltpu.VMEM(hproj.shape, BF16),
-            pltpu.SemaphoreType.DMA((NX - 1, NY + 1)),
+            pltpu.SemaphoreType.DMA((NX - 1, HALF + 1)),
             pltpu.SemaphoreType.DMA((NX - 1,)),
             pltpu.SemaphoreType.DMA((6,)),
         ],
@@ -125,10 +126,14 @@
     )(grad, gate, up, inp, model, hproj)
 
 
-def main_kernel(grad, own, x1, x2, x3, w0, w1, w2, w3, w4, w5, w6, w7, proj, out, g, gate, w, p, g_sem, w_sem):
+def main_kernel(grad, own, x1, x2, x3, o1, o2, o3, w0, w1, w2, w3, w4, w5, w6, w7, proj, out, g, gate, w, p, g_sem, w_sem):
     y, x, _ = here()
+    core = lax.axis_index("core")
     nx, tok, hid = gate.shape
     wide = w0.shape[1]
+    n = HALF * wide
+    near = pl.ds(pl.multiple_of(core * n, n), n)
+    away = pl.ds(pl.multiple_of((1 - core) * n, n), n)
     per = proj.shape[0] // NB
     firsts = []
     for i in range(NY):
@@ -137,13 +142,14 @@
                 grad.at[:, pl.ds(columns(y, i, x, wide), wide)], g.at[0, :, pl.ds(i * wide, wide)], g_sem.at[0, i]
             )
         )
-    for s, got in enumerate((x1, x2, x3)):
-        firsts.append(pltpu.make_async_copy(got.at[:, pl.ds(hid, NY * wide)], g.at[s + 1], g_sem.at[s + 1, 0]))
+    for s, (mine, other) in enumerate(((x1, o1), (x2, o2), (x3, o3))):
+        firsts.append(pltpu.make_async_copy(mine.at[:, pl.ds(hid, n)], g.at[s + 1, :, near], g_sem.at[s + 1, 0]))
+        firsts.append(pltpu.make_async_copy(other.at[:, pl.ds(hid, n)], g.at[s + 1, :, away], g_sem.at[s + 1, 1]))
     for i, src in enumerate((w0, w1, w2, w3, w4, w5, w6, w7)):
         firsts.append(pltpu.make_async_copy(src, w.at[:, pl.ds(i * wide, wide)], w_sem.at[i]))
     seconds = [pltpu.make_async_copy(own, gate.at[0], g_sem.at[0, NY]), pltpu.make_async_copy(proj, p, g_sem.at[1, NY])]
     for s, got in enumerate((x1, x2, x3)):
-        seconds.append(pltpu.make_async_copy(got.at[:, pl.ds(0, hid)], gate.at[s + 1], g_sem.at[s + 1, 1]))
+        seconds.append(pltpu.make_async_copy(got.at[:, pl.ds(0, hid)], gate.at[s + 1], g_sem.at[s + 1, 2]))
     for c in firsts + seconds:
         c.start()
     for c in firsts:
@@ -162,14 +168,14 @@
             out[to, b] = total[b * per : (b + 1) * per, :]
 
 
-def main(grad, own, got, shards, proj):
+def main(grad, own, got, swapped, shards, proj):
     tok = grad.shape[0]
     hid, wide = shards[0].shape
     per = proj.shape[0] // NB
     return pl.pallas_call(
         main_kernel,
         out_shape=jax.ShapeDtypeStruct((NX, NB, per, tok), F32),
-        in_specs=[HBM] * 14,
+        in_specs=[HBM] * 17,
         out_specs=VMEM,
         scratch_shapes=[
             pltpu.VMEM((NX, tok, NY * wide), BF16),
@@ -179,12 +185,12 @@
             pltpu.SemaphoreType.DMA((NX, NY + 1)),
             pltpu.SemaphoreType.DMA((NY,)),
         ],
-        compiler_params=pltpu.CompilerParams(vmem_limit_bytes=32 << 20),
+        compiler_params=pltpu.CompilerParams(vmem_limit_bytes=50 << 20),
         cost_estimate=pl.CostEstimate(
-            flops=7 * NX * tok * hid * (NY * wide + 128), bytes_accessed=9_000_000, transcendentals=NX * tok * hid
+            flops=4 * NX * tok * hid * (NY * wide + 128), bytes_accessed=9_000_000, transcendentals=NX * tok * hid
         ),
         name="main",
-    )(grad, own, *got, *shards, proj)
+    )(grad, own, *got, *swapped, *shards, proj)
 
 
 def score(left, right, which, out):
@@ -248,12 +254,14 @@
     up2 = lax.ppermute(up1, "y", turn(NY, 1))
     dn2 = lax.ppermute(dn1, "y", turn(NY, -1))
     got = lax.all_to_all(early, ZC, 0, 0)
+    up2, dn2, x1 = lax.optimization_barrier((up2, dn2, x1))
     up3 = lax.ppermute(up2, "y", turn(NY, 1))
     dn3 = lax.ppermute(dn2, "y", turn(NY, -1))
-    up3, dn3, x1 = lax.optimization_barrier((up3, dn3, x1))
+    up3, dn3, x3 = lax.optimization_barrier((up3, dn3, x3))
     w4 = lax.ppermute(up3, "y", turn(NY, 1))
-    x2, x3, w4 = lax.optimization_barrier((x2, x3, w4))
-    up_part = main(out_grad, gate_pre, (x1, x2, x3), (down_weight, up1, up2, up3, w4, dn3, dn2, dn1), hproj)
+    o1, o2, o3 = [lax.ppermute(v, "core", turn(NC, 1)) for v in (x1, x2, x3)]
+    o1, o2, o3, w4 = lax.optimization_barrier((o1, o2, o3, w4))
+    up_part = main(out_grad, gate_pre, (x1, x2, x3), (o1, o2, o3), (down_weight, up1, up2, up3, w4, dn3, dn2, dn1), hproj)
     up_part, got = lax.optimization_barrier((up_part, got))
     up_side = lax.all_to_all(up_part.reshape((NX * NB,) + up_part.shape[2:]), ("x",) + ZC, 0, 0)
     mine, hid_side = settle(got, up_part.shape[2])

time: 121 us -> 119 us (0.983)
  starting transfers between devices: 65.6 us -> 73.5 us
  waiting for transfers between devices: 32.1 us -> 25.8 us
  local copies, waits for them, and re-layouts: 5.1 us -> 1.6 us
    ppermute x3, waiting for transfers between devices: 24.4 us -> 3.27 us  [on_device(): lax.ppermute(p, 'x', turn(NX, s + 1))]
    ppermute x1, waiting for transfers between devices: 0.01 us -> 12.8 us  [on_device(): w4 = lax.ppermute(up3, 'y', turn(NY, 1))]
    ppermute x0 -> x3, starting transfers between devices: none -> 7.78 us  [on_device(): o1, o2, o3 = [lax.ppermute(v, 'core', turn(NC, 1)) for v in (x1, x2, x3)]]
    unnamed x18 -> x20, local copies, waits for them, and re-layouts: 5.1 us -> 1.6 us
    ppermute x1, waiting for transfers between devices: 0.01 us -> 2.04 us  [on_device(): dn2 = lax.ppermute(dn1, 'y', turn(NY, -1))]
    ppermute x1, starting transfers between devices: 4.06 us -> 2.56 us  [on_device(): dn3 = lax.ppermute(dn2, 'y', turn(NY, -1))]
    ppermute x1, starting transfers between devices: 2.44 us -> 3.93 us  [on_device(): up3 = lax.ppermute(up2, 'y', turn(NY, 1))]
  transfers between devices with their start and end apart: 13 -> 16, of which waited for: 4 -> 5; matrix products, arithmetic and copies ran while one was open for 0% -> 0% of each run, Pallas kernels for 12% -> 13%
where the time goes in v6:
time: 119 us
  starting transfers between devices  73.5 us (62%)
  waiting for transfers between devices  25.8 us (22%)
  Pallas kernels  16.8 us (14%)
  local copies, waits for them, and re-layouts  1.6 us (1%)
    all_to_all x1, starting transfers between devices, on_device(): lax.all_to_all(up_part.reshape((NX * NB,) + up_part.shape[2:]), ('x',) +...  13.7 us
    all_to_all x1, starting transfers between devices, on_device(): got = lax.all_to_all(early, ZC, 0, 0)  13.4 us
    ppermute x1, waiting for transfers between devices, on_device(): w4 = lax.ppermute(up3, 'y', turn(NY, 1))  12.8 us
    ppermute x3, starting transfers between devices, on_device(): lax.ppermute(p, 'x', turn(NX, s + 1))  12.7 us
    pallas_call x1, Pallas kernels, main(): pl.pallas_call(main_kernel, out_shape=jax.ShapeDtypeStruct((NX, NB, per,...  8.38 us
    ppermute x3, starting transfers between devices, on_device(): o1, o2, o3 = [lax.ppermute(v, 'core', turn(NC, 1)) for v in (x1, x2, x3)]  7.78 us
    all_to_all x1, waiting for transfers between devices, on_device(): lax.all_to_all(up_part.reshape((NX * NB,) + up_part.shape[2:]), ('x',) +...  6.58 us
    ppermute x1, starting transfers between devices, on_device(): up2 = lax.ppermute(up1, 'y', turn(NY, 1))  4.69 us
  transfers between devices with their start and end apart: 16, of which 5 were waited for; matrix products, arithmetic and copies ran while one was open for 0% of the time, Pallas kernels for 13%

profile of v6, /device:TPU:1, one launch (start us, length us, event | category | flops | bytes accessed | tf_op | source)
XLA Modules:
  0.0 118.6 jit_solution(14040425713141560143)
XLA Ops:
  0.7 4.2 %collective-permute-start = (bf16[896,256]{1,0:T(8,128)(2,1)}, bf16[896,256]{1,0:T(8,128)(2,1)S(1)}, u32[]{:S(2)}, u32[]{:S(2)}) collective-permute-start(bf16[896,256]{1,0:T(8,128)(2,1)} %w0.1), channel_id=1, source_target_pairs={{0,64},{64,128},{128,192},{192,256},{256,320},{320,384},{384,448},... | collective-permute-start | bytes 1376264 | tf_op jit(solution)/shard_map/ppermute | solution.py:249
  4.8 3.8 %collective-permute-start.1 = (bf16[896,256]{1,0:T(8,128)(2,1)}, bf16[896,256]{1,0:T(8,128)(2,1)S(1)}, u32[]{:S(2)}, u32[]{:S(2)}) collective-permute-start(bf16[896,256]{1,0:T(8,128)(2,1)} %w0.1), channel_id=1, source_target_pairs={{0,448},{64,0},{128,64},{192,128},{256,192},{320,256},{384,320},{4... | collective-permute-start | bytes 1376264 | tf_op jit(solution)/shard_map/ppermute | solution.py:250
  8.7 4.6 %prepare.1 = (bf16[192,1920]{1,0:T(8,128)(2,1)}, bf16[192,1920]{1,0:T(8,128)(2,1)}, bf16[192,1920]{1,0:T(8,128)(2,1)}, bf16[16,112,256]{2,1,0:T(8,128)(2,1)}) custom-call(bf16[192,8192]{1,0:T(8,128)(2,1)} %grad.3, bf16[192,896]{1,0:T(8,128)(2,1)} %own.1, bf16[192,896]{1,0:T(8,128)(2,1)} %up.1, bf16[192,512]{1,0:T(8,128)(2,1)} %inp.1, ...), custom_call_target="tpu_custom_call" | custom-call | flops 80000000 | bytes 8000000 | tf_op jit(solution)/shard_map/prepare/pallas_call | solution.py:106
  13.3 3.2 %collective-permute-start.4 = (bf16[192,1920]{1,0:T(8,128)(2,1)}, bf16[192,1920]{1,0:T(8,128)(2,1)S(1)}, u32[]{:S(2)}, u32[]{:S(2)}) collective-permute-start(bf16[192,1920]{1,0:T(8,128)(2,1)} %get-tuple-element.26), channel_id=1, source_target_pairs={{0,16},{16,32},{32,48},{48,0},{1,17},{17,33},{33,49},{49,1},{2,18}... | collective-permute-start | bytes 2211848 | tf_op jit(solution)/shard_map/ppermute | solution.py:253
  16.5 0.0 collective-permute-done.w1
  16.5 0.0 collective-permute-done.1.w7
  16.5 4.7 %collective-permute-start.2 = (bf16[896,256]{1,0:T(8,128)(2,1)S(1)}, bf16[896,256]{1,0:T(8,128)(2,1)S(1)}, u32[]{:S(2)}, u32[]{:S(2)}) collective-permute-start(bf16[896,256]{1,0:T(8,128)(2,1)S(1)} %collective-permute-done.w1), channel_id=1, source_target_pairs={{0,64},{64,128},{128,192},{192,256},{256,320},{320,384},{384,448},... | collective-permute-start | bytes 1376264 | tf_op jit(solution)/shard_map/ppermute | solution.py:254
  21.2 1.9 %collective-permute-start.3 = (bf16[896,256]{1,0:T(8,128)(2,1)S(1)}, bf16[896,256]{1,0:T(8,128)(2,1)S(1)}, u32[]{:S(2)}, u32[]{:S(2)}) collective-permute-start(bf16[896,256]{1,0:T(8,128)(2,1)S(1)} %collective-permute-done.1.w7), channel_id=1, source_target_pairs={{0,448},{64,0},{128,64},{192,128},{256,192},{320,256},{384,320},{4... | collective-permute-start | bytes 1376264 | tf_op jit(solution)/shard_map/ppermute | solution.py:255
  23.1 6.8 %collective-permute-start.5 = (bf16[192,1920]{1,0:T(8,128)(2,1)}, bf16[192,1920]{1,0:T(8,128)(2,1)}, u32[]{:S(2)}, u32[]{:S(2)}) collective-permute-start(bf16[192,1920]{1,0:T(8,128)(2,1)} %get-tuple-element.28), channel_id=1, source_target_pairs={{0,32},{16,48},{32,0},{48,16},{1,33},{17,49},{33,1},{49,17},{2,34}... | collective-permute-start | bytes 2211848 | tf_op jit(solution)/shard_map/ppermute | solution.py:253
  29.9 2.8 %collective-permute-start.8 = (bf16[192,1920]{1,0:T(8,128)(2,1)}, bf16[192,1920]{1,0:T(8,128)(2,1)}, u32[]{:S(2)}, u32[]{:S(2)}) collective-permute-start(bf16[192,1920]{1,0:T(8,128)(2,1)} %get-tuple-element.31), channel_id=1, source_target_pairs={{0,48},{16,0},{32,16},{48,32},{1,49},{17,1},{33,17},{49,33},{2,50}... | collective-permute-start | bytes 2211848 | tf_op jit(solution)/shard_map/ppermute | solution.py:253
  32.7 0.0 collective-permute-done.4.x1
  32.7 2.0 %collective-permute-done.3.w6 = bf16[896,256]{1,0:T(8,128)(2,1)S(1)} collective-permute-done((bf16[896,256]{1,0:T(8,128)(2,1)S(1)}, bf16[896,256]{1,0:T(8,128)(2,1)S(1)}, u32[]{:S(2)}, u32[]{:S(2)}) %collective-permute-start.3) | collective-permute-done | bytes 458784 | tf_op jit(solution)/shard_map/ppermute | solution.py:255
  34.8 3.9 %collective-permute-start.6 = (bf16[896,256]{1,0:T(8,128)(2,1)S(1)}, bf16[896,256]{1,0:T(8,128)(2,1)S(1)}, u32[]{:S(2)}, u32[]{:S(2)}) collective-permute-start(bf16[896,256]{1,0:T(8,128)(2,1)S(1)} %collective-permute-done.2.w2), channel_id=1, source_target_pairs={{0,64},{64,128},{128,192},{192,256},{256,320},{320,384},{384,448},... | collective-permute-start | bytes 1376264 | tf_op jit(solution)/shard_map/ppermute | solution.py:258
  38.7 2.6 %collective-permute-start.7 = (bf16[896,256]{1,0:T(8,128)(2,1)S(1)}, bf16[896,256]{1,0:T(8,128)(2,1)S(1)}, u32[]{:S(2)}, u32[]{:S(2)}) collective-permute-start(bf16[896,256]{1,0:T(8,128)(2,1)S(1)} %collective-permute-done.3.w6), channel_id=1, source_target_pairs={{0,448},{64,0},{128,64},{192,128},{256,192},{320,256},{384,320},{4... | collective-permute-start | bytes 1376264 | tf_op jit(solution)/shard_map/ppermute | solution.py:259
  41.3 13.4 %all-to-all-start = ((bf16[16,112,256]{2,1,0:T(8,128)(2,1)}), bf16[16,112,256]{2,1,0:T(8,128)(2,1)}, u32[]{:S(2)}, u32[]{:S(2)}) async-start(bf16[16,112,256]{2,1,0:T(8,128)(2,1)} %get-tuple-element.39), calls=%async_computation | async-start | bytes 1835008 | tf_op jit(solution)/shard_map/all_to_all | solution.py:256
  54.7 0.0 collective-permute-done.5.x2
  54.7 2.1 %collective-permute-start.10 = (bf16[192,1920]{1,0:T(8,128)(2,1)}, bf16[192,1920]{1,0:T(8,128)(2,1)S(1)}, u32[]{:S(2)}, u32[]{:S(2)}) collective-permute-start(bf16[192,1920]{1,0:T(8,128)(2,1)} %collective-permute-done.5.x2), channel_id=1, source_target_pairs={{0,1},{1,0},{2,3},{3,2},{4,5},{5,4},{6,7},{7,6},{8,9},{9,8},{10,11... | collective-permute-start | bytes 2211848 | tf_op jit(solution)/shard_map/ppermute | solution.py:262
  56.7 2.3 %collective-permute-start.9 = (bf16[192,1920]{1,0:T(8,128)(2,1)}, bf16[192,1920]{1,0:T(8,128)(2,1)S(1)}, u32[]{:S(2)}, u32[]{:S(2)}) collective-permute-start(bf16[192,1920]{1,0:T(8,128)(2,1)} %copy-done.5), channel_id=1, source_target_pairs={{0,1},{1,0},{2,3},{3,2},{4,5},{5,4},{6,7},{7,6},{8,9},{9,8},{10,11... | collective-permute-start | bytes 2211848 | tf_op jit(solution)/shard_map/ppermute | solution.py:262
  59.0 3.3 %collective-permute-done.8.x3 = bf16[192,1920]{1,0:T(8,128)(2,1)} collective-permute-done((bf16[192,1920]{1,0:T(8,128)(2,1)}, bf16[192,1920]{1,0:T(8,128)(2,1)}, u32[]{:S(2)}, u32[]{:S(2)}) %collective-permute-start.8) | collective-permute-done | bytes 737312 | tf_op jit(solution)/shard_map/ppermute | solution.py:253
  62.3 3.5 %collective-permute-start.11 = (bf16[192,1920]{1,0:T(8,128)(2,1)}, bf16[192,1920]{1,0:T(8,128)(2,1)S(1)}, u32[]{:S(2)}, u32[]{:S(2)}) collective-permute-start(bf16[192,1920]{1,0:T(8,128)(2,1)} %collective-permute-done.8.x3), channel_id=1, source_target_pairs={{0,1},{1,0},{2,3},{3,2},{4,5},{5,4},{6,7},{7,6},{8,9},{9,8},{10,11... | collective-permute-start | bytes 2211848 | tf_op jit(solution)/shard_map/ppermute | solution.py:262
  65.7 2.4 %collective-permute-start.12 = (bf16[896,256]{1,0:T(8,128)(2,1)S(1)}, bf16[896,256]{1,0:T(8,128)(2,1)S(1)}, u32[]{:S(2)}, u32[]{:S(2)}) collective-permute-start(bf16[896,256]{1,0:T(8,128)(2,1)S(1)} %collective-permute-done.6.w3), channel_id=1, source_target_pairs={{0,64},{64,128},{128,192},{192,256},{256,320},{320,384},{384,448},... | collective-permute-start | bytes 1376264 | tf_op jit(solution)/shard_map/ppermute | solution.py:261
  68.2 0.0 collective-permute-done.10.o2
  68.2 12.8 %collective-permute-done.12.w4 = bf16[896,256]{1,0:T(8,128)(2,1)S(1)} collective-permute-done((bf16[896,256]{1,0:T(8,128)(2,1)S(1)}, bf16[896,256]{1,0:T(8,128)(2,1)S(1)}, u32[]{:S(2)}, u32[]{:S(2)}) %collective-permute-start.12) | collective-permute-done | bytes 458784 | tf_op jit(solution)/shard_map/ppermute | solution.py:261
  81.0 0.9 copy-done.8
  81.9 8.4 %main.1 = f32[4,16,4,192]{3,2,1,0:T(4,128)} custom-call(bf16[192,8192]{1,0:T(8,128)(2,1)} %grad.3, bf16[192,896]{1,0:T(8,128)(2,1)S(1)} %copy-done, bf16[192,1920]{1,0:T(8,128)(2,1)} %copy-done.5, bf16[192,1920]{1,0:T(8,128)(2,1)} %collective-permute-done.5.x2, bf16[192,1920]{1,0:T(8,128)(2,1)} %collective-permute-done.8.x3, bf16[192,1920]{1,0:T(8,128)(2,1)} %copy-done.7, ...), custom_call_target="tpu_custom_call" | custom-call | flops 5989466112 | bytes 9000000 | tf_op jit(solution)/shard_map/main/pallas_call | solution.py:175
  90.3 13.7 %all-to-all-start.1 = ((f32[64,4,192]{2,1,0:T(4,128)}), f32[64,4,192]{2,1,0:T(4,128)S(1)}, u32[]{:S(2)}, u32[]{:S(2)}) async-start(f32[64,4,192]{2,1,0:T(4,128)} %bitcast.1), calls=%async_computation.1 | async-start | bytes 524288 | tf_op jit(solution)/shard_map/all_to_all | solution.py:266
  104.0 1.9 %settle.1 = (f32[96,256]{1,0:T(8,128)}, f32[4,192]{1,0:T(4,128)}) custom-call(bf16[16,112,256]{2,1,0:T(8,128)(2,1)} %all-to-all-done.got), custom_call_target="tpu_custom_call" | custom-call | tf_op jit(solution)/shard_map/settle/pallas_call | solution.py:218
  105.9 2.4 %collective-permute-start.13 = (f32[96,256]{1,0:T(8,128)}, f32[96,256]{1,0:T(8,128)S(1)}, u32[]{:S(2)}, u32[]{:S(2)}) collective-permute-start(f32[96,256]{1,0:T(8,128)} %get-tuple-element.43.mine), channel_id=1, source_target_pairs={{0,1},{1,0},{2,3},{3,2},{4,5},{5,4},{6,7},{7,6},{8,9},{9,8},{10,11... | collective-permute-start | bytes 294920 | tf_op jit(solution)/shard_map/ppermute | solution.py:268
  108.3 1.1 collective-permute-done.13.other
  109.4 6.6 %all-to-all-done.1.got = f32[64,4,192]{2,1,0:T(4,128)S(1)} async-done(((f32[64,4,192]{2,1,0:T(4,128)}), f32[64,4,192]{2,1,0:T(4,128)S(1)}, u32[]{:S(2)}, u32[]{:S(2)}) %all-to-all-start.1) | async-done | bytes 196640 | tf_op jit(solution)/shard_map/all_to_all | solution.py:266
  116.0 0.7 copy-done.3
  116.7 1.9 %finish.1 = (f32[2,512]{1,0:T(2,128)}, f32[2,512]{1,0:T(2,128)}) custom-call(f32[64,4,192]{2,1,0:T(4,128)} %copy-done.3, f32[4,192]{1,0:T(4,128)} %get-tuple-element.42.hid_side, f32[96,256]{1,0:T(8,128)} %get-tuple-element.43.mine, f32[96,256]{1,0:T(8,128)} %copy-done.4, s32[1,192]{1,0:T(1,128)} %ids.1), custom_call_target="tpu_custom_call" | custom-call | tf_op jit(solution)/shard_map/finish/pallas_call | solution.py:242
  (24 shorter events, 0.1 us)
Async XLA Ops:
  0.6 81.2 %copy-start.2 = (bf16[896,256]{1,0:T(8,128)(2,1)S(1)}, bf16[896,256]{1,0:T(8,128)(2,1)}, u32[]{:S(2)}) copy-start(bf16[896,256]{1,0:T(8,128)(2,1)} %w0.1) | copy-start | bytes 1376260
  0.6 81.2 %copy-start = (bf16[192,896]{1,0:T(8,128)(2,1)S(1)}, bf16[192,896]{1,0:T(8,128)(2,1)}, u32[]{:S(2)}) copy-start(bf16[192,896]{1,0:T(8,128)(2,1)} %own.1) | copy-start | bytes 1032196
  0.7 81.2 %copy-start.1 = (bf16[896,64]{0,1:T(8,128)(2,1)S(1)}, bf16[896,64]{0,1:T(8,128)(2,1)}, u32[]{:S(2)}) copy-start(bf16[896,64]{0,1:T(8,128)(2,1)} %param.13) | copy-start | bytes 344068
  0.7 15.8 %collective-permute-start = (bf16[896,256]{1,0:T(8,128)(2,1)}, bf16[896,256]{1,0:T(8,128)(2,1)S(1)}, u32[]{:S(2)}, u32[]{:S(2)}) collective-permute-start(bf16[896,256]{1,0:T(8,128)(2,1)} %w0.1), channel_id=1, source_target_pairs={{0,64},{64,128},{128,192},{192,256},{256,320},{320,384},{384,448},... | collective-permute-start | bytes 1376264 | tf_op jit(solution)/shard_map/ppermute | solution.py:249
  4.8 11.7 %collective-permute-start.1 = (bf16[896,256]{1,0:T(8,128)(2,1)}, bf16[896,256]{1,0:T(8,128)(2,1)S(1)}, u32[]{:S(2)}, u32[]{:S(2)}) collective-permute-start(bf16[896,256]{1,0:T(8,128)(2,1)} %w0.1), channel_id=1, source_target_pairs={{0,448},{64,0},{128,64},{192,128},{256,192},{320,256},{384,320},{4... | collective-permute-start | bytes 1376264 | tf_op jit(solution)/shard_map/ppermute | solution.py:250
  13.3 19.4 %collective-permute-start.4 = (bf16[192,1920]{1,0:T(8,128)(2,1)}, bf16[192,1920]{1,0:T(8,128)(2,1)S(1)}, u32[]{:S(2)}, u32[]{:S(2)}) collective-permute-start(bf16[192,1920]{1,0:T(8,128)(2,1)} %get-tuple-element.26), channel_id=1, source_target_pairs={{0,16},{16,32},{32,48},{48,0},{1,17},{17,33},{33,49},{49,1},{2,18}... | collective-permute-start | bytes 2211848 | tf_op jit(solution)/shard_map/ppermute | solution.py:253
  16.5 22.2 %copy-start.9 = (bf16[896,256]{1,0:T(8,128)(2,1)}, bf16[896,256]{1,0:T(8,128)(2,1)S(1)}, u32[]{:S(2)}) copy-start(bf16[896,256]{1,0:T(8,128)(2,1)S(1)} %collective-permute-done.1.w7) | copy-start | bytes 1376260
  16.5 16.2 %collective-permute-start.2 = (bf16[896,256]{1,0:T(8,128)(2,1)S(1)}, bf16[896,256]{1,0:T(8,128)(2,1)S(1)}, u32[]{:S(2)}, u32[]{:S(2)}) collective-permute-start(bf16[896,256]{1,0:T(8,128)(2,1)S(1)} %collective-permute-done.w1), channel_id=1, source_target_pairs={{0,64},{64,128},{128,192},{192,256},{256,320},{320,384},{384,448},... | collective-permute-start | bytes 1376264 | tf_op jit(solution)/shard_map/ppermute | solution.py:254
  21.2 13.6 %collective-permute-start.3 = (bf16[896,256]{1,0:T(8,128)(2,1)S(1)}, bf16[896,256]{1,0:T(8,128)(2,1)S(1)}, u32[]{:S(2)}, u32[]{:S(2)}) collective-permute-start(bf16[896,256]{1,0:T(8,128)(2,1)S(1)} %collective-permute-done.1.w7), channel_id=1, source_target_pairs={{0,448},{64,0},{128,64},{192,128},{256,192},{320,256},{384,320},{4... | collective-permute-start | bytes 1376264 | tf_op jit(solution)/shard_map/ppermute | solution.py:255
  23.1 31.5 %collective-permute-start.5 = (bf16[192,1920]{1,0:T(8,128)(2,1)}, bf16[192,1920]{1,0:T(8,128)(2,1)}, u32[]{:S(2)}, u32[]{:S(2)}) collective-permute-start(bf16[192,1920]{1,0:T(8,128)(2,1)} %get-tuple-element.28), channel_id=1, source_target_pairs={{0,32},{16,48},{32,0},{48,16},{1,33},{17,49},{33,1},{49,17},{2,34}... | collective-permute-start | bytes 2211848 | tf_op jit(solution)/shard_map/ppermute | solution.py:253
  29.9 32.3 %collective-permute-start.8 = (bf16[192,1920]{1,0:T(8,128)(2,1)}, bf16[192,1920]{1,0:T(8,128)(2,1)}, u32[]{:S(2)}, u32[]{:S(2)}) collective-permute-start(bf16[192,1920]{1,0:T(8,128)(2,1)} %get-tuple-element.31), channel_id=1, source_target_pairs={{0,48},{16,0},{32,16},{48,32},{1,49},{17,1},{33,17},{49,33},{2,50}... | collective-permute-start | bytes 2211848 | tf_op jit(solution)/shard_map/ppermute | solution.py:253
  32.7 2.1 %copy-start.5 = (bf16[192,1920]{1,0:T(8,128)(2,1)}, bf16[192,1920]{1,0:T(8,128)(2,1)S(1)}, u32[]{:S(2)}) copy-start(bf16[192,1920]{1,0:T(8,128)(2,1)S(1)} %collective-permute-done.4.x1) | copy-start | bytes 2211844
  34.8 27.5 %collective-permute-start.6 = (bf16[896,256]{1,0:T(8,128)(2,1)S(1)}, bf16[896,256]{1,0:T(8,128)(2,1)S(1)}, u32[]{:S(2)}, u32[]{:S(2)}) collective-permute-start(bf16[896,256]{1,0:T(8,128)(2,1)S(1)} %collective-permute-done.2.w2), channel_id=1, source_target_pairs={{0,64},{64,128},{128,192},{192,256},{256,320},{320,384},{384,448},... | collective-permute-start | bytes 1376264 | tf_op jit(solution)/shard_map/ppermute | solution.py:258
  38.7 23.5 %collective-permute-start.7 = (bf16[896,256]{1,0:T(8,128)(2,1)S(1)}, bf16[896,256]{1,0:T(8,128)(2,1)S(1)}, u32[]{:S(2)}, u32[]{:S(2)}) collective-permute-start(bf16[896,256]{1,0:T(8,128)(2,1)S(1)} %collective-permute-done.3.w6), channel_id=1, source_target_pairs={{0,448},{64,0},{128,64},{192,128},{256,192},{320,256},{384,320},{4... | collective-permute-start | bytes 1376264 | tf_op jit(solution)/shard_map/ppermute | solution.py:259
  41.3 49.0 %all-to-all-start = ((bf16[16,112,256]{2,1,0:T(8,128)(2,1)}), bf16[16,112,256]{2,1,0:T(8,128)(2,1)}, u32[]{:S(2)}, u32[]{:S(2)}) async-start(bf16[16,112,256]{2,1,0:T(8,128)(2,1)} %get-tuple-element.39), calls=%async_computation | async-start | bytes 1835008 | tf_op jit(solution)/shard_map/all_to_all | solution.py:256
  54.7 13.5 %collective-permute-start.10 = (bf16[192,1920]{1,0:T(8,128)(2,1)}, bf16[192,1920]{1,0:T(8,128)(2,1)S(1)}, u32[]{:S(2)}, u32[]{:S(2)}) collective-permute-start(bf16[192,1920]{1,0:T(8,128)(2,1)} %collective-permute-done.5.x2), channel_id=1, source_target_pairs={{0,1},{1,0},{2,3},{3,2},{4,5},{5,4},{6,7},{7,6},{8,9},{9,8},{10,11... | collective-permute-start | bytes 2211848 | tf_op jit(solution)/shard_map/ppermute | solution.py:262
  56.7 11.5 %collective-permute-start.9 = (bf16[192,1920]{1,0:T(8,128)(2,1)}, bf16[192,1920]{1,0:T(8,128)(2,1)S(1)}, u32[]{:S(2)}, u32[]{:S(2)}) collective-permute-start(bf16[192,1920]{1,0:T(8,128)(2,1)} %copy-done.5), channel_id=1, source_target_pairs={{0,1},{1,0},{2,3},{3,2},{4,5},{5,4},{6,7},{7,6},{8,9},{9,8},{10,11... | collective-permute-start | bytes 2211848 | tf_op jit(solution)/shard_map/ppermute | solution.py:262
  62.3 18.7 %collective-permute-start.11 = (bf16[192,1920]{1,0:T(8,128)(2,1)}, bf16[192,1920]{1,0:T(8,128)(2,1)S(1)}, u32[]{:S(2)}, u32[]{:S(2)}) collective-permute-start(bf16[192,1920]{1,0:T(8,128)(2,1)} %collective-permute-done.8.x3), channel_id=1, source_target_pairs={{0,1},{1,0},{2,3},{3,2},{4,5},{5,4},{6,7},{7,6},{8,9},{9,8},{10,11... | collective-permute-start | bytes 2211848 | tf_op jit(solution)/shard_map/ppermute | solution.py:262
  65.7 15.2 %collective-permute-start.12 = (bf16[896,256]{1,0:T(8,128)(2,1)S(1)}, bf16[896,256]{1,0:T(8,128)(2,1)S(1)}, u32[]{:S(2)}, u32[]{:S(2)}) collective-permute-start(bf16[896,256]{1,0:T(8,128)(2,1)S(1)} %collective-permute-done.6.w3), channel_id=1, source_target_pairs={{0,64},{64,128},{128,192},{192,256},{256,320},{320,384},{384,448},... | collective-permute-start | bytes 1376264 | tf_op jit(solution)/shard_map/ppermute | solution.py:261
  68.2 12.8 %copy-start.6 = (bf16[192,1920]{1,0:T(8,128)(2,1)}, bf16[192,1920]{1,0:T(8,128)(2,1)S(1)}, u32[]{:S(2)}) copy-start(bf16[192,1920]{1,0:T(8,128)(2,1)S(1)} %collective-permute-done.10.o2) | copy-start | bytes 2211844
  68.2 12.8 %copy-start.7 = (bf16[192,1920]{1,0:T(8,128)(2,1)}, bf16[192,1920]{1,0:T(8,128)(2,1)S(1)}, u32[]{:S(2)}) copy-start(bf16[192,1920]{1,0:T(8,128)(2,1)S(1)} %collective-permute-done.9.o1) | copy-start | bytes 2211844
  81.0 0.9 copy-start.8
  90.3 25.7 %all-to-all-start.1 = ((f32[64,4,192]{2,1,0:T(4,128)}), f32[64,4,192]{2,1,0:T(4,128)S(1)}, u32[]{:S(2)}, u32[]{:S(2)}) async-start(f32[64,4,192]{2,1,0:T(4,128)} %bitcast.1), calls=%async_computation.1 | async-start | bytes 524288 | tf_op jit(solution)/shard_map/all_to_all | solution.py:266
  105.9 3.5 %collective-permute-start.13 = (f32[96,256]{1,0:T(8,128)}, f32[96,256]{1,0:T(8,128)S(1)}, u32[]{:S(2)}, u32[]{:S(2)}) collective-permute-start(f32[96,256]{1,0:T(8,128)} %get-tuple-element.43.mine), channel_id=1, source_target_pairs={{0,1},{1,0},{2,3},{3,2},{4,5},{5,4},{6,7},{7,6},{8,9},{9,8},{10,11... | collective-permute-start | bytes 294920 | tf_op jit(solution)/shard_map/ppermute | solution.py:268
  109.4 6.6 %copy-start.4 = (f32[96,256]{1,0:T(8,128)}, f32[96,256]{1,0:T(8,128)S(1)}, u32[]{:S(2)}) copy-start(f32[96,256]{1,0:T(8,128)S(1)} %collective-permute-done.13.other) | copy-start | bytes 294916
  116.0 0.7 copy-start.3

commit v7 on v5

--- a/solution.py
+++ b/solution.py
@@ -8,7 +8,7 @@
 
 NY, NX, NZ, NC = 8, 4, 8, 2
 NB = NZ * NC
-FAR = NY // 2
+HALF = NY // NC
 EXTRA = 16
 ZC = ("z", "core")
 BF16, F32 = jnp.bfloat16, jnp.float32
@@ -38,25 +38,28 @@
 
 
 def prepare_kernel(grad, gate, up, inp, model, hproj, p1, p2, p3, early, buf, gate_v, up_v, inp_v, gcols, model_v, hproj_v, in_sem, out_sem, side_sem):
-    outs = (p1, p2, p3)
     tok, hid = gate.shape
-    wide = (p1.shape[1] - hid) // NY
     feat = inp.shape[1]
     y, x, blk = here()
+    core = lax.axis_index("core")
+    wide = (p1.shape[1] - hid) // NY
     fills, sends = [], []
-    for s, out in enumerate(outs):
-        at = lax.rem(x + s + 1, NX)
-        fill = [pltpu.make_async_copy(gate, buf.at[s, :, pl.ds(0, hid)], in_sem.at[s, NY])]
-        for i in range(NY):
+    for s, out in ((2, p2), (1, p1), (3, p3)):
+        at = lax.rem(x + s, NX)
+        size = out.shape[1]
+        part = (size - hid) // wide
+        first = core * HALF if part < NY else 0
+        fill = [pltpu.make_async_copy(gate, buf.at[s - 1, :, pl.ds(0, hid)], in_sem.at[s - 1, NY])]
+        for i in range(part):
             fill.append(
                 pltpu.make_async_copy(
-                    grad.at[:, pl.ds(columns(y, i, at, wide), wide)],
-                    buf.at[s, :, pl.ds(hid + i * wide, wide)],
-                    in_sem.at[s, i],
+                    grad.at[:, pl.ds(columns(y, first + i, at, wide), wide)],
+                    buf.at[s - 1, :, pl.ds(hid + i * wide, wide)],
+                    in_sem.at[s - 1, i],
                 )
             )
         fills.append(fill)
-        sends.append(pltpu.make_async_copy(buf.at[s], out, out_sem.at[s]))
+        sends.append(pltpu.make_async_copy(buf.at[s - 1, :, pl.ds(0, size)], out, out_sem.at[s - 1]))
         for c in fill:
             c.start()
     loads = [
@@ -101,10 +104,10 @@
 def prepare(grad, gate, up, inp, model, hproj, wide):
     tok, hid = gate.shape
     feat = inp.shape[1]
-    out = jax.ShapeDtypeStruct((tok, hid + NY * wide), BF16)
+    full, part = [jax.ShapeDtypeStruct((tok, hid + n * wide), BF16) for n in (NY, HALF)]
     return pl.pallas_call(
         prepare_kernel,
-        out_shape=[out] * 3 + [jax.ShapeDtypeStruct((NB, tok // NC + EXTRA, 2 * model.shape[1]), BF16)],
+        out_shape=[full, part, full] + [jax.ShapeDtypeStruct((NB, tok // NC + EXTRA, 2 * model.shape[1]), BF16)],
         in_specs=[HBM] * 6,
         out_specs=[HBM] * 3 + [VMEM],
         scratch_shapes=[
@@ -125,10 +128,14 @@
     )(grad, gate, up, inp, model, hproj)
 
 
-def main_kernel(grad, own, x1, x2, x3, w0, w1, w2, w3, w4, w5, w6, w7, proj, out, g, gate, w, p, g_sem, w_sem):
+def main_kernel(grad, own, x1, x2, x3, o2, w0, w1, w2, w3, w4, w5, w6, w7, proj, out, g, gate, w, p, g_sem, w_sem):
     y, x, _ = here()
+    core = lax.axis_index("core")
     nx, tok, hid = gate.shape
     wide = w0.shape[1]
+    n = HALF * wide
+    near = pl.ds(pl.multiple_of(core * n, n), n)
+    away = pl.ds(pl.multiple_of((1 - core) * n, n), n)
     per = proj.shape[0] // NB
     firsts = []
     for i in range(NY):
@@ -137,13 +144,15 @@
                 grad.at[:, pl.ds(columns(y, i, x, wide), wide)], g.at[0, :, pl.ds(i * wide, wide)], g_sem.at[0, i]
             )
         )
-    for s, got in enumerate((x1, x2, x3)):
-        firsts.append(pltpu.make_async_copy(got.at[:, pl.ds(hid, NY * wide)], g.at[s + 1], g_sem.at[s + 1, 0]))
+    for s, got in ((1, x1), (3, x3)):
+        firsts.append(pltpu.make_async_copy(got.at[:, pl.ds(hid, NY * wide)], g.at[s], g_sem.at[s, 0]))
+    firsts.append(pltpu.make_async_copy(x2.at[:, pl.ds(hid, n)], g.at[2, :, near], g_sem.at[2, 0]))
+    firsts.append(pltpu.make_async_copy(o2.at[:, pl.ds(hid, n)], g.at[2, :, away], g_sem.at[2, 1]))
     for i, src in enumerate((w0, w1, w2, w3, w4, w5, w6, w7)):
         firsts.append(pltpu.make_async_copy(src, w.at[:, pl.ds(i * wide, wide)], w_sem.at[i]))
     seconds = [pltpu.make_async_copy(own, gate.at[0], g_sem.at[0, NY]), pltpu.make_async_copy(proj, p, g_sem.at[1, NY])]
     for s, got in enumerate((x1, x2, x3)):
-        seconds.append(pltpu.make_async_copy(got.at[:, pl.ds(0, hid)], gate.at[s + 1], g_sem.at[s + 1, 1]))
+        seconds.append(pltpu.make_async_copy(got.at[:, pl.ds(0, hid)], gate.at[s + 1], g_sem.at[s + 1, 2]))
     for c in firsts + seconds:
         c.start()
     for c in firsts:
@@ -169,7 +178,7 @@
     return pl.pallas_call(
         main_kernel,
         out_shape=jax.ShapeDtypeStruct((NX, NB, per, tok), F32),
-        in_specs=[HBM] * 14,
+        in_specs=[HBM] * 15,
         out_specs=VMEM,
         scratch_shapes=[
             pltpu.VMEM((NX, tok, NY * wide), BF16),
@@ -179,9 +188,9 @@
             pltpu.SemaphoreType.DMA((NX, NY + 1)),
             pltpu.SemaphoreType.DMA((NY,)),
         ],
-        compiler_params=pltpu.CompilerParams(vmem_limit_bytes=32 << 20),
+        compiler_params=pltpu.CompilerParams(vmem_limit_bytes=50 << 20),
         cost_estimate=pl.CostEstimate(
-            flops=7 * NX * tok * hid * (NY * wide + 128), bytes_accessed=9_000_000, transcendentals=NX * tok * hid
+            flops=8 * NX * tok * hid * (NY * wide + 128), bytes_accessed=9_000_000, transcendentals=NX * tok * hid
         ),
         name="main",
     )(grad, own, *got, *shards, proj)
@@ -248,12 +257,14 @@
     up2 = lax.ppermute(up1, "y", turn(NY, 1))
     dn2 = lax.ppermute(dn1, "y", turn(NY, -1))
     got = lax.all_to_all(early, ZC, 0, 0)
+    up2, dn2, x2 = lax.optimization_barrier((up2, dn2, x2))
     up3 = lax.ppermute(up2, "y", turn(NY, 1))
     dn3 = lax.ppermute(dn2, "y", turn(NY, -1))
-    up3, dn3, x1 = lax.optimization_barrier((up3, dn3, x1))
+    up3, dn3 = lax.optimization_barrier((up3, dn3))
     w4 = lax.ppermute(up3, "y", turn(NY, 1))
-    x2, x3, w4 = lax.optimization_barrier((x2, x3, w4))
-    up_part = main(out_grad, gate_pre, (x1, x2, x3), (down_weight, up1, up2, up3, w4, dn3, dn2, dn1), hproj)
+    o2 = lax.ppermute(x2, "core", turn(NC, 1))
+    o2, x1, x3, w4 = lax.optimization_barrier((o2, x1, x3, w4))
+    up_part = main(out_grad, gate_pre, (x1, x2, x3, o2), (down_weight, up1, up2, up3, w4, dn3, dn2, dn1), hproj)
     up_part, got = lax.optimization_barrier((up_part, got))
     up_side = lax.all_to_all(up_part.reshape((NX * NB,) + up_part.shape[2:]), ("x",) + ZC, 0, 0)
     mine, hid_side = settle(got, up_part.shape[2])

time: 121 us -> 107 us (0.88)
  waiting for transfers between devices: 32.1 us -> 25.5 us
  local copies, waits for them, and re-layouts: 5.1 us -> 0.72 us
  starting transfers between devices: 65.6 us -> 62 us
    ppermute x3, waiting for transfers between devices: 24.4 us -> 0.1 us  [on_device(): lax.ppermute(p, 'x', turn(NX, s + 1))]
    ppermute x1, waiting for transfers between devices: 0.01 us -> 12.7 us  [on_device(): w4 = lax.ppermute(up3, 'y', turn(NY, 1))]
    ppermute x0 -> x1, starting transfers between devices: none -> 7.43 us  [on_device(): o2 = lax.ppermute(x2, 'core', turn(NC, 1))]
    all_to_all x1, starting transfers between devices: 14.5 us -> 9.02 us  [on_device(): lax.all_to_all(up_part.reshape((NX * NB,) + up_part.shape[2:]), ('x',) +...]
    all_to_all x1, starting transfers between devices: 13.3 us -> 8.43 us  [on_device(): got = lax.all_to_all(early, ZC, 0, 0)]
    unnamed x18 -> x12, local copies, waits for them, and re-layouts: 5.1 us -> 0.72 us
    ppermute x1, waiting for transfers between devices: 0.01 us -> 3.19 us  [on_device(): dn2 = lax.ppermute(dn1, 'y', turn(NY, -1))]
    all_to_all x1, waiting for transfers between devices: 0.01 us -> 1.83 us  [on_device(): got = lax.all_to_all(early, ZC, 0, 0)]
  transfers between devices with their start and end apart: 13 -> 14, of which waited for: 4 -> 6; matrix products, arithmetic and copies ran while one was open for 0% -> 0% of each run, Pallas kernels for 12% -> 14%
where the time goes in v7:
time: 107 us; the launch traced here: 106 us
  starting transfers between devices  62 us (58%)
  waiting for transfers between devices  25.5 us (24%)
  Pallas kernels  17.1 us (16%)
    ppermute x1, waiting for transfers between devices, on_device(): w4 = lax.ppermute(up3, 'y', turn(NY, 1))  12.7 us
    ppermute x3, starting transfers between devices, on_device(): lax.ppermute(p, 'x', turn(NX, s + 1))  11.4 us
    all_to_all x1, starting transfers between devices, on_device(): lax.all_to_all(up_part.reshape((NX * NB,) + up_part.shape[2:]), ('x',) +...  9.02 us
    all_to_all x1, starting transfers between devices, on_device(): got = lax.all_to_all(early, ZC, 0, 0)  8.43 us
    pallas_call x1, Pallas kernels, main(): pl.pallas_call(main_kernel, out_shape=jax.ShapeDtypeStruct((NX, NB, per,...  8.36 us
    ppermute x1, starting transfers between devices, on_device(): o2 = lax.ppermute(x2, 'core', turn(NC, 1))  7.43 us
    all_to_all x1, waiting for transfers between devices, on_device(): lax.all_to_all(up_part.reshape((NX * NB,) + up_part.shape[2:]), ('x',) +...  6.58 us
    pallas_call x1, Pallas kernels, prepare(): pl.pallas_call(prepare_kernel, out_shape=[full, part, full] + [jax.ShapeD...  4.89 us
  transfers between devices with their start and end apart: 14, of which 6 were waited for; matrix products, arithmetic and copies ran while one was open for 0% of the time, Pallas kernels for 14%

profile of v7, /device:TPU:1, one launch (start us, length us, event | category | flops | bytes accessed | tf_op | source)
XLA Modules:
  0.0 106.2 jit_solution(6759692558070852498)
XLA Ops:
  0.6 4.0 %collective-permute-start = (bf16[896,256]{1,0:T(8,128)(2,1)}, bf16[896,256]{1,0:T(8,128)(2,1)S(1)}, u32[]{:S(2)}, u32[]{:S(2)}) collective-permute-start(bf16[896,256]{1,0:T(8,128)(2,1)} %w0.1), channel_id=1, source_target_pairs={{0,64},{64,128},{128,192},{192,256},{256,320},{320,384},{384,448},... | collective-permute-start | bytes 1376264 | tf_op jit(solution)/shard_map/ppermute | solution.py:252
  4.7 3.8 %collective-permute-start.1 = (bf16[896,256]{1,0:T(8,128)(2,1)}, bf16[896,256]{1,0:T(8,128)(2,1)S(1)}, u32[]{:S(2)}, u32[]{:S(2)}) collective-permute-start(bf16[896,256]{1,0:T(8,128)(2,1)} %w0.1), channel_id=1, source_target_pairs={{0,448},{64,0},{128,64},{192,128},{256,192},{320,256},{384,320},{4... | collective-permute-start | bytes 1376264 | tf_op jit(solution)/shard_map/ppermute | solution.py:253
  8.5 4.9 %prepare.1 = (bf16[192,2944]{1,0:T(8,128)(2,1)}, bf16[192,1920]{1,0:T(8,128)(2,1)}, bf16[192,2944]{1,0:T(8,128)(2,1)}, bf16[16,112,256]{2,1,0:T(8,128)(2,1)}) custom-call(bf16[192,8192]{1,0:T(8,128)(2,1)} %grad.3, bf16[192,896]{1,0:T(8,128)(2,1)} %own.1, bf16[192,896]{1,0:T(8,128)(2,1)} %up.1, bf16[192,512]{1,0:T(8,128)(2,1)} %inp.1, ...), custom_call_target="tpu_custom_call" | custom-call | flops 80000000 | bytes 8000000 | tf_op jit(solution)/shard_map/prepare/pallas_call | solution.py:108
  13.4 0.0 copy-start
  13.4 0.0 copy-start.1
  13.4 0.0 copy-start.2
  13.4 4.9 %collective-permute-start.4 = (bf16[192,1920]{1,0:T(8,128)(2,1)}, bf16[192,1920]{1,0:T(8,128)(2,1)}, u32[]{:S(2)}, u32[]{:S(2)}) collective-permute-start(bf16[192,1920]{1,0:T(8,128)(2,1)} %get-tuple-element.25), channel_id=1, source_target_pairs={{0,32},{16,48},{32,0},{48,16},{1,33},{17,49},{33,1},{49,17},{2,34}... | collective-permute-start | bytes 2211848 | tf_op jit(solution)/shard_map/ppermute | solution.py:256
  18.3 0.0 collective-permute-done.w1
  18.4 2.7 %collective-permute-start.2 = (bf16[896,256]{1,0:T(8,128)(2,1)S(1)}, bf16[896,256]{1,0:T(8,128)(2,1)S(1)}, u32[]{:S(2)}, u32[]{:S(2)}) collective-permute-start(bf16[896,256]{1,0:T(8,128)(2,1)S(1)} %collective-permute-done.w1), channel_id=1, source_target_pairs={{0,64},{64,128},{128,192},{192,256},{256,320},{320,384},{384,448},... | collective-permute-start | bytes 1376264 | tf_op jit(solution)/shard_map/ppermute | solution.py:257
  21.1 3.8 %collective-permute-start.3 = (bf16[896,256]{1,0:T(8,128)(2,1)S(1)}, bf16[896,256]{1,0:T(8,128)(2,1)S(1)}, u32[]{:S(2)}, u32[]{:S(2)}) collective-permute-start(bf16[896,256]{1,0:T(8,128)(2,1)S(1)} %collective-permute-done.1.w7), channel_id=1, source_target_pairs={{0,448},{64,0},{128,64},{192,128},{256,192},{320,256},{384,320},{4... | collective-permute-start | bytes 1376264 | tf_op jit(solution)/shard_map/ppermute | solution.py:258
  24.9 3.4 %collective-permute-start.6 = (bf16[192,2944]{1,0:T(8,128)(2,1)}, bf16[192,2944]{1,0:T(8,128)(2,1)}, u32[]{:S(2)}, u32[]{:S(2)}) collective-permute-start(bf16[192,2944]{1,0:T(8,128)(2,1)} %get-tuple-element.27), channel_id=1, source_target_pairs={{0,16},{16,32},{32,48},{48,0},{1,17},{17,33},{33,49},{49,1},{2,18}... | collective-permute-start | bytes 3391496 | tf_op jit(solution)/shard_map/ppermute | solution.py:256
  28.2 3.2 %collective-permute-start.7 = (bf16[192,2944]{1,0:T(8,128)(2,1)}, bf16[192,2944]{1,0:T(8,128)(2,1)}, u32[]{:S(2)}, u32[]{:S(2)}) collective-permute-start(bf16[192,2944]{1,0:T(8,128)(2,1)} %get-tuple-element.28), channel_id=1, source_target_pairs={{0,48},{16,0},{32,16},{48,32},{1,49},{17,1},{33,17},{49,33},{2,50}... | collective-permute-start | bytes 3391496 | tf_op jit(solution)/shard_map/ppermute | solution.py:256
  31.4 0.1 collective-permute-done.4.x2
  31.5 0.0 collective-permute-done.2.w2
  31.5 3.2 %collective-permute-done.3.w6 = bf16[896,256]{1,0:T(8,128)(2,1)S(1)} collective-permute-done((bf16[896,256]{1,0:T(8,128)(2,1)S(1)}, bf16[896,256]{1,0:T(8,128)(2,1)S(1)}, u32[]{:S(2)}, u32[]{:S(2)}) %collective-permute-start.3) | collective-permute-done | bytes 458784 | tf_op jit(solution)/shard_map/ppermute | solution.py:258
  34.7 3.9 %collective-permute-start.8 = (bf16[896,256]{1,0:T(8,128)(2,1)S(1)}, bf16[896,256]{1,0:T(8,128)(2,1)S(1)}, u32[]{:S(2)}, u32[]{:S(2)}) collective-permute-start(bf16[896,256]{1,0:T(8,128)(2,1)S(1)} %collective-permute-done.2.w2), channel_id=1, source_target_pairs={{0,64},{64,128},{128,192},{192,256},{256,320},{320,384},{384,448},... | collective-permute-start | bytes 1376264 | tf_op jit(solution)/shard_map/ppermute | solution.py:261
  38.7 2.6 %collective-permute-start.9 = (bf16[896,256]{1,0:T(8,128)(2,1)S(1)}, bf16[896,256]{1,0:T(8,128)(2,1)S(1)}, u32[]{:S(2)}, u32[]{:S(2)}) collective-permute-start(bf16[896,256]{1,0:T(8,128)(2,1)S(1)} %collective-permute-done.3.w6), channel_id=1, source_target_pairs={{0,448},{64,0},{128,64},{192,128},{256,192},{320,256},{384,320},{4... | collective-permute-start | bytes 1376264 | tf_op jit(solution)/shard_map/ppermute | solution.py:262
  41.2 7.4 %collective-permute-start.5 = (bf16[192,1920]{1,0:T(8,128)(2,1)}, bf16[192,1920]{1,0:T(8,128)(2,1)}, u32[]{:S(2)}, u32[]{:S(2)}) collective-permute-start(bf16[192,1920]{1,0:T(8,128)(2,1)} %collective-permute-done.4.x2), channel_id=1, source_target_pairs={{0,1},{1,0},{2,3},{3,2},{4,5},{5,4},{6,7},{7,6},{8,9},{9,8},{10,11... | collective-permute-start | bytes 2211848 | tf_op jit(solution)/shard_map/ppermute | solution.py:265
  48.7 8.4 %all-to-all-start = ((bf16[16,112,256]{2,1,0:T(8,128)(2,1)}), bf16[16,112,256]{2,1,0:T(8,128)(2,1)}, u32[]{:S(2)}, u32[]{:S(2)}) async-start(bf16[16,112,256]{2,1,0:T(8,128)(2,1)} %get-tuple-element.37), calls=%async_computation | async-start | bytes 1835008 | tf_op jit(solution)/shard_map/all_to_all | solution.py:259
  57.1 0.0 collective-permute-done.9.w5
  57.1 2.5 %collective-permute-start.10 = (bf16[896,256]{1,0:T(8,128)(2,1)S(1)}, bf16[896,256]{1,0:T(8,128)(2,1)S(1)}, u32[]{:S(2)}, u32[]{:S(2)}) collective-permute-start(bf16[896,256]{1,0:T(8,128)(2,1)S(1)} %collective-permute-done.8.w3), channel_id=1, source_target_pairs={{0,64},{64,128},{128,192},{192,256},{256,320},{320,384},{384,448},... | collective-permute-start | bytes 1376264 | tf_op jit(solution)/shard_map/ppermute | solution.py:264
  59.6 0.0 collective-permute-done.6.x1
  59.6 12.7 %collective-permute-done.10.w4 = bf16[896,256]{1,0:T(8,128)(2,1)S(1)} collective-permute-done((bf16[896,256]{1,0:T(8,128)(2,1)S(1)}, bf16[896,256]{1,0:T(8,128)(2,1)S(1)}, u32[]{:S(2)}, u32[]{:S(2)}) %collective-permute-start.10) | collective-permute-done | bytes 458784 | tf_op jit(solution)/shard_map/ppermute | solution.py:264
  72.3 8.4 %main.1 = f32[4,16,4,192]{3,2,1,0:T(4,128)} custom-call(bf16[192,8192]{1,0:T(8,128)(2,1)} %grad.3, bf16[192,896]{1,0:T(8,128)(2,1)S(1)} %copy-done, bf16[192,2944]{1,0:T(8,128)(2,1)} %collective-permute-done.6.x1, bf16[192,1920]{1,0:T(8,128)(2,1)} %collective-permute-done.4.x2, bf16[192,2944]{1,0:T(8,128)(2,1)} %collective-permute-done.7.x3, ...), custom_call_target="tpu_custom_call" | custom-call | flops 11978932224 | bytes 9000000 | tf_op jit(solution)/shard_map/main/pallas_call | solution.py:178
  80.7 1.8 %all-to-all-done.got = bf16[16,112,256]{2,1,0:T(8,128)(2,1)} async-done(((bf16[16,112,256]{2,1,0:T(8,128)(2,1)}), bf16[16,112,256]{2,1,0:T(8,128)(2,1)}, u32[]{:S(2)}, u32[]{:S(2)}) %all-to-all-start) | async-done | bytes 917536 | tf_op jit(solution)/shard_map/all_to_all | solution.py:259
  82.5 9.0 %all-to-all-start.1 = ((f32[64,4,192]{2,1,0:T(4,128)}), f32[64,4,192]{2,1,0:T(4,128)S(1)}, u32[]{:S(2)}, u32[]{:S(2)}) async-start(f32[64,4,192]{2,1,0:T(4,128)} %bitcast.1), calls=%async_computation.1 | async-start | bytes 524288 | tf_op jit(solution)/shard_map/all_to_all | solution.py:269
  91.5 1.9 %settle.1 = (f32[96,256]{1,0:T(8,128)}, f32[4,192]{1,0:T(4,128)}) custom-call(bf16[16,112,256]{2,1,0:T(8,128)(2,1)} %all-to-all-done.got), custom_call_target="tpu_custom_call" | custom-call | tf_op jit(solution)/shard_map/settle/pallas_call | solution.py:221
  93.5 2.4 %collective-permute-start.11 = (f32[96,256]{1,0:T(8,128)}, f32[96,256]{1,0:T(8,128)S(1)}, u32[]{:S(2)}, u32[]{:S(2)}) collective-permute-start(f32[96,256]{1,0:T(8,128)} %get-tuple-element.41.mine), channel_id=1, source_target_pairs={{0,1},{1,0},{2,3},{3,2},{4,5},{5,4},{6,7},{7,6},{8,9},{9,8},{10,11... | collective-permute-start | bytes 294920 | tf_op jit(solution)/shard_map/ppermute | solution.py:271
  95.8 1.1 %collective-permute-done.11.other = f32[96,256]{1,0:T(8,128)S(1)} collective-permute-done((f32[96,256]{1,0:T(8,128)}, f32[96,256]{1,0:T(8,128)S(1)}, u32[]{:S(2)}, u32[]{:S(2)}) %collective-permute-start.11) | collective-permute-done | bytes 98336 | tf_op jit(solution)/shard_map/ppermute | solution.py:271
  97.0 6.6 %all-to-all-done.1.got = f32[64,4,192]{2,1,0:T(4,128)S(1)} async-done(((f32[64,4,192]{2,1,0:T(4,128)}), f32[64,4,192]{2,1,0:T(4,128)S(1)}, u32[]{:S(2)}, u32[]{:S(2)}) %all-to-all-start.1) | async-done | bytes 196640 | tf_op jit(solution)/shard_map/all_to_all | solution.py:269
  103.5 0.7 copy-done.3
  104.2 1.9 %finish.1 = (f32[2,512]{1,0:T(2,128)}, f32[2,512]{1,0:T(2,128)}) custom-call(f32[64,4,192]{2,1,0:T(4,128)} %copy-done.3, f32[4,192]{1,0:T(4,128)} %get-tuple-element.40.hid_side, f32[96,256]{1,0:T(8,128)} %get-tuple-element.41.mine, f32[96,256]{1,0:T(8,128)} %copy-done.4, s32[1,192]{1,0:T(1,128)} %ids.1), custom_call_target="tpu_custom_call" | custom-call | tf_op jit(solution)/shard_map/finish/pallas_call | solution.py:245
  (12 shorter events, 0.0 us)
Async XLA Ops:
  0.6 17.7 %collective-permute-start = (bf16[896,256]{1,0:T(8,128)(2,1)}, bf16[896,256]{1,0:T(8,128)(2,1)S(1)}, u32[]{:S(2)}, u32[]{:S(2)}) collective-permute-start(bf16[896,256]{1,0:T(8,128)(2,1)} %w0.1), channel_id=1, source_target_pairs={{0,64},{64,128},{128,192},{192,256},{256,320},{320,384},{384,448},... | collective-permute-start | bytes 1376264 | tf_op jit(solution)/shard_map/ppermute | solution.py:252
  4.7 13.7 %collective-permute-start.1 = (bf16[896,256]{1,0:T(8,128)(2,1)}, bf16[896,256]{1,0:T(8,128)(2,1)S(1)}, u32[]{:S(2)}, u32[]{:S(2)}) collective-permute-start(bf16[896,256]{1,0:T(8,128)(2,1)} %w0.1), channel_id=1, source_target_pairs={{0,448},{64,0},{128,64},{192,128},{256,192},{320,256},{384,320},{4... | collective-permute-start | bytes 1376264 | tf_op jit(solution)/shard_map/ppermute | solution.py:253
  13.4 58.9 %copy-start = (bf16[192,896]{1,0:T(8,128)(2,1)S(1)}, bf16[192,896]{1,0:T(8,128)(2,1)}, u32[]{:S(2)}) copy-start(bf16[192,896]{1,0:T(8,128)(2,1)} %own.1) | copy-start | bytes 1032196
  13.4 58.9 %copy-start.1 = (bf16[896,64]{0,1:T(8,128)(2,1)S(1)}, bf16[896,64]{0,1:T(8,128)(2,1)}, u32[]{:S(2)}) copy-start(bf16[896,64]{0,1:T(8,128)(2,1)} %param.13) | copy-start | bytes 344068
  13.4 58.9 %copy-start.2 = (bf16[896,256]{1,0:T(8,128)(2,1)S(1)}, bf16[896,256]{1,0:T(8,128)(2,1)}, u32[]{:S(2)}) copy-start(bf16[896,256]{1,0:T(8,128)(2,1)} %w0.1) | copy-start | bytes 1376260
  13.4 18.1 %collective-permute-start.4 = (bf16[192,1920]{1,0:T(8,128)(2,1)}, bf16[192,1920]{1,0:T(8,128)(2,1)}, u32[]{:S(2)}, u32[]{:S(2)}) collective-permute-start(bf16[192,1920]{1,0:T(8,128)(2,1)} %get-tuple-element.25), channel_id=1, source_target_pairs={{0,32},{16,48},{32,0},{48,16},{1,33},{17,49},{33,1},{49,17},{2,34}... | collective-permute-start | bytes 2211848 | tf_op jit(solution)/shard_map/ppermute | solution.py:256
  18.4 16.4 %copy-start.5 = (bf16[896,256]{1,0:T(8,128)(2,1)}, bf16[896,256]{1,0:T(8,128)(2,1)S(1)}, u32[]{:S(2)}) copy-start(bf16[896,256]{1,0:T(8,128)(2,1)S(1)} %collective-permute-done.1.w7) | copy-start | bytes 1376260
  18.4 13.2 %collective-permute-start.2 = (bf16[896,256]{1,0:T(8,128)(2,1)S(1)}, bf16[896,256]{1,0:T(8,128)(2,1)S(1)}, u32[]{:S(2)}, u32[]{:S(2)}) collective-permute-start(bf16[896,256]{1,0:T(8,128)(2,1)S(1)} %collective-permute-done.w1), channel_id=1, source_target_pairs={{0,64},{64,128},{128,192},{192,256},{256,320},{320,384},{384,448},... | collective-permute-start | bytes 1376264 | tf_op jit(solution)/shard_map/ppermute | solution.py:257
  21.1 13.7 %collective-permute-start.3 = (bf16[896,256]{1,0:T(8,128)(2,1)S(1)}, bf16[896,256]{1,0:T(8,128)(2,1)S(1)}, u32[]{:S(2)}, u32[]{:S(2)}) collective-permute-start(bf16[896,256]{1,0:T(8,128)(2,1)S(1)} %collective-permute-done.1.w7), channel_id=1, source_target_pairs={{0,448},{64,0},{128,64},{192,128},{256,192},{320,256},{384,320},{4... | collective-permute-start | bytes 1376264 | tf_op jit(solution)/shard_map/ppermute | solution.py:258
  24.9 34.7 %collective-permute-start.6 = (bf16[192,2944]{1,0:T(8,128)(2,1)}, bf16[192,2944]{1,0:T(8,128)(2,1)}, u32[]{:S(2)}, u32[]{:S(2)}) collective-permute-start(bf16[192,2944]{1,0:T(8,128)(2,1)} %get-tuple-element.27), channel_id=1, source_target_pairs={{0,16},{16,32},{32,48},{48,0},{1,17},{17,33},{33,49},{49,1},{2,18}... | collective-permute-start | bytes 3391496 | tf_op jit(solution)/shard_map/ppermute | solution.py:256
  28.2 31.4 %collective-permute-start.7 = (bf16[192,2944]{1,0:T(8,128)(2,1)}, bf16[192,2944]{1,0:T(8,128)(2,1)}, u32[]{:S(2)}, u32[]{:S(2)}) collective-permute-start(bf16[192,2944]{1,0:T(8,128)(2,1)} %get-tuple-element.28), channel_id=1, source_target_pairs={{0,48},{16,0},{32,16},{48,32},{1,49},{17,1},{33,17},{49,33},{2,50}... | collective-permute-start | bytes 3391496 | tf_op jit(solution)/shard_map/ppermute | solution.py:256
  34.7 22.4 %collective-permute-start.8 = (bf16[896,256]{1,0:T(8,128)(2,1)S(1)}, bf16[896,256]{1,0:T(8,128)(2,1)S(1)}, u32[]{:S(2)}, u32[]{:S(2)}) collective-permute-start(bf16[896,256]{1,0:T(8,128)(2,1)S(1)} %collective-permute-done.2.w2), channel_id=1, source_target_pairs={{0,64},{64,128},{128,192},{192,256},{256,320},{320,384},{384,448},... | collective-permute-start | bytes 1376264 | tf_op jit(solution)/shard_map/ppermute | solution.py:261
  38.7 18.4 %collective-permute-start.9 = (bf16[896,256]{1,0:T(8,128)(2,1)S(1)}, bf16[896,256]{1,0:T(8,128)(2,1)S(1)}, u32[]{:S(2)}, u32[]{:S(2)}) collective-permute-start(bf16[896,256]{1,0:T(8,128)(2,1)S(1)} %collective-permute-done.3.w6), channel_id=1, source_target_pairs={{0,448},{64,0},{128,64},{192,128},{256,192},{320,256},{384,320},{4... | collective-permute-start | bytes 1376264 | tf_op jit(solution)/shard_map/ppermute | solution.py:262
  41.2 18.4 %collective-permute-start.5 = (bf16[192,1920]{1,0:T(8,128)(2,1)}, bf16[192,1920]{1,0:T(8,128)(2,1)}, u32[]{:S(2)}, u32[]{:S(2)}) collective-permute-start(bf16[192,1920]{1,0:T(8,128)(2,1)} %collective-permute-done.4.x2), channel_id=1, source_target_pairs={{0,1},{1,0},{2,3},{3,2},{4,5},{5,4},{6,7},{7,6},{8,9},{9,8},{10,11... | collective-permute-start | bytes 2211848 | tf_op jit(solution)/shard_map/ppermute | solution.py:265
  48.7 33.8 %all-to-all-start = ((bf16[16,112,256]{2,1,0:T(8,128)(2,1)}), bf16[16,112,256]{2,1,0:T(8,128)(2,1)}, u32[]{:S(2)}, u32[]{:S(2)}) async-start(bf16[16,112,256]{2,1,0:T(8,128)(2,1)} %get-tuple-element.37), calls=%async_computation | async-start | bytes 1835008 | tf_op jit(solution)/shard_map/all_to_all | solution.py:259
  57.1 15.2 %collective-permute-start.10 = (bf16[896,256]{1,0:T(8,128)(2,1)S(1)}, bf16[896,256]{1,0:T(8,128)(2,1)S(1)}, u32[]{:S(2)}, u32[]{:S(2)}) collective-permute-start(bf16[896,256]{1,0:T(8,128)(2,1)S(1)} %collective-permute-done.8.w3), channel_id=1, source_target_pairs={{0,64},{64,128},{128,192},{192,256},{256,320},{320,384},{384,448},... | collective-permute-start | bytes 1376264 | tf_op jit(solution)/shard_map/ppermute | solution.py:264
  82.5 21.0 %all-to-all-start.1 = ((f32[64,4,192]{2,1,0:T(4,128)}), f32[64,4,192]{2,1,0:T(4,128)S(1)}, u32[]{:S(2)}, u32[]{:S(2)}) async-start(f32[64,4,192]{2,1,0:T(4,128)} %bitcast.1), calls=%async_computation.1 | async-start | bytes 524288 | tf_op jit(solution)/shard_map/all_to_all | solution.py:269
  93.5 3.5 %collective-permute-start.11 = (f32[96,256]{1,0:T(8,128)}, f32[96,256]{1,0:T(8,128)S(1)}, u32[]{:S(2)}, u32[]{:S(2)}) collective-permute-start(f32[96,256]{1,0:T(8,128)} %get-tuple-element.41.mine), channel_id=1, source_target_pairs={{0,1},{1,0},{2,3},{3,2},{4,5},{5,4},{6,7},{7,6},{8,9},{9,8},{10,11... | collective-permute-start | bytes 294920 | tf_op jit(solution)/shard_map/ppermute | solution.py:271
  97.0 6.6 %copy-start.4 = (f32[96,256]{1,0:T(8,128)}, f32[96,256]{1,0:T(8,128)S(1)}, u32[]{:S(2)}) copy-start(f32[96,256]{1,0:T(8,128)S(1)} %collective-permute-done.11.other) | copy-start | bytes 294916
  103.5 0.7 copy-start.3

commit v8 on v7

--- a/solution.py
+++ b/solution.py
@@ -128,72 +128,128 @@
     )(grad, gate, up, inp, model, hproj)
 
 
-def main_kernel(grad, own, x1, x2, x3, o2, w0, w1, w2, w3, w4, w5, w6, w7, proj, out, g, gate, w, p, g_sem, w_sem):
+def near_kernel(grad, own, x1, x2, x3, o2, w0, w1, w2, w3, w5, w6, w7, acc, last, gate, g, w, g_sem, w_sem, gate_sem):
     y, x, _ = here()
     core = lax.axis_index("core")
-    nx, tok, hid = gate.shape
+    nx, tok, hid = acc.shape
     wide = w0.shape[1]
     n = HALF * wide
     near = pl.ds(pl.multiple_of(core * n, n), n)
     away = pl.ds(pl.multiple_of((1 - core) * n, n), n)
-    per = proj.shape[0] // NB
-    firsts = []
+    copies = []
     for i in range(NY):
-        firsts.append(
+        copies.append(
             pltpu.make_async_copy(
                 grad.at[:, pl.ds(columns(y, i, x, wide), wide)], g.at[0, :, pl.ds(i * wide, wide)], g_sem.at[0, i]
             )
         )
     for s, got in ((1, x1), (3, x3)):
-        firsts.append(pltpu.make_async_copy(got.at[:, pl.ds(hid, NY * wide)], g.at[s], g_sem.at[s, 0]))
-    firsts.append(pltpu.make_async_copy(x2.at[:, pl.ds(hid, n)], g.at[2, :, near], g_sem.at[2, 0]))
-    firsts.append(pltpu.make_async_copy(o2.at[:, pl.ds(hid, n)], g.at[2, :, away], g_sem.at[2, 1]))
-    for i, src in enumerate((w0, w1, w2, w3, w4, w5, w6, w7)):
-        firsts.append(pltpu.make_async_copy(src, w.at[:, pl.ds(i * wide, wide)], w_sem.at[i]))
-    seconds = [pltpu.make_async_copy(own, gate.at[0], g_sem.at[0, NY]), pltpu.make_async_copy(proj, p, g_sem.at[1, NY])]
+        copies.append(pltpu.make_async_copy(got.at[:, pl.ds(hid, NY * wide)], g.at[s], g_sem.at[s, 0]))
+    copies.append(pltpu.make_async_copy(x2.at[:, pl.ds(hid, n)], g.at[2, :, near], g_sem.at[2, 0]))
+    copies.append(pltpu.make_async_copy(o2.at[:, pl.ds(hid, n)], g.at[2, :, away], g_sem.at[2, 1]))
+    for i, src in enumerate((w0, w1, w2, w3, w5, w6, w7)):
+        copies.append(pltpu.make_async_copy(src, w.at[:, pl.ds(i * wide, wide)], w_sem.at[i]))
+    gates = [pltpu.make_async_copy(own, gate.at[0], gate_sem.at[0])]
     for s, got in enumerate((x1, x2, x3)):
-        seconds.append(pltpu.make_async_copy(got.at[:, pl.ds(0, hid)], gate.at[s + 1], g_sem.at[s + 1, 2]))
-    for c in firsts + seconds:
+        gates.append(pltpu.make_async_copy(got.at[:, pl.ds(0, hid)], gate.at[s + 1], gate_sem.at[s + 1]))
+    for c in copies + gates:
         c.start()
-    for c in firsts:
-        c.wait()
-    gh = dot_nt(g[...].reshape(nx * tok, NY * wide), w[...])
-    for c in seconds:
-        c.wait()
-    gu = gh * silu(gate[...].reshape(nx * tok, hid).astype(F32))
-    hi = gu.astype(BF16)
-    lo = (gu - hi.astype(F32)).astype(BF16)
+    for c in copies:
+        c.wait()
+    low = g[:, :, 0:n].reshape(nx * tok, n)
+    high = g[:, :, n + wide :].reshape(nx * tok, n - wide)
+    gh = dot_nt(low, w[:, 0:n]) + dot_nt(high, w[:, n:])
+    acc[...] = gh.reshape(nx, tok, hid)
+    last[...] = g[:, :, n : n + wide]
+    for c in gates:
+        c.wait()
+
+
+def near(grad, own, got, shards):
+    tok = grad.shape[0]
+    hid, wide = shards[0].shape
+    k = (NY - 1) * wide
+    return pl.pallas_call(
+        near_kernel,
+        out_shape=[
+            jax.ShapeDtypeStruct((NX, tok, hid), F32),
+            jax.ShapeDtypeStruct((NX, tok, wide), BF16),
+            jax.ShapeDtypeStruct((NX, tok, hid), BF16),
+        ],
+        in_specs=[HBM] * 13,
+        out_specs=[VMEM] * 3,
+        scratch_shapes=[
+            pltpu.VMEM((NX, tok, NY * wide), BF16),
+            pltpu.VMEM((hid, k), BF16),
+            pltpu.SemaphoreType.DMA((NX, NY)),
+            pltpu.SemaphoreType.DMA((NY - 1,)),
+            pltpu.SemaphoreType.DMA((NX,)),
+        ],
+        compiler_params=pltpu.CompilerParams(vmem_limit_bytes=50 << 20),
+        cost_estimate=pl.CostEstimate(flops=1_000_000, bytes_accessed=100_000, transcendentals=0),
+        name="near",
+    )(grad, own, *got, *shards)
+
+
+def far_kernel(acc, last, gates, w4, proj, out, a_v, g, gate, w, p, sems):
+    _, x, _ = here()
+    nx, tok, hid = acc.shape
+    per = proj.shape[0] // NB
+    heads = [
+        pltpu.make_async_copy(w4, w, sems.at[nx, 0]),
+        pltpu.make_async_copy(last, g, sems.at[nx, 1]),
+        pltpu.make_async_copy(proj, p, sems.at[nx, 2]),
+    ]
+    waits = []
     for s in range(nx):
-        rows = slice(s * tok, (s + 1) * tok)
-        total = dot_nt(p[...], hi[rows]) + dot_nt(p[...], lo[rows])
+        waits.append(
+            [
+                pltpu.make_async_copy(acc.at[s], a_v.at[s], sems.at[s, 0]),
+                pltpu.make_async_copy(gates.at[s], gate.at[s], sems.at[s, 1]),
+            ]
+        )
+    for c in heads:
+        c.start()
+    for pair in waits:
+        for c in pair:
+            c.start()
+    for c in heads:
+        c.wait()
+    for s in range(nx):
+        for c in waits[s]:
+            c.wait()
+        gu = (a_v[s] + dot_nt(g[s], w[...])) * silu(gate[s].astype(F32))
+        hi = gu.astype(BF16)
+        lo = (gu - hi.astype(F32)).astype(BF16)
+        total = dot_nt(p[...], hi) + dot_nt(p[...], lo)
         to = lax.rem(x - s + nx, nx)
         for b in range(NB):
             out[to, b] = total[b * per : (b + 1) * per, :]
 
 
-def main(grad, own, got, shards, proj):
-    tok = grad.shape[0]
-    hid, wide = shards[0].shape
+def far(acc, last, gates, w4, proj):
+    nx, tok, hid = acc.shape
+    wide = w4.shape[1]
     per = proj.shape[0] // NB
     return pl.pallas_call(
-        main_kernel,
-        out_shape=jax.ShapeDtypeStruct((NX, NB, per, tok), F32),
-        in_specs=[HBM] * 15,
+        far_kernel,
+        out_shape=jax.ShapeDtypeStruct((nx, NB, per, tok), F32),
+        in_specs=[HBM] * 5,
         out_specs=VMEM,
         scratch_shapes=[
-            pltpu.VMEM((NX, tok, NY * wide), BF16),
-            pltpu.VMEM((NX, tok, hid), BF16),
-            pltpu.VMEM((hid, NY * wide), BF16),
+            pltpu.VMEM((nx, tok, hid), F32),
+            pltpu.VMEM((nx, tok, wide), BF16),
+            pltpu.VMEM((nx, tok, hid), BF16),
+            pltpu.VMEM((hid, wide), BF16),
             pltpu.VMEM(proj.shape, BF16),
-            pltpu.SemaphoreType.DMA((NX, NY + 1)),
-            pltpu.SemaphoreType.DMA((NY,)),
+            pltpu.SemaphoreType.DMA((nx + 1, 3)),
         ],
         compiler_params=pltpu.CompilerParams(vmem_limit_bytes=50 << 20),
         cost_estimate=pl.CostEstimate(
-            flops=8 * NX * tok * hid * (NY * wide + 128), bytes_accessed=9_000_000, transcendentals=NX * tok * hid
+            flops=7 * nx * tok * hid * (NY * wide + 128), bytes_accessed=9_000_000, transcendentals=nx * tok * hid
         ),
-        name="main",
-    )(grad, own, *got, *shards, proj)
+        name="far",
+    )(acc, last, gates, w4, proj)
 
 
 def score(left, right, which, out):
@@ -263,8 +319,9 @@
     up3, dn3 = lax.optimization_barrier((up3, dn3))
     w4 = lax.ppermute(up3, "y", turn(NY, 1))
     o2 = lax.ppermute(x2, "core", turn(NC, 1))
-    o2, x1, x3, w4 = lax.optimization_barrier((o2, x1, x3, w4))
-    up_part = main(out_grad, gate_pre, (x1, x2, x3, o2), (down_weight, up1, up2, up3, w4, dn3, dn2, dn1), hproj)
+    o2, x1, x3 = lax.optimization_barrier((o2, x1, x3))
+    acc, last, gates = near(out_grad, gate_pre, (x1, x2, x3, o2), (down_weight, up1, up2, up3, dn3, dn2, dn1))
+    up_part = far(acc, last, gates, w4, hproj)
     up_part, got = lax.optimization_barrier((up_part, got))
     up_side = lax.all_to_all(up_part.reshape((NX * NB,) + up_part.shape[2:]), ("x",) + ZC, 0, 0)
     mine, hid_side = settle(got, up_part.shape[2])

time: 107 us -> 107 us (level)
  waiting for transfers between devices: 25.5 us -> 16.7 us
  Pallas kernels: 17.1 us -> 21.8 us
  local copies, waits for them, and re-layouts: 0.72 us -> 2.94 us
  starting transfers between devices: 62 us -> 63.7 us
    ppermute x1, waiting for transfers between devices: 12.7 us -> 4.46 us  [on_device(): w4 = lax.ppermute(up3, 'y', turn(NY, 1))]
    all_to_all x1, starting transfers between devices: 8.43 us -> 14.7 us  [on_device(): got = lax.all_to_all(early, ZC, 0, 0)]
    ppermute x1, starting transfers between devices: 7.43 us -> 2.19 us  [on_device(): o2 = lax.ppermute(x2, 'core', turn(NC, 1))]
    pallas_call x1 -> x2, Pallas kernels: 8.36 us -> 13.1 us  [the longest x1 7.37 us: near(): pl.pallas_call(near_kernel, out_shape=[jax.ShapeDtypeStruct((NX, tok, hid...]
    unnamed x12 -> x16, local copies, waits for them, and re-layouts: 0.72 us -> 2.94 us
    all_to_all x1, starting transfers between devices: 9.02 us -> 10.2 us  [on_device(): lax.all_to_all(up_part.reshape((NX * NB,) + up_part.shape[2:]), ('x',) +...]
  transfers between devices with their start and end apart: 14 -> 14, of which waited for: 6 -> 6; matrix products, arithmetic and copies ran while one was open for 0% -> 0% of each run, Pallas kernels for 14% -> 19%
where the time goes in v8:
time: 107 us; the launch traced here: 106 us
  starting transfers between devices  63.7 us (60%)
  Pallas kernels  21.8 us (20%)
  waiting for transfers between devices  16.7 us (16%)
  local copies, waits for them, and re-layouts  2.94 us (3%)
    all_to_all x1, starting transfers between devices, on_device(): got = lax.all_to_all(early, ZC, 0, 0)  14.7 us
    ppermute x3, starting transfers between devices, on_device(): lax.ppermute(p, 'x', turn(NX, s + 1))  11.5 us
    all_to_all x1, starting transfers between devices, on_device(): lax.all_to_all(up_part.reshape((NX * NB,) + up_part.shape[2:]), ('x',) +...  10.2 us
    pallas_call x1, Pallas kernels, near(): pl.pallas_call(near_kernel, out_shape=[jax.ShapeDtypeStruct((NX, tok, hid...  7.37 us
    all_to_all x1, waiting for transfers between devices, on_device(): lax.all_to_all(up_part.reshape((NX * NB,) + up_part.shape[2:]), ('x',) +...  6.57 us
    pallas_call x1, Pallas kernels, far(): pl.pallas_call(far_kernel, out_shape=jax.ShapeDtypeStruct((nx, NB, per, t...  5.76 us
    pallas_call x1, Pallas kernels, prepare(): pl.pallas_call(prepare_kernel, out_shape=[full, part, full] + [jax.ShapeD...  4.83 us
    ppermute x1, waiting for transfers between devices, on_device(): w4 = lax.ppermute(up3, 'y', turn(NY, 1))  4.46 us
  transfers between devices with their start and end apart: 14, of which 6 were waited for; matrix products, arithmetic and copies ran while one was open for 0% of the time, Pallas kernels for 19%

profile of v8, /device:TPU:1, one launch (start us, length us, event | category | flops | bytes accessed | tf_op | source)
XLA Modules:
  0.0 106.0 jit_solution(3405391930097769344)
XLA Ops:
  0.6 4.0 %collective-permute-start = (bf16[896,256]{1,0:T(8,128)(2,1)}, bf16[896,256]{1,0:T(8,128)(2,1)S(1)}, u32[]{:S(2)}, u32[]{:S(2)}) collective-permute-start(bf16[896,256]{1,0:T(8,128)(2,1)} %w0.1), channel_id=1, source_target_pairs={{0,64},{64,128},{128,192},{192,256},{256,320},{320,384},{384,448},... | collective-permute-start | bytes 1376264 | tf_op jit(solution)/shard_map/ppermute | solution.py:308
  4.7 3.8 %collective-permute-start.1 = (bf16[896,256]{1,0:T(8,128)(2,1)}, bf16[896,256]{1,0:T(8,128)(2,1)S(1)}, u32[]{:S(2)}, u32[]{:S(2)}) collective-permute-start(bf16[896,256]{1,0:T(8,128)(2,1)} %w0.1), channel_id=1, source_target_pairs={{0,448},{64,0},{128,64},{192,128},{256,192},{320,256},{384,320},{4... | collective-permute-start | bytes 1376264 | tf_op jit(solution)/shard_map/ppermute | solution.py:309
  8.5 4.8 %prepare.1 = (bf16[192,2944]{1,0:T(8,128)(2,1)}, bf16[192,1920]{1,0:T(8,128)(2,1)}, bf16[192,2944]{1,0:T(8,128)(2,1)}, bf16[16,112,256]{2,1,0:T(8,128)(2,1)}) custom-call(bf16[192,8192]{1,0:T(8,128)(2,1)} %grad.3, bf16[192,896]{1,0:T(8,128)(2,1)} %own.1, bf16[192,896]{1,0:T(8,128)(2,1)} %up.1, bf16[192,512]{1,0:T(8,128)(2,1)} %inp.1, ...), custom_call_target="tpu_custom_call" | custom-call | flops 80000000 | bytes 8000000 | tf_op jit(solution)/shard_map/prepare/pallas_call | solution.py:108
  13.3 0.0 copy-start
  13.3 0.0 copy-start.1
  13.4 4.9 %collective-permute-start.4 = (bf16[192,1920]{1,0:T(8,128)(2,1)}, bf16[192,1920]{1,0:T(8,128)(2,1)S(1)}, u32[]{:S(2)}, u32[]{:S(2)}) collective-permute-start(bf16[192,1920]{1,0:T(8,128)(2,1)} %get-tuple-element.27), channel_id=1, source_target_pairs={{0,32},{16,48},{32,0},{48,16},{1,33},{17,49},{33,1},{49,17},{2,34}... | collective-permute-start | bytes 2211848 | tf_op jit(solution)/shard_map/ppermute | solution.py:312
  18.3 0.0 collective-permute-done.w1
  18.3 2.8 %collective-permute-start.2 = (bf16[896,256]{1,0:T(8,128)(2,1)S(1)}, bf16[896,256]{1,0:T(8,128)(2,1)S(1)}, u32[]{:S(2)}, u32[]{:S(2)}) collective-permute-start(bf16[896,256]{1,0:T(8,128)(2,1)S(1)} %collective-permute-done.w1), channel_id=1, source_target_pairs={{0,64},{64,128},{128,192},{192,256},{256,320},{320,384},{384,448},... | collective-permute-start | bytes 1376264 | tf_op jit(solution)/shard_map/ppermute | solution.py:313
  21.1 3.7 %collective-permute-start.3 = (bf16[896,256]{1,0:T(8,128)(2,1)S(1)}, bf16[896,256]{1,0:T(8,128)(2,1)S(1)}, u32[]{:S(2)}, u32[]{:S(2)}) collective-permute-start(bf16[896,256]{1,0:T(8,128)(2,1)S(1)} %collective-permute-done.1.w7), channel_id=1, source_target_pairs={{0,448},{64,0},{128,64},{192,128},{256,192},{320,256},{384,320},{4... | collective-permute-start | bytes 1376264 | tf_op jit(solution)/shard_map/ppermute | solution.py:314
  24.8 3.4 %collective-permute-start.6 = (bf16[192,2944]{1,0:T(8,128)(2,1)}, bf16[192,2944]{1,0:T(8,128)(2,1)}, u32[]{:S(2)}, u32[]{:S(2)}) collective-permute-start(bf16[192,2944]{1,0:T(8,128)(2,1)} %get-tuple-element.29), channel_id=1, source_target_pairs={{0,16},{16,32},{32,48},{48,0},{1,17},{17,33},{33,49},{49,1},{2,18}... | collective-permute-start | bytes 3391496 | tf_op jit(solution)/shard_map/ppermute | solution.py:312
  28.2 3.2 %collective-permute-start.7 = (bf16[192,2944]{1,0:T(8,128)(2,1)}, bf16[192,2944]{1,0:T(8,128)(2,1)}, u32[]{:S(2)}, u32[]{:S(2)}) collective-permute-start(bf16[192,2944]{1,0:T(8,128)(2,1)} %get-tuple-element.30), channel_id=1, source_target_pairs={{0,48},{16,0},{32,16},{48,32},{1,49},{17,1},{33,17},{49,33},{2,50}... | collective-permute-start | bytes 3391496 | tf_op jit(solution)/shard_map/ppermute | solution.py:312
  31.4 0.0 collective-permute-done.4.x2
  31.5 3.2 %collective-permute-done.3.w6 = bf16[896,256]{1,0:T(8,128)(2,1)S(1)} collective-permute-done((bf16[896,256]{1,0:T(8,128)(2,1)S(1)}, bf16[896,256]{1,0:T(8,128)(2,1)S(1)}, u32[]{:S(2)}, u32[]{:S(2)}) %collective-permute-start.3) | collective-permute-done | bytes 458784 | tf_op jit(solution)/shard_map/ppermute | solution.py:314
  34.6 4.0 %collective-permute-start.8 = (bf16[896,256]{1,0:T(8,128)(2,1)S(1)}, bf16[896,256]{1,0:T(8,128)(2,1)S(1)}, u32[]{:S(2)}, u32[]{:S(2)}) collective-permute-start(bf16[896,256]{1,0:T(8,128)(2,1)S(1)} %collective-permute-done.2.w2), channel_id=1, source_target_pairs={{0,64},{64,128},{128,192},{192,256},{256,320},{320,384},{384,448},... | collective-permute-start | bytes 1376264 | tf_op jit(solution)/shard_map/ppermute | solution.py:317
  38.7 2.5 %collective-permute-start.9 = (bf16[896,256]{1,0:T(8,128)(2,1)S(1)}, bf16[896,256]{1,0:T(8,128)(2,1)S(1)}, u32[]{:S(2)}, u32[]{:S(2)}) collective-permute-start(bf16[896,256]{1,0:T(8,128)(2,1)S(1)} %collective-permute-done.3.w6), channel_id=1, source_target_pairs={{0,448},{64,0},{128,64},{192,128},{256,192},{320,256},{384,320},{4... | collective-permute-start | bytes 1376264 | tf_op jit(solution)/shard_map/ppermute | solution.py:318
  41.1 14.7 %all-to-all-start = ((bf16[16,112,256]{2,1,0:T(8,128)(2,1)}), bf16[16,112,256]{2,1,0:T(8,128)(2,1)}, u32[]{:S(2)}, u32[]{:S(2)}) async-start(bf16[16,112,256]{2,1,0:T(8,128)(2,1)} %get-tuple-element.41), calls=%async_computation | async-start | bytes 1835008 | tf_op jit(solution)/shard_map/all_to_all | solution.py:315
  55.8 2.2 %collective-permute-start.5 = (bf16[192,1920]{1,0:T(8,128)(2,1)}, bf16[192,1920]{1,0:T(8,128)(2,1)S(1)}, u32[]{:S(2)}, u32[]{:S(2)}) collective-permute-start(bf16[192,1920]{1,0:T(8,128)(2,1)} %copy-done.5), channel_id=1, source_target_pairs={{0,1},{1,0},{2,3},{3,2},{4,5},{5,4},{6,7},{7,6},{8,9},{9,8},{10,11... | collective-permute-start | bytes 2211848 | tf_op jit(solution)/shard_map/ppermute | solution.py:321
  58.0 1.9 %collective-permute-start.10 = (bf16[896,256]{1,0:T(8,128)(2,1)S(1)}, bf16[896,256]{1,0:T(8,128)(2,1)S(1)}, u32[]{:S(2)}, u32[]{:S(2)}) collective-permute-start(bf16[896,256]{1,0:T(8,128)(2,1)S(1)} %collective-permute-done.8.w3), channel_id=1, source_target_pairs={{0,64},{64,128},{128,192},{192,256},{256,320},{320,384},{384,448},... | collective-permute-start | bytes 1376264 | tf_op jit(solution)/shard_map/ppermute | solution.py:320
  60.0 0.3 collective-permute-done.5.o2
  60.3 0.9 copy-done.6
  61.2 7.4 %near.1 = (f32[4,192,896]{2,1,0:T(8,128)}, bf16[4,192,256]{2,1,0:T(8,128)(2,1)S(1)}, bf16[4,192,896]{2,1,0:T(8,128)(2,1)}) custom-call(bf16[192,8192]{1,0:T(8,128)(2,1)} %grad.3, bf16[192,896]{1,0:T(8,128)(2,1)S(1)} %copy-done, bf16[192,2944]{1,0:T(8,128)(2,1)} %collective-permute-done.6.x1, bf16[192,1920]{1,0:T(8,128)(2,1)} %copy-done.5, ...), custom_call_target="tpu_custom_call" | custom-call | flops 1000000 | bytes 100000 | tf_op jit(solution)/shard_map/near/pallas_call | solution.py:172
  68.5 4.5 %collective-permute-done.10.w4 = bf16[896,256]{1,0:T(8,128)(2,1)S(1)} collective-permute-done((bf16[896,256]{1,0:T(8,128)(2,1)S(1)}, bf16[896,256]{1,0:T(8,128)(2,1)S(1)}, u32[]{:S(2)}, u32[]{:S(2)}) %collective-permute-start.10) | collective-permute-done | bytes 458784 | tf_op jit(solution)/shard_map/ppermute | solution.py:320
  73.0 1.3 %copy-done.3 = bf16[4,192,896]{2,1,0:T(8,128)(2,1)S(1)} copy-done((bf16[4,192,896]{2,1,0:T(8,128)(2,1)S(1)}, bf16[4,192,896]{2,1,0:T(8,128)(2,1)}, u32[]{:S(2)}) %copy-start.3) | copy-done | bytes 1376280
  74.3 5.8 %far.1 = f32[4,16,4,192]{3,2,1,0:T(4,128)} custom-call(f32[4,192,896]{2,1,0:T(8,128)} %get-tuple-element.38.acc, bf16[4,192,256]{2,1,0:T(8,128)(2,1)S(1)} %get-tuple-element.39.last, bf16[4,192,896]{2,1,0:T(8,128)(2,1)S(1)} %copy-done.3, bf16[896,256]{1,0:T(8,128)(2,1)S(1)} %collective-permute-done.10.w4, bf16[64,896]{1,0:T(8,128)(2,1)S(1)} %bitcast.3), custom_call_target="tpu_custom_call" | custom-call | flops 10481565696 | bytes 9000000 | tf_op jit(solution)/shard_map/far/pallas_call | solution.py:234
  80.1 1.1 %all-to-all-done.got = bf16[16,112,256]{2,1,0:T(8,128)(2,1)} async-done(((bf16[16,112,256]{2,1,0:T(8,128)(2,1)}), bf16[16,112,256]{2,1,0:T(8,128)(2,1)}, u32[]{:S(2)}, u32[]{:S(2)}) %all-to-all-start) | async-done | bytes 917536 | tf_op jit(solution)/shard_map/all_to_all | solution.py:315
  81.2 10.2 %all-to-all-start.1 = ((f32[64,4,192]{2,1,0:T(4,128)}), f32[64,4,192]{2,1,0:T(4,128)S(1)}, u32[]{:S(2)}, u32[]{:S(2)}) async-start(f32[64,4,192]{2,1,0:T(4,128)} %bitcast.1), calls=%async_computation.1 | async-start | bytes 524288 | tf_op jit(solution)/shard_map/all_to_all | solution.py:326
  91.4 1.9 %settle.1 = (f32[96,256]{1,0:T(8,128)}, f32[4,192]{1,0:T(4,128)}) custom-call(bf16[16,112,256]{2,1,0:T(8,128)(2,1)} %all-to-all-done.got), custom_call_target="tpu_custom_call" | custom-call | tf_op jit(solution)/shard_map/settle/pallas_call | solution.py:277
  93.3 2.4 %collective-permute-start.11 = (f32[96,256]{1,0:T(8,128)}, f32[96,256]{1,0:T(8,128)S(1)}, u32[]{:S(2)}, u32[]{:S(2)}) collective-permute-start(f32[96,256]{1,0:T(8,128)} %get-tuple-element.45.mine), channel_id=1, source_target_pairs={{0,1},{1,0},{2,3},{3,2},{4,5},{5,4},{6,7},{7,6},{8,9},{9,8},{10,11... | collective-permute-start | bytes 294920 | tf_op jit(solution)/shard_map/ppermute | solution.py:328
  95.7 1.1 %collective-permute-done.11.other = f32[96,256]{1,0:T(8,128)S(1)} collective-permute-done((f32[96,256]{1,0:T(8,128)}, f32[96,256]{1,0:T(8,128)S(1)}, u32[]{:S(2)}, u32[]{:S(2)}) %collective-permute-start.11) | collective-permute-done | bytes 98336 | tf_op jit(solution)/shard_map/ppermute | solution.py:328
  96.8 6.6 %all-to-all-done.1.got = f32[64,4,192]{2,1,0:T(4,128)S(1)} async-done(((f32[64,4,192]{2,1,0:T(4,128)}), f32[64,4,192]{2,1,0:T(4,128)S(1)}, u32[]{:S(2)}, u32[]{:S(2)}) %all-to-all-start.1) | async-done | bytes 196640 | tf_op jit(solution)/shard_map/all_to_all | solution.py:326
  103.4 0.7 copy-done.4
  104.1 1.9 %finish.1 = (f32[2,512]{1,0:T(2,128)}, f32[2,512]{1,0:T(2,128)}) custom-call(f32[64,4,192]{2,1,0:T(4,128)} %copy-done.4, f32[4,192]{1,0:T(4,128)} %get-tuple-element.44.hid_side, f32[96,256]{1,0:T(8,128)} %get-tuple-element.45.mine, f32[96,256]{1,0:T(8,128)} %copy-done.7, s32[1,192]{1,0:T(1,128)} %ids.1), custom_call_target="tpu_custom_call" | custom-call | tf_op jit(solution)/shard_map/finish/pallas_call | solution.py:301
  (17 shorter events, 0.0 us)
Async XLA Ops:
  0.6 17.6 %collective-permute-start = (bf16[896,256]{1,0:T(8,128)(2,1)}, bf16[896,256]{1,0:T(8,128)(2,1)S(1)}, u32[]{:S(2)}, u32[]{:S(2)}) collective-permute-start(bf16[896,256]{1,0:T(8,128)(2,1)} %w0.1), channel_id=1, source_target_pairs={{0,64},{64,128},{128,192},{192,256},{256,320},{320,384},{384,448},... | collective-permute-start | bytes 1376264 | tf_op jit(solution)/shard_map/ppermute | solution.py:308
  4.7 13.6 %collective-permute-start.1 = (bf16[896,256]{1,0:T(8,128)(2,1)}, bf16[896,256]{1,0:T(8,128)(2,1)S(1)}, u32[]{:S(2)}, u32[]{:S(2)}) collective-permute-start(bf16[896,256]{1,0:T(8,128)(2,1)} %w0.1), channel_id=1, source_target_pairs={{0,448},{64,0},{128,64},{192,128},{256,192},{320,256},{384,320},{4... | collective-permute-start | bytes 1376264 | tf_op jit(solution)/shard_map/ppermute | solution.py:309
  13.3 47.8 %copy-start = (bf16[192,896]{1,0:T(8,128)(2,1)S(1)}, bf16[192,896]{1,0:T(8,128)(2,1)}, u32[]{:S(2)}) copy-start(bf16[192,896]{1,0:T(8,128)(2,1)} %own.1) | copy-start | bytes 1032196
  13.3 47.8 %copy-start.1 = (bf16[896,256]{1,0:T(8,128)(2,1)S(1)}, bf16[896,256]{1,0:T(8,128)(2,1)}, u32[]{:S(2)}) copy-start(bf16[896,256]{1,0:T(8,128)(2,1)} %w0.1) | copy-start | bytes 1376260
  13.4 18.1 %collective-permute-start.4 = (bf16[192,1920]{1,0:T(8,128)(2,1)}, bf16[192,1920]{1,0:T(8,128)(2,1)S(1)}, u32[]{:S(2)}, u32[]{:S(2)}) collective-permute-start(bf16[192,1920]{1,0:T(8,128)(2,1)} %get-tuple-element.27), channel_id=1, source_target_pairs={{0,32},{16,48},{32,0},{48,16},{1,33},{17,49},{33,1},{49,17},{2,34}... | collective-permute-start | bytes 2211848 | tf_op jit(solution)/shard_map/ppermute | solution.py:312
  18.3 13.2 %collective-permute-start.2 = (bf16[896,256]{1,0:T(8,128)(2,1)S(1)}, bf16[896,256]{1,0:T(8,128)(2,1)S(1)}, u32[]{:S(2)}, u32[]{:S(2)}) collective-permute-start(bf16[896,256]{1,0:T(8,128)(2,1)S(1)} %collective-permute-done.w1), channel_id=1, source_target_pairs={{0,64},{64,128},{128,192},{192,256},{256,320},{320,384},{384,448},... | collective-permute-start | bytes 1376264 | tf_op jit(solution)/shard_map/ppermute | solution.py:313
  21.1 13.6 %collective-permute-start.3 = (bf16[896,256]{1,0:T(8,128)(2,1)S(1)}, bf16[896,256]{1,0:T(8,128)(2,1)S(1)}, u32[]{:S(2)}, u32[]{:S(2)}) collective-permute-start(bf16[896,256]{1,0:T(8,128)(2,1)S(1)} %collective-permute-done.1.w7), channel_id=1, source_target_pairs={{0,448},{64,0},{128,64},{192,128},{256,192},{320,256},{384,320},{4... | collective-permute-start | bytes 1376264 | tf_op jit(solution)/shard_map/ppermute | solution.py:314
  24.8 35.2 %collective-permute-start.6 = (bf16[192,2944]{1,0:T(8,128)(2,1)}, bf16[192,2944]{1,0:T(8,128)(2,1)}, u32[]{:S(2)}, u32[]{:S(2)}) collective-permute-start(bf16[192,2944]{1,0:T(8,128)(2,1)} %get-tuple-element.29), channel_id=1, source_target_pairs={{0,16},{16,32},{32,48},{48,0},{1,17},{17,33},{33,49},{49,1},{2,18}... | collective-permute-start | bytes 3391496 | tf_op jit(solution)/shard_map/ppermute | solution.py:312
  28.2 31.7 %collective-permute-start.7 = (bf16[192,2944]{1,0:T(8,128)(2,1)}, bf16[192,2944]{1,0:T(8,128)(2,1)}, u32[]{:S(2)}, u32[]{:S(2)}) collective-permute-start(bf16[192,2944]{1,0:T(8,128)(2,1)} %get-tuple-element.30), channel_id=1, source_target_pairs={{0,48},{16,0},{32,16},{48,32},{1,49},{17,1},{33,17},{49,33},{2,50}... | collective-permute-start | bytes 3391496 | tf_op jit(solution)/shard_map/ppermute | solution.py:312
  31.5 3.2 %copy-start.5 = (bf16[192,1920]{1,0:T(8,128)(2,1)}, bf16[192,1920]{1,0:T(8,128)(2,1)S(1)}, u32[]{:S(2)}) copy-start(bf16[192,1920]{1,0:T(8,128)(2,1)S(1)} %collective-permute-done.4.x2) | copy-start | bytes 2211844
  34.6 23.4 %collective-permute-start.8 = (bf16[896,256]{1,0:T(8,128)(2,1)S(1)}, bf16[896,256]{1,0:T(8,128)(2,1)S(1)}, u32[]{:S(2)}, u32[]{:S(2)}) collective-permute-start(bf16[896,256]{1,0:T(8,128)(2,1)S(1)} %collective-permute-done.2.w2), channel_id=1, source_target_pairs={{0,64},{64,128},{128,192},{192,256},{256,320},{320,384},{384,448},... | collective-permute-start | bytes 1376264 | tf_op jit(solution)/shard_map/ppermute | solution.py:317
  38.7 19.4 %collective-permute-start.9 = (bf16[896,256]{1,0:T(8,128)(2,1)S(1)}, bf16[896,256]{1,0:T(8,128)(2,1)S(1)}, u32[]{:S(2)}, u32[]{:S(2)}) collective-permute-start(bf16[896,256]{1,0:T(8,128)(2,1)S(1)} %collective-permute-done.3.w6), channel_id=1, source_target_pairs={{0,448},{64,0},{128,64},{192,128},{256,192},{320,256},{384,320},{4... | collective-permute-start | bytes 1376264 | tf_op jit(solution)/shard_map/ppermute | solution.py:318
  41.1 40.1 %all-to-all-start = ((bf16[16,112,256]{2,1,0:T(8,128)(2,1)}), bf16[16,112,256]{2,1,0:T(8,128)(2,1)}, u32[]{:S(2)}, u32[]{:S(2)}) async-start(bf16[16,112,256]{2,1,0:T(8,128)(2,1)} %get-tuple-element.41), calls=%async_computation | async-start | bytes 1835008 | tf_op jit(solution)/shard_map/all_to_all | solution.py:315
  55.8 17.2 %copy-start.2 = (bf16[896,64]{0,1:T(8,128)(2,1)S(1)}, bf16[896,64]{0,1:T(8,128)(2,1)}, u32[]{:S(2)}) copy-start(bf16[896,64]{0,1:T(8,128)(2,1)} %param.13) | copy-start | bytes 344068
  55.8 4.5 %collective-permute-start.5 = (bf16[192,1920]{1,0:T(8,128)(2,1)}, bf16[192,1920]{1,0:T(8,128)(2,1)S(1)}, u32[]{:S(2)}, u32[]{:S(2)}) collective-permute-start(bf16[192,1920]{1,0:T(8,128)(2,1)} %copy-done.5), channel_id=1, source_target_pairs={{0,1},{1,0},{2,3},{3,2},{4,5},{5,4},{6,7},{7,6},{8,9},{9,8},{10,11... | collective-permute-start | bytes 2211848 | tf_op jit(solution)/shard_map/ppermute | solution.py:321
  58.0 15.0 %collective-permute-start.10 = (bf16[896,256]{1,0:T(8,128)(2,1)S(1)}, bf16[896,256]{1,0:T(8,128)(2,1)S(1)}, u32[]{:S(2)}, u32[]{:S(2)}) collective-permute-start(bf16[896,256]{1,0:T(8,128)(2,1)S(1)} %collective-permute-done.8.w3), channel_id=1, source_target_pairs={{0,64},{64,128},{128,192},{192,256},{256,320},{320,384},{384,448},... | collective-permute-start | bytes 1376264 | tf_op jit(solution)/shard_map/ppermute | solution.py:320
  60.3 0.9 copy-start.6
  73.0 1.3 %copy-start.3 = (bf16[4,192,896]{2,1,0:T(8,128)(2,1)S(1)}, bf16[4,192,896]{2,1,0:T(8,128)(2,1)}, u32[]{:S(2)}) copy-start(bf16[4,192,896]{2,1,0:T(8,128)(2,1)} %get-tuple-element.40.gates) | copy-start | bytes 4128772
  81.2 22.2 %all-to-all-start.1 = ((f32[64,4,192]{2,1,0:T(4,128)}), f32[64,4,192]{2,1,0:T(4,128)S(1)}, u32[]{:S(2)}, u32[]{:S(2)}) async-start(f32[64,4,192]{2,1,0:T(4,128)} %bitcast.1), calls=%async_computation.1 | async-start | bytes 524288 | tf_op jit(solution)/shard_map/all_to_all | solution.py:326
  93.3 3.5 %collective-permute-start.11 = (f32[96,256]{1,0:T(8,128)}, f32[96,256]{1,0:T(8,128)S(1)}, u32[]{:S(2)}, u32[]{:S(2)}) collective-permute-start(f32[96,256]{1,0:T(8,128)} %get-tuple-element.45.mine), channel_id=1, source_target_pairs={{0,1},{1,0},{2,3},{3,2},{4,5},{5,4},{6,7},{7,6},{8,9},{9,8},{10,11... | collective-permute-start | bytes 294920 | tf_op jit(solution)/shard_map/ppermute | solution.py:328
  96.8 6.6 %copy-start.7 = (f32[96,256]{1,0:T(8,128)}, f32[96,256]{1,0:T(8,128)S(1)}, u32[]{:S(2)}) copy-start(f32[96,256]{1,0:T(8,128)S(1)} %collective-permute-done.11.other) | copy-start | bytes 294916
  103.4 0.7 copy-start.4

commit v9 on v8

--- a/solution.py
+++ b/solution.py
@@ -224,7 +224,7 @@
         total = dot_nt(p[...], hi) + dot_nt(p[...], lo)
         to = lax.rem(x - s + nx, nx)
         for b in range(NB):
-            out[to, b] = total[b * per : (b + 1) * per, :]
+            out[b, to] = total[b * per : (b + 1) * per, :]
 
 
 def far(acc, last, gates, w4, proj):
@@ -233,7 +233,7 @@
     per = proj.shape[0] // NB
     return pl.pallas_call(
         far_kernel,
-        out_shape=jax.ShapeDtypeStruct((nx, NB, per, tok), F32),
+        out_shape=jax.ShapeDtypeStruct((NB, nx, per, tok), F32),
         in_specs=[HBM] * 5,
         out_specs=VMEM,
         scratch_shapes=[
@@ -323,7 +323,7 @@
     acc, last, gates = near(out_grad, gate_pre, (x1, x2, x3, o2), (down_weight, up1, up2, up3, dn3, dn2, dn1))
     up_part = far(acc, last, gates, w4, hproj)
     up_part, got = lax.optimization_barrier((up_part, got))
-    up_side = lax.all_to_all(up_part.reshape((NX * NB,) + up_part.shape[2:]), ("x",) + ZC, 0, 0)
+    up_side = lax.all_to_all(up_part.reshape((NX * NB,) + up_part.shape[2:]), ZC + ("x",), 0, 0)
     mine, hid_side = settle(got, up_part.shape[2])
     other = lax.ppermute(mine, "core", turn(NC, 1))
     return tuple(finish(up_side, hid_side, mine, other, example_ids))

time: 107 us -> 107 us (level)
  no operation moved by 1% of the time
where the time goes in v9:
time: 107 us; the launch traced here: 106 us
  starting transfers between devices  63.7 us (60%)
  Pallas kernels  21.8 us (20%)
  waiting for transfers between devices  17 us (16%)
  local copies, waits for them, and re-layouts  2.94 us (3%)
    all_to_all x1, starting transfers between devices, on_device(): got = lax.all_to_all(early, ZC, 0, 0)  14.7 us
    ppermute x3, starting transfers between devices, on_device(): lax.ppermute(p, 'x', turn(NX, s + 1))  11.5 us
    all_to_all x1, starting transfers between devices, on_device(): lax.all_to_all(up_part.reshape((NX * NB,) + up_part.shape[2:]), ZC + ('x'...  10.2 us
    pallas_call x1, Pallas kernels, near(): pl.pallas_call(near_kernel, out_shape=[jax.ShapeDtypeStruct((NX, tok, hid...  7.37 us
    all_to_all x1, waiting for transfers between devices, on_device(): lax.all_to_all(up_part.reshape((NX * NB,) + up_part.shape[2:]), ZC + ('x'...  6.86 us
    pallas_call x1, Pallas kernels, far(): pl.pallas_call(far_kernel, out_shape=jax.ShapeDtypeStruct((NB, nx, per, t...  5.76 us
    pallas_call x1, Pallas kernels, prepare(): pl.pallas_call(prepare_kernel, out_shape=[full, part, full] + [jax.ShapeD...  4.83 us
    ppermute x1, waiting for transfers between devices, on_device(): w4 = lax.ppermute(up3, 'y', turn(NY, 1))  4.46 us
  transfers between devices with their start and end apart: 14, of which 6 were waited for; matrix products, arithmetic and copies ran while one was open for 0% of the time, Pallas kernels for 19%

profile of v9, /device:TPU:1, one launch (start us, length us, event | category | flops | bytes accessed | tf_op | source)
XLA Modules:
  0.0 106.3 jit_solution(13685640438395307128)
XLA Ops:
  0.6 4.0 %collective-permute-start = (bf16[896,256]{1,0:T(8,128)(2,1)}, bf16[896,256]{1,0:T(8,128)(2,1)S(1)}, u32[]{:S(2)}, u32[]{:S(2)}) collective-permute-start(bf16[896,256]{1,0:T(8,128)(2,1)} %w0.1), channel_id=1, source_target_pairs={{0,64},{64,128},{128,192},{192,256},{256,320},{320,384},{384,448},... | collective-permute-start | bytes 1376264 | tf_op jit(solution)/shard_map/ppermute | solution.py:308
  4.7 3.8 %collective-permute-start.1 = (bf16[896,256]{1,0:T(8,128)(2,1)}, bf16[896,256]{1,0:T(8,128)(2,1)S(1)}, u32[]{:S(2)}, u32[]{:S(2)}) collective-permute-start(bf16[896,256]{1,0:T(8,128)(2,1)} %w0.1), channel_id=1, source_target_pairs={{0,448},{64,0},{128,64},{192,128},{256,192},{320,256},{384,320},{4... | collective-permute-start | bytes 1376264 | tf_op jit(solution)/shard_map/ppermute | solution.py:309
  8.5 4.8 %prepare.1 = (bf16[192,2944]{1,0:T(8,128)(2,1)}, bf16[192,1920]{1,0:T(8,128)(2,1)}, bf16[192,2944]{1,0:T(8,128)(2,1)}, bf16[16,112,256]{2,1,0:T(8,128)(2,1)}) custom-call(bf16[192,8192]{1,0:T(8,128)(2,1)} %grad.3, bf16[192,896]{1,0:T(8,128)(2,1)} %own.1, bf16[192,896]{1,0:T(8,128)(2,1)} %up.1, bf16[192,512]{1,0:T(8,128)(2,1)} %inp.1, ...), custom_call_target="tpu_custom_call" | custom-call | flops 80000000 | bytes 8000000 | tf_op jit(solution)/shard_map/prepare/pallas_call | solution.py:108
  13.3 0.0 copy-start
  13.3 0.0 copy-start.1
  13.4 4.9 %collective-permute-start.4 = (bf16[192,1920]{1,0:T(8,128)(2,1)}, bf16[192,1920]{1,0:T(8,128)(2,1)S(1)}, u32[]{:S(2)}, u32[]{:S(2)}) collective-permute-start(bf16[192,1920]{1,0:T(8,128)(2,1)} %get-tuple-element.27), channel_id=1, source_target_pairs={{0,32},{16,48},{32,0},{48,16},{1,33},{17,49},{33,1},{49,17},{2,34}... | collective-permute-start | bytes 2211848 | tf_op jit(solution)/shard_map/ppermute | solution.py:312
  18.3 0.0 collective-permute-done.w1
  18.3 2.8 %collective-permute-start.2 = (bf16[896,256]{1,0:T(8,128)(2,1)S(1)}, bf16[896,256]{1,0:T(8,128)(2,1)S(1)}, u32[]{:S(2)}, u32[]{:S(2)}) collective-permute-start(bf16[896,256]{1,0:T(8,128)(2,1)S(1)} %collective-permute-done.w1), channel_id=1, source_target_pairs={{0,64},{64,128},{128,192},{192,256},{256,320},{320,384},{384,448},... | collective-permute-start | bytes 1376264 | tf_op jit(solution)/shard_map/ppermute | solution.py:313
  21.1 3.7 %collective-permute-start.3 = (bf16[896,256]{1,0:T(8,128)(2,1)S(1)}, bf16[896,256]{1,0:T(8,128)(2,1)S(1)}, u32[]{:S(2)}, u32[]{:S(2)}) collective-permute-start(bf16[896,256]{1,0:T(8,128)(2,1)S(1)} %collective-permute-done.1.w7), channel_id=1, source_target_pairs={{0,448},{64,0},{128,64},{192,128},{256,192},{320,256},{384,320},{4... | collective-permute-start | bytes 1376264 | tf_op jit(solution)/shard_map/ppermute | solution.py:314
  24.8 3.4 %collective-permute-start.6 = (bf16[192,2944]{1,0:T(8,128)(2,1)}, bf16[192,2944]{1,0:T(8,128)(2,1)}, u32[]{:S(2)}, u32[]{:S(2)}) collective-permute-start(bf16[192,2944]{1,0:T(8,128)(2,1)} %get-tuple-element.29), channel_id=1, source_target_pairs={{0,16},{16,32},{32,48},{48,0},{1,17},{17,33},{33,49},{49,1},{2,18}... | collective-permute-start | bytes 3391496 | tf_op jit(solution)/shard_map/ppermute | solution.py:312
  28.2 3.2 %collective-permute-start.7 = (bf16[192,2944]{1,0:T(8,128)(2,1)}, bf16[192,2944]{1,0:T(8,128)(2,1)}, u32[]{:S(2)}, u32[]{:S(2)}) collective-permute-start(bf16[192,2944]{1,0:T(8,128)(2,1)} %get-tuple-element.30), channel_id=1, source_target_pairs={{0,48},{16,0},{32,16},{48,32},{1,49},{17,1},{33,17},{49,33},{2,50}... | collective-permute-start | bytes 3391496 | tf_op jit(solution)/shard_map/ppermute | solution.py:312
  31.4 0.0 collective-permute-done.4.x2
  31.5 3.2 %collective-permute-done.3.w6 = bf16[896,256]{1,0:T(8,128)(2,1)S(1)} collective-permute-done((bf16[896,256]{1,0:T(8,128)(2,1)S(1)}, bf16[896,256]{1,0:T(8,128)(2,1)S(1)}, u32[]{:S(2)}, u32[]{:S(2)}) %collective-permute-start.3) | collective-permute-done | bytes 458784 | tf_op jit(solution)/shard_map/ppermute | solution.py:314
  34.6 4.0 %collective-permute-start.8 = (bf16[896,256]{1,0:T(8,128)(2,1)S(1)}, bf16[896,256]{1,0:T(8,128)(2,1)S(1)}, u32[]{:S(2)}, u32[]{:S(2)}) collective-permute-start(bf16[896,256]{1,0:T(8,128)(2,1)S(1)} %collective-permute-done.2.w2), channel_id=1, source_target_pairs={{0,64},{64,128},{128,192},{192,256},{256,320},{320,384},{384,448},... | collective-permute-start | bytes 1376264 | tf_op jit(solution)/shard_map/ppermute | solution.py:317
  38.7 2.5 %collective-permute-start.9 = (bf16[896,256]{1,0:T(8,128)(2,1)S(1)}, bf16[896,256]{1,0:T(8,128)(2,1)S(1)}, u32[]{:S(2)}, u32[]{:S(2)}) collective-permute-start(bf16[896,256]{1,0:T(8,128)(2,1)S(1)} %collective-permute-done.3.w6), channel_id=1, source_target_pairs={{0,448},{64,0},{128,64},{192,128},{256,192},{320,256},{384,320},{4... | collective-permute-start | bytes 1376264 | tf_op jit(solution)/shard_map/ppermute | solution.py:318
  41.1 14.7 %all-to-all-start = ((bf16[16,112,256]{2,1,0:T(8,128)(2,1)}), bf16[16,112,256]{2,1,0:T(8,128)(2,1)}, u32[]{:S(2)}, u32[]{:S(2)}) async-start(bf16[16,112,256]{2,1,0:T(8,128)(2,1)} %get-tuple-element.41), calls=%async_computation | async-start | bytes 1835008 | tf_op jit(solution)/shard_map/all_to_all | solution.py:315
  55.8 2.2 %collective-permute-start.5 = (bf16[192,1920]{1,0:T(8,128)(2,1)}, bf16[192,1920]{1,0:T(8,128)(2,1)S(1)}, u32[]{:S(2)}, u32[]{:S(2)}) collective-permute-start(bf16[192,1920]{1,0:T(8,128)(2,1)} %copy-done.5), channel_id=1, source_target_pairs={{0,1},{1,0},{2,3},{3,2},{4,5},{5,4},{6,7},{7,6},{8,9},{9,8},{10,11... | collective-permute-start | bytes 2211848 | tf_op jit(solution)/shard_map/ppermute | solution.py:321
  58.0 1.9 %collective-permute-start.10 = (bf16[896,256]{1,0:T(8,128)(2,1)S(1)}, bf16[896,256]{1,0:T(8,128)(2,1)S(1)}, u32[]{:S(2)}, u32[]{:S(2)}) collective-permute-start(bf16[896,256]{1,0:T(8,128)(2,1)S(1)} %collective-permute-done.8.w3), channel_id=1, source_target_pairs={{0,64},{64,128},{128,192},{192,256},{256,320},{320,384},{384,448},... | collective-permute-start | bytes 1376264 | tf_op jit(solution)/shard_map/ppermute | solution.py:320
  60.0 0.3 collective-permute-done.5.o2
  60.3 0.9 copy-done.6
  61.2 7.4 %near.1 = (f32[4,192,896]{2,1,0:T(8,128)}, bf16[4,192,256]{2,1,0:T(8,128)(2,1)S(1)}, bf16[4,192,896]{2,1,0:T(8,128)(2,1)}) custom-call(bf16[192,8192]{1,0:T(8,128)(2,1)} %grad.3, bf16[192,896]{1,0:T(8,128)(2,1)S(1)} %copy-done, bf16[192,2944]{1,0:T(8,128)(2,1)} %collective-permute-done.6.x1, bf16[192,1920]{1,0:T(8,128)(2,1)} %copy-done.5, ...), custom_call_target="tpu_custom_call" | custom-call | flops 1000000 | bytes 100000 | tf_op jit(solution)/shard_map/near/pallas_call | solution.py:172
  68.5 4.5 %collective-permute-done.10.w4 = bf16[896,256]{1,0:T(8,128)(2,1)S(1)} collective-permute-done((bf16[896,256]{1,0:T(8,128)(2,1)S(1)}, bf16[896,256]{1,0:T(8,128)(2,1)S(1)}, u32[]{:S(2)}, u32[]{:S(2)}) %collective-permute-start.10) | collective-permute-done | bytes 458784 | tf_op jit(solution)/shard_map/ppermute | solution.py:320
  73.0 1.3 %copy-done.3 = bf16[4,192,896]{2,1,0:T(8,128)(2,1)S(1)} copy-done((bf16[4,192,896]{2,1,0:T(8,128)(2,1)S(1)}, bf16[4,192,896]{2,1,0:T(8,128)(2,1)}, u32[]{:S(2)}) %copy-start.3) | copy-done | bytes 1376280
  74.3 5.8 %far.1 = f32[16,4,4,192]{3,2,1,0:T(4,128)} custom-call(f32[4,192,896]{2,1,0:T(8,128)} %get-tuple-element.38.acc, bf16[4,192,256]{2,1,0:T(8,128)(2,1)S(1)} %get-tuple-element.39.last, bf16[4,192,896]{2,1,0:T(8,128)(2,1)S(1)} %copy-done.3, bf16[896,256]{1,0:T(8,128)(2,1)S(1)} %collective-permute-done.10.w4, bf16[64,896]{1,0:T(8,128)(2,1)S(1)} %bitcast.3), custom_call_target="tpu_custom_call" | custom-call | flops 10481565696 | bytes 9000000 | tf_op jit(solution)/shard_map/far/pallas_call | solution.py:234
  80.1 1.1 %all-to-all-done.got = bf16[16,112,256]{2,1,0:T(8,128)(2,1)} async-done(((bf16[16,112,256]{2,1,0:T(8,128)(2,1)}), bf16[16,112,256]{2,1,0:T(8,128)(2,1)}, u32[]{:S(2)}, u32[]{:S(2)}) %all-to-all-start) | async-done | bytes 917536 | tf_op jit(solution)/shard_map/all_to_all | solution.py:315
  81.2 10.2 %all-to-all-start.1 = ((f32[64,4,192]{2,1,0:T(4,128)}), f32[64,4,192]{2,1,0:T(4,128)S(1)}, u32[]{:S(2)}, u32[]{:S(2)}) async-start(f32[64,4,192]{2,1,0:T(4,128)} %bitcast.1), calls=%async_computation.1 | async-start | bytes 524288 | tf_op jit(solution)/shard_map/all_to_all | solution.py:326
  91.4 1.9 %settle.1 = (f32[96,256]{1,0:T(8,128)}, f32[4,192]{1,0:T(4,128)}) custom-call(bf16[16,112,256]{2,1,0:T(8,128)(2,1)} %all-to-all-done.got), custom_call_target="tpu_custom_call" | custom-call | tf_op jit(solution)/shard_map/settle/pallas_call | solution.py:277
  93.3 2.4 %collective-permute-start.11 = (f32[96,256]{1,0:T(8,128)}, f32[96,256]{1,0:T(8,128)S(1)}, u32[]{:S(2)}, u32[]{:S(2)}) collective-permute-start(f32[96,256]{1,0:T(8,128)} %get-tuple-element.45.mine), channel_id=1, source_target_pairs={{0,1},{1,0},{2,3},{3,2},{4,5},{5,4},{6,7},{7,6},{8,9},{9,8},{10,11... | collective-permute-start | bytes 294920 | tf_op jit(solution)/shard_map/ppermute | solution.py:328
  95.7 1.1 %collective-permute-done.11.other = f32[96,256]{1,0:T(8,128)S(1)} collective-permute-done((f32[96,256]{1,0:T(8,128)}, f32[96,256]{1,0:T(8,128)S(1)}, u32[]{:S(2)}, u32[]{:S(2)}) %collective-permute-start.11) | collective-permute-done | bytes 98336 | tf_op jit(solution)/shard_map/ppermute | solution.py:328
  96.8 6.9 %all-to-all-done.1.got = f32[64,4,192]{2,1,0:T(4,128)S(1)} async-done(((f32[64,4,192]{2,1,0:T(4,128)}), f32[64,4,192]{2,1,0:T(4,128)S(1)}, u32[]{:S(2)}, u32[]{:S(2)}) %all-to-all-start.1) | async-done | bytes 196640 | tf_op jit(solution)/shard_map/all_to_all | solution.py:326
  103.7 0.7 copy-done.4
  104.4 1.9 %finish.1 = (f32[2,512]{1,0:T(2,128)}, f32[2,512]{1,0:T(2,128)}) custom-call(f32[64,4,192]{2,1,0:T(4,128)} %copy-done.4, f32[4,192]{1,0:T(4,128)} %get-tuple-element.44.hid_side, f32[96,256]{1,0:T(8,128)} %get-tuple-element.45.mine, f32[96,256]{1,0:T(8,128)} %copy-done.7, s32[1,192]{1,0:T(1,128)} %ids.1), custom_call_target="tpu_custom_call" | custom-call | tf_op jit(solution)/shard_map/finish/pallas_call | solution.py:301
  (17 shorter events, 0.0 us)
Async XLA Ops:
  0.6 17.6 %collective-permute-start = (bf16[896,256]{1,0:T(8,128)(2,1)}, bf16[896,256]{1,0:T(8,128)(2,1)S(1)}, u32[]{:S(2)}, u32[]{:S(2)}) collective-permute-start(bf16[896,256]{1,0:T(8,128)(2,1)} %w0.1), channel_id=1, source_target_pairs={{0,64},{64,128},{128,192},{192,256},{256,320},{320,384},{384,448},... | collective-permute-start | bytes 1376264 | tf_op jit(solution)/shard_map/ppermute | solution.py:308
  4.7 13.6 %collective-permute-start.1 = (bf16[896,256]{1,0:T(8,128)(2,1)}, bf16[896,256]{1,0:T(8,128)(2,1)S(1)}, u32[]{:S(2)}, u32[]{:S(2)}) collective-permute-start(bf16[896,256]{1,0:T(8,128)(2,1)} %w0.1), channel_id=1, source_target_pairs={{0,448},{64,0},{128,64},{192,128},{256,192},{320,256},{384,320},{4... | collective-permute-start | bytes 1376264 | tf_op jit(solution)/shard_map/ppermute | solution.py:309
  13.3 47.8 %copy-start = (bf16[192,896]{1,0:T(8,128)(2,1)S(1)}, bf16[192,896]{1,0:T(8,128)(2,1)}, u32[]{:S(2)}) copy-start(bf16[192,896]{1,0:T(8,128)(2,1)} %own.1) | copy-start | bytes 1032196
  13.3 47.8 %copy-start.1 = (bf16[896,256]{1,0:T(8,128)(2,1)S(1)}, bf16[896,256]{1,0:T(8,128)(2,1)}, u32[]{:S(2)}) copy-start(bf16[896,256]{1,0:T(8,128)(2,1)} %w0.1) | copy-start | bytes 1376260
  13.4 18.1 %collective-permute-start.4 = (bf16[192,1920]{1,0:T(8,128)(2,1)}, bf16[192,1920]{1,0:T(8,128)(2,1)S(1)}, u32[]{:S(2)}, u32[]{:S(2)}) collective-permute-start(bf16[192,1920]{1,0:T(8,128)(2,1)} %get-tuple-element.27), channel_id=1, source_target_pairs={{0,32},{16,48},{32,0},{48,16},{1,33},{17,49},{33,1},{49,17},{2,34}... | collective-permute-start | bytes 2211848 | tf_op jit(solution)/shard_map/ppermute | solution.py:312
  18.3 13.2 %collective-permute-start.2 = (bf16[896,256]{1,0:T(8,128)(2,1)S(1)}, bf16[896,256]{1,0:T(8,128)(2,1)S(1)}, u32[]{:S(2)}, u32[]{:S(2)}) collective-permute-start(bf16[896,256]{1,0:T(8,128)(2,1)S(1)} %collective-permute-done.w1), channel_id=1, source_target_pairs={{0,64},{64,128},{128,192},{192,256},{256,320},{320,384},{384,448},... | collective-permute-start | bytes 1376264 | tf_op jit(solution)/shard_map/ppermute | solution.py:313
  21.1 13.6 %collective-permute-start.3 = (bf16[896,256]{1,0:T(8,128)(2,1)S(1)}, bf16[896,256]{1,0:T(8,128)(2,1)S(1)}, u32[]{:S(2)}, u32[]{:S(2)}) collective-permute-start(bf16[896,256]{1,0:T(8,128)(2,1)S(1)} %collective-permute-done.1.w7), channel_id=1, source_target_pairs={{0,448},{64,0},{128,64},{192,128},{256,192},{320,256},{384,320},{4... | collective-permute-start | bytes 1376264 | tf_op jit(solution)/shard_map/ppermute | solution.py:314
  24.8 35.2 %collective-permute-start.6 = (bf16[192,2944]{1,0:T(8,128)(2,1)}, bf16[192,2944]{1,0:T(8,128)(2,1)}, u32[]{:S(2)}, u32[]{:S(2)}) collective-permute-start(bf16[192,2944]{1,0:T(8,128)(2,1)} %get-tuple-element.29), channel_id=1, source_target_pairs={{0,16},{16,32},{32,48},{48,0},{1,17},{17,33},{33,49},{49,1},{2,18}... | collective-permute-start | bytes 3391496 | tf_op jit(solution)/shard_map/ppermute | solution.py:312
  28.2 31.7 %collective-permute-start.7 = (bf16[192,2944]{1,0:T(8,128)(2,1)}, bf16[192,2944]{1,0:T(8,128)(2,1)}, u32[]{:S(2)}, u32[]{:S(2)}) collective-permute-start(bf16[192,2944]{1,0:T(8,128)(2,1)} %get-tuple-element.30), channel_id=1, source_target_pairs={{0,48},{16,0},{32,16},{48,32},{1,49},{17,1},{33,17},{49,33},{2,50}... | collective-permute-start | bytes 3391496 | tf_op jit(solution)/shard_map/ppermute | solution.py:312
  31.5 3.2 %copy-start.5 = (bf16[192,1920]{1,0:T(8,128)(2,1)}, bf16[192,1920]{1,0:T(8,128)(2,1)S(1)}, u32[]{:S(2)}) copy-start(bf16[192,1920]{1,0:T(8,128)(2,1)S(1)} %collective-permute-done.4.x2) | copy-start | bytes 2211844
  34.6 23.4 %collective-permute-start.8 = (bf16[896,256]{1,0:T(8,128)(2,1)S(1)}, bf16[896,256]{1,0:T(8,128)(2,1)S(1)}, u32[]{:S(2)}, u32[]{:S(2)}) collective-permute-start(bf16[896,256]{1,0:T(8,128)(2,1)S(1)} %collective-permute-done.2.w2), channel_id=1, source_target_pairs={{0,64},{64,128},{128,192},{192,256},{256,320},{320,384},{384,448},... | collective-permute-start | bytes 1376264 | tf_op jit(solution)/shard_map/ppermute | solution.py:317
  38.7 19.4 %collective-permute-start.9 = (bf16[896,256]{1,0:T(8,128)(2,1)S(1)}, bf16[896,256]{1,0:T(8,128)(2,1)S(1)}, u32[]{:S(2)}, u32[]{:S(2)}) collective-permute-start(bf16[896,256]{1,0:T(8,128)(2,1)S(1)} %collective-permute-done.3.w6), channel_id=1, source_target_pairs={{0,448},{64,0},{128,64},{192,128},{256,192},{320,256},{384,320},{4... | collective-permute-start | bytes 1376264 | tf_op jit(solution)/shard_map/ppermute | solution.py:318
  41.1 40.1 %all-to-all-start = ((bf16[16,112,256]{2,1,0:T(8,128)(2,1)}), bf16[16,112,256]{2,1,0:T(8,128)(2,1)}, u32[]{:S(2)}, u32[]{:S(2)}) async-start(bf16[16,112,256]{2,1,0:T(8,128)(2,1)} %get-tuple-element.41), calls=%async_computation | async-start | bytes 1835008 | tf_op jit(solution)/shard_map/all_to_all | solution.py:315
  55.8 17.2 %copy-start.2 = (bf16[896,64]{0,1:T(8,128)(2,1)S(1)}, bf16[896,64]{0,1:T(8,128)(2,1)}, u32[]{:S(2)}) copy-start(bf16[896,64]{0,1:T(8,128)(2,1)} %param.13) | copy-start | bytes 344068
  55.8 4.5 %collective-permute-start.5 = (bf16[192,1920]{1,0:T(8,128)(2,1)}, bf16[192,1920]{1,0:T(8,128)(2,1)S(1)}, u32[]{:S(2)}, u32[]{:S(2)}) collective-permute-start(bf16[192,1920]{1,0:T(8,128)(2,1)} %copy-done.5), channel_id=1, source_target_pairs={{0,1},{1,0},{2,3},{3,2},{4,5},{5,4},{6,7},{7,6},{8,9},{9,8},{10,11... | collective-permute-start | bytes 2211848 | tf_op jit(solution)/shard_map/ppermute | solution.py:321
  58.0 15.0 %collective-permute-start.10 = (bf16[896,256]{1,0:T(8,128)(2,1)S(1)}, bf16[896,256]{1,0:T(8,128)(2,1)S(1)}, u32[]{:S(2)}, u32[]{:S(2)}) collective-permute-start(bf16[896,256]{1,0:T(8,128)(2,1)S(1)} %collective-permute-done.8.w3), channel_id=1, source_target_pairs={{0,64},{64,128},{128,192},{192,256},{256,320},{320,384},{384,448},... | collective-permute-start | bytes 1376264 | tf_op jit(solution)/shard_map/ppermute | solution.py:320
  60.3 0.9 copy-start.6
  73.0 1.3 %copy-start.3 = (bf16[4,192,896]{2,1,0:T(8,128)(2,1)S(1)}, bf16[4,192,896]{2,1,0:T(8,128)(2,1)}, u32[]{:S(2)}) copy-start(bf16[4,192,896]{2,1,0:T(8,128)(2,1)} %get-tuple-element.40.gates) | copy-start | bytes 4128772
  81.2 22.5 %all-to-all-start.1 = ((f32[64,4,192]{2,1,0:T(4,128)}), f32[64,4,192]{2,1,0:T(4,128)S(1)}, u32[]{:S(2)}, u32[]{:S(2)}) async-start(f32[64,4,192]{2,1,0:T(4,128)} %bitcast.1), calls=%async_computation.1 | async-start | bytes 524288 | tf_op jit(solution)/shard_map/all_to_all | solution.py:326
  93.3 3.5 %collective-permute-start.11 = (f32[96,256]{1,0:T(8,128)}, f32[96,256]{1,0:T(8,128)S(1)}, u32[]{:S(2)}, u32[]{:S(2)}) collective-permute-start(f32[96,256]{1,0:T(8,128)} %get-tuple-element.45.mine), channel_id=1, source_target_pairs={{0,1},{1,0},{2,3},{3,2},{4,5},{5,4},{6,7},{7,6},{8,9},{9,8},{10,11... | collective-permute-start | bytes 294920 | tf_op jit(solution)/shard_map/ppermute | solution.py:328
  96.8 6.9 %copy-start.7 = (f32[96,256]{1,0:T(8,128)}, f32[96,256]{1,0:T(8,128)S(1)}, u32[]{:S(2)}) copy-start(f32[96,256]{1,0:T(8,128)S(1)} %collective-permute-done.11.other) | copy-start | bytes 294916
  103.7 0.7 copy-start.4
